TPU v7x, 32 devices: a whole 2x2x4 slice. The times are simulated.
32 devices in a mesh: dp: 16 (over z, y, core), seq: 2 (over x).
Axes of the slice: x: 2, y: 2, z: 4, core: 2. Of those that a mesh axis runs over, the one named last changes fastest.
Arguments:
- frames: bfloat16 [32, 1728, 768], P('dp', 'seq'), may hold values from -6 to 6
- targets: bfloat16 [32, 1728, 768], P('dp', 'seq'), may hold values from -6 to 6
- lead_index: int32 [32], P('dp'), may hold values from 0 to 39
- lead_counts: int32 [16, 40], P('dp'), may hold values from 15 to 855, as said below
- first_gain: bfloat16 [768], P('seq'), may hold values from 0.099609375 to 1.8984375
- first_shift: bfloat16 [768], P('seq'), may hold values from -0.19921875 to 0.19921875
- query_weight: bfloat16 [768, 768], P('seq'), may hold values from -0.3125 to 0.3125
- key_weight: bfloat16 [768, 768], P('seq'), may hold values from -0.3125 to 0.3125
- value_weight: bfloat16 [768, 768], P('seq'), may hold values from -0.21875 to 0.21875
- output_weight: bfloat16 [768, 768], P('seq'), may hold values from -1.25 to 1.25
- second_gain: bfloat16 [768], P('seq'), may hold values from 0.099609375 to 1.8984375
- second_shift: bfloat16 [768], P('seq'), may hold values from -0.19921875 to 0.19921875
- up_weight: bfloat16 [768, 3072], P('seq'), may hold values from -0.21875 to 0.21875
- down_weight: bfloat16 [3072, 768], P('seq'), may hold values from -0.109375 to 0.109375
- lead_table: bfloat16 [40, 768], P(None, 'seq'), may hold values from -0.29882812 to 0.29882812
Outputs:
- output: bfloat16 [32, 1728, 768], P('dp', 'seq')
- input_grad: bfloat16 [32, 1728, 768], P('dp', 'seq')
- first_gain_grad: float32 [768], P('seq')
- first_shift_grad: float32 [768], P('seq')
- query_grad: float32 [768, 768], P('seq')
- key_grad: float32 [768, 768], P('seq')
- value_grad: float32 [768, 768], P('seq')
- output_weight_grad: float32 [768, 768], P('seq')
- second_gain_grad: float32 [768], P('seq')
- second_shift_grad: float32 [768], P('seq')
- up_grad: float32 [768, 3072], P('seq')
- down_grad: float32 [3072, 768], P('seq')
- lead_table_grad: float32 [40, 768], P(None, 'seq')
Inputs may be any that keep to these rules, and one draw needn't show every extreme that they name: `lead_counts`: positive sample counts, in each lead larger on higher rows on the whole.
All inputs are finite; a program needn't handle non-finite values.
Results may differ from a plain program's by a relative error of at most 0.012.
The roundings to bfloat16 on the way count: a program that leaves them out, or rounds other values in their place, can miss the bound.
Values may be sent and summed in bfloat16 or wider, within the bound.
A program may use at most 256 MiB of HBM per device.

v0:
```python
import jax
import jax.numpy as jnp
from jax import lax
from jax.sharding import PartitionSpec as P

HEAD_DIM = 64


EPSILON = 1e-06
PAIR_WIDTH = 128
INV_ROOT_TWO = 0.7071067811865476
INV_ROOT_TAU = 0.3989422804014327


def matmul(left_side, right_side):
    return jnp.dot(left_side, right_side, preferred_element_type=jnp.float32)


def matmul_left_t(left_side, right_side):
    return lax.dot_general(
        left_side, right_side, (((0,), (0,)), ((), ())), preferred_element_type=jnp.float32
    )


def matmul_right_t(left_side, right_side):
    return lax.dot_general(
        left_side, right_side, (((1,), (1,)), ((), ())), preferred_element_type=jnp.float32
    )


def layer_norm(hidden, gain_row, shift_row):
    center = hidden - jnp.mean(hidden, axis=-1, keepdims=True)
    inv_std = lax.rsqrt(jnp.mean(center * center, axis=-1, keepdims=True) + EPSILON)
    normed = center * inv_std
    return (normed * gain_row + shift_row, normed, inv_std)


def norm_back(grad_out, normed, inv_std, gain_row):
    scaled = grad_out * gain_row
    row_inner = (
        scaled
        - jnp.mean(scaled, axis=-1, keepdims=True)
        - normed * jnp.mean(scaled * normed, axis=-1, keepdims=True)
    )
    return (inv_std * row_inner, jnp.sum(grad_out * normed, axis=0), jnp.sum(grad_out, axis=0))


def gelu_slope(hidden):
    return (
        0.5 * (1.0 + lax.erf(hidden * INV_ROOT_TWO))
        + hidden * jnp.exp(-0.5 * hidden * hidden) * INV_ROOT_TAU
    )


def pair_slice(matrix, pair_index):
    return lax.dynamic_slice_in_dim(matrix, pair_index * PAIR_WIDTH, PAIR_WIDTH, 1).reshape(
        matrix.shape[0], PAIR_WIDTH // HEAD_DIM, HEAD_DIM
    )


def join_pairs(stacked):
    return jnp.moveaxis(stacked, 0, 1).reshape(stacked.shape[1], stacked.shape[0] * PAIR_WIDTH)


def attend_forward(queries, keys_all, values_all):
    scale = HEAD_DIM ** (-0.5)

    def one_pair(pair_index):
        query_part = pair_slice(queries, pair_index)
        key_part = pair_slice(keys_all, pair_index)
        value_part = pair_slice(values_all, pair_index)
        scores = (
            jnp.einsum("qhd,khd->hqk", query_part, key_part, preferred_element_type=jnp.float32)
            * scale
        )
        row_peak = jnp.max(scores, axis=-1, keepdims=True)
        exponent = jnp.exp(scores - row_peak)
        row_total = jnp.sum(exponent, axis=-1, keepdims=True)
        softmaxed = (exponent / row_total).astype(jnp.bfloat16)
        mixed_rows = jnp.einsum(
            "hqk,khd->qhd", softmaxed, value_part, preferred_element_type=jnp.float32
        )
        return (
            mixed_rows.reshape(mixed_rows.shape[0], PAIR_WIDTH),
            (row_peak + jnp.log(row_total))[..., 0],
        )

    mixed_all, log_totals = lax.map(one_pair, jnp.arange(queries.shape[1] // PAIR_WIDTH))
    return (join_pairs(mixed_all), log_totals)


def attend_backward(queries, keys_all, values_all, log_totals, attended_grad):
    scale = HEAD_DIM ** (-0.5)

    def one_pair(pieces):
        pair_index, log_part = pieces
        query_part = pair_slice(queries, pair_index)
        key_part = pair_slice(keys_all, pair_index)
        value_part = pair_slice(values_all, pair_index)
        grad_part = pair_slice(attended_grad, pair_index)
        scores = (
            jnp.einsum("qhd,khd->hqk", query_part, key_part, preferred_element_type=jnp.float32)
            * scale
        )
        softmaxed = jnp.exp(scores - log_part[..., None])
        prob_grad = jnp.einsum(
            "qhd,khd->hqk", grad_part, value_part, preferred_element_type=jnp.float32
        )
        value_term = jnp.einsum(
            "hqk,qhd->khd",
            softmaxed.astype(jnp.bfloat16),
            grad_part,
            preferred_element_type=jnp.float32,
        )
        row_inner = jnp.sum(softmaxed * prob_grad, axis=-1, keepdims=True)
        score_grad = (softmaxed * (prob_grad - row_inner)).astype(jnp.bfloat16)
        query_term = (
            jnp.einsum("hqk,khd->qhd", score_grad, key_part, preferred_element_type=jnp.float32)
            * scale
        )
        key_term = (
            jnp.einsum("hqk,qhd->khd", score_grad, query_part, preferred_element_type=jnp.float32)
            * scale
        )
        return (
            query_term.reshape(query_term.shape[0], PAIR_WIDTH),
            key_term.reshape(key_term.shape[0], PAIR_WIDTH),
            value_term.reshape(value_term.shape[0], PAIR_WIDTH),
        )

    query_all, key_terms, value_terms = lax.map(
        one_pair, (jnp.arange(queries.shape[1] // PAIR_WIDTH), log_totals)
    )
    return (join_pairs(query_all), join_pairs(key_terms), join_pairs(value_terms))


def frame_pass(weight_set, back_set, frame_in, target, lead_row, frame_weight):
    (
        first_gain,
        first_shift,
        query_weight,
        key_weight,
        value_weight,
        output_weight,
        second_gain,
        second_shift,
        up_weight,
        down_weight,
        lead_table,
    ) = weight_set
    embedding = jnp.dot(lead_row, lead_table.astype(jnp.float32), precision=lax.Precision.HIGHEST)
    hidden0 = frame_in.astype(jnp.float32) + embedding[None, :]
    first_out, normed1, inv_std1 = layer_norm(
        hidden0, first_gain.astype(jnp.float32), first_shift.astype(jnp.float32)
    )
    first_in = first_out.astype(jnp.bfloat16)
    queries = matmul(first_in, query_weight).astype(jnp.bfloat16)
    keys = matmul(first_in, key_weight).astype(jnp.bfloat16)
    values = matmul(first_in, value_weight).astype(jnp.bfloat16)
    keys_all, values_all = (
        lax.all_gather(keys, "seq", axis=0, tiled=True),
        lax.all_gather(values, "seq", axis=0, tiled=True),
    )
    attended, log_totals = attend_forward(queries, keys_all, values_all)
    attended_low = attended.astype(jnp.bfloat16)
    hidden1 = hidden0 + matmul(attended_low, output_weight)
    second_out, normed2, inv_std2 = layer_norm(
        hidden1, second_gain.astype(jnp.float32), second_shift.astype(jnp.float32)
    )
    second_in = second_out.astype(jnp.bfloat16)
    pre_act = matmul(second_in, up_weight)
    activated = jax.nn.gelu(pre_act, approximate=False).astype(jnp.bfloat16)
    result = hidden1 + matmul(activated, down_weight)
    output = result.astype(jnp.bfloat16)
    (
        first_gain,
        first_shift,
        query_weight,
        key_weight,
        value_weight,
        output_weight,
        second_gain,
        second_shift,
        up_weight,
        down_weight,
        lead_table,
    ) = back_set
    result_grad = frame_weight * (result - target.astype(jnp.float32))
    branch_grad = result_grad.astype(jnp.bfloat16)
    down_term = matmul_left_t(activated, branch_grad)
    pre_grad = (matmul_right_t(branch_grad, down_weight) * gelu_slope(pre_act)).astype(jnp.bfloat16)
    up_term = matmul_left_t(second_in, pre_grad)
    second_back, second_gain_term, second_shift_term = norm_back(
        matmul_right_t(pre_grad, up_weight), normed2, inv_std2, second_gain.astype(jnp.float32)
    )
    hidden1_grad = result_grad + second_back
    attn_branch = hidden1_grad.astype(jnp.bfloat16)
    output_term = matmul_left_t(attended_low, attn_branch)
    attended_grad = matmul_right_t(attn_branch, output_weight).astype(jnp.bfloat16)
    query_all, key_terms, value_terms = attend_backward(
        queries, keys_all, values_all, log_totals, attended_grad
    )
    key_sums, value_sums = (
        lax.psum_scatter(
            key_terms.astype(jnp.bfloat16), "seq", scatter_dimension=0, tiled=True
        ).astype(jnp.float32),
        lax.psum_scatter(
            value_terms.astype(jnp.bfloat16), "seq", scatter_dimension=0, tiled=True
        ).astype(jnp.float32),
    )
    query_low = query_all.astype(jnp.bfloat16)
    key_low = key_sums.astype(jnp.bfloat16)
    value_low = value_sums.astype(jnp.bfloat16)
    query_term = matmul_left_t(first_in, query_low)
    key_term = matmul_left_t(first_in, key_low)
    value_term = matmul_left_t(first_in, value_low)
    first_grad = (
        matmul_right_t(query_low, query_weight)
        + matmul_right_t(key_low, key_weight)
        + matmul_right_t(value_low, value_weight)
    )
    first_back, first_gain_term, first_shift_term = norm_back(
        first_grad, normed1, inv_std1, first_gain.astype(jnp.float32)
    )
    hidden0_grad = hidden1_grad + first_back
    table_term = lead_row[:, None] * jnp.sum(hidden0_grad, axis=0)[None, :]
    frame_grads = (
        first_gain_term,
        first_shift_term,
        query_term,
        key_term,
        value_term,
        output_term,
        second_gain_term,
        second_shift_term,
        up_term,
        down_term,
        table_term,
    )
    return (output, hidden0_grad.astype(jnp.bfloat16), frame_grads)


def body(
    frames,
    targets,
    lead_index,
    lead_counts,
    first_gain,
    first_shift,
    query_weight,
    key_weight,
    value_weight,
    output_weight,
    second_gain,
    second_shift,
    up_weight,
    down_weight,
    lead_table,
):
    shard_set = (
        first_gain,
        first_shift,
        query_weight,
        key_weight,
        value_weight,
        output_weight,
        second_gain,
        second_shift,
        up_weight,
        down_weight,
        lead_table,
    )
    lead_totals = lax.psum(lead_counts[0].astype(jnp.float32), "dp")
    lead_weight = jnp.mean(lead_totals) / lead_totals
    lead_rows = (
        lead_index[:, None] == jnp.arange(lead_table.shape[0], dtype=jnp.int32)[None, :]
    ).astype(jnp.float32)
    frame_weights = jnp.sum(lead_rows * lead_weight[None, :], axis=1)
    running = tuple((jnp.zeros(weight.shape, jnp.float32) for weight in shard_set))

    def scan_frame(running_in, pieces):
        frame_in, target, lead_row, frame_weight = pieces
        weight_set = (
            lax.all_gather(shard_set[0], "seq", axis=0, tiled=True),
            lax.all_gather(shard_set[1], "seq", axis=0, tiled=True),
            lax.all_gather(shard_set[2], "seq", axis=0, tiled=True),
            lax.all_gather(shard_set[3], "seq", axis=0, tiled=True),
            lax.all_gather(shard_set[4], "seq", axis=0, tiled=True),
            lax.all_gather(shard_set[5], "seq", axis=0, tiled=True),
            lax.all_gather(shard_set[6], "seq", axis=0, tiled=True),
            lax.all_gather(shard_set[7], "seq", axis=0, tiled=True),
            lax.all_gather(shard_set[8], "seq", axis=0, tiled=True),
            lax.all_gather(shard_set[9], "seq", axis=0, tiled=True),
            lax.all_gather(shard_set[10], "seq", axis=1, tiled=True),
        )
        output, input_grad, frame_grads = frame_pass(
            weight_set, weight_set, frame_in, target, lead_row, frame_weight
        )
        frame_grads = (
            lax.psum_scatter(
                frame_grads[0].astype(jnp.bfloat16), "seq", scatter_dimension=0, tiled=True
            ).astype(jnp.float32),
            lax.psum_scatter(
                frame_grads[1].astype(jnp.bfloat16), "seq", scatter_dimension=0, tiled=True
            ).astype(jnp.float32),
            lax.psum_scatter(
                frame_grads[2].astype(jnp.bfloat16), "seq", scatter_dimension=0, tiled=True
            ).astype(jnp.float32),
            lax.psum_scatter(
                frame_grads[3].astype(jnp.bfloat16), "seq", scatter_dimension=0, tiled=True
            ).astype(jnp.float32),
            lax.psum_scatter(
                frame_grads[4].astype(jnp.bfloat16), "seq", scatter_dimension=0, tiled=True
            ).astype(jnp.float32),
            lax.psum_scatter(
                frame_grads[5].astype(jnp.bfloat16), "seq", scatter_dimension=0, tiled=True
            ).astype(jnp.float32),
            lax.psum_scatter(
                frame_grads[6].astype(jnp.bfloat16), "seq", scatter_dimension=0, tiled=True
            ).astype(jnp.float32),
            lax.psum_scatter(
                frame_grads[7].astype(jnp.bfloat16), "seq", scatter_dimension=0, tiled=True
            ).astype(jnp.float32),
            lax.psum_scatter(
                frame_grads[8].astype(jnp.bfloat16), "seq", scatter_dimension=0, tiled=True
            ).astype(jnp.float32),
            lax.psum_scatter(
                frame_grads[9].astype(jnp.bfloat16), "seq", scatter_dimension=0, tiled=True
            ).astype(jnp.float32),
            lax.psum_scatter(
                frame_grads[10].astype(jnp.bfloat16), "seq", scatter_dimension=1, tiled=True
            ).astype(jnp.float32),
        )
        running_out = tuple(
            (left_side + right_side for left_side, right_side in zip(running_in, frame_grads))
        )
        return (running_out, (output, input_grad))

    running, stacked = lax.scan(scan_frame, running, (frames, targets, lead_rows, frame_weights))
    outputs, input_grads = stacked
    summed = lax.psum(running, "dp")
    return (
        outputs,
        input_grads,
        summed[0],
        summed[1],
        summed[2],
        summed[3],
        summed[4],
        summed[5],
        summed[6],
        summed[7],
        summed[8],
        summed[9],
        summed[10],
    )


def solution(mesh):
    placed = (
        P("dp", "seq", None),
        P("dp", "seq", None),
        P("dp"),
        P("dp", None),
        P("seq"),
        P("seq"),
        P("seq", None),
        P("seq", None),
        P("seq", None),
        P("seq", None),
        P("seq"),
        P("seq"),
        P("seq", None),
        P("seq", None),
        P(None, "seq"),
    )
    return jax.shard_map(
        body,
        mesh=mesh,
        in_specs=placed,
        out_specs=(
            P("dp", "seq", None),
            P("dp", "seq", None),
            P("seq"),
            P("seq"),
            P("seq", None),
            P("seq", None),
            P("seq", None),
            P("seq", None),
            P("seq"),
            P("seq"),
            P("seq", None),
            P("seq", None),
            P(None, "seq"),
        ),
        check_vma=False,
    )
```

profile of v0, /device:TPU:0, one launch (start us, length us, event | category | flops | bytes accessed | tf_op | source)
XLA Modules:
  0.0 2088.7 jit_solution(1622963706985567583)
XLA Ops:
  8.8 34.9 %psum.84 = f32[40]{0:T(128)S(1)} all-reduce(f32[40]{0:T(128)S(1)} %convert_bitcast_fusion.1), channel_id=1, replica_groups=mesh['dp'=16,'seq'=2] {'dp'}, use_global_device_ids=true, to_apply=%region_0.0 | all-reduce | flops 40 | bytes 320 | tf_op jit(solution)/shard_map/psum | solution.py:273
  46.6 1659.6 %while.65 = (s32[]{:T(128)}, f32[384]{0:T(512)}, f32[384]{0:T(512)}, f32[384,768]{1,0:T(8,128)}, f32[384,768]{1,0:T(8,128)}, /*index=5*/f32[384,768]{1,0:T(8,128...) while((s32[]{:T(128)}, f32[384]{0:T(512)}, ...), condition=%wide.region_37.38_spmd.clone, body=%wide.region_3.37_spmd.clone.sunk | while | flops 39730098176 | bytes 859276608 | solution.py:339
  74.0 20.5 all-gather.25.cloned.1.call-done
  110.2 8.7 all-gather.29.cloned.1.call-done
  125.3 34.5 %all-gather.33.cloned.1.call-done = bf16[1728,768]{1,0:T(8,128)(2,1)} async-done(((bf16[864,768]{1,0:T(8,128)(2,1)}), bf16[1728,768]{1,0:T(8,128)(2,1)}) %all-gather.33.cloned.1.call-update) | async-done | bytes 2654224 | tf_op jit(solution)/shard_map/while/body/eval_jaxpr/all_gather | solution.py:162
  163.1 37.6 %all-gather.27.cloned.1.call-done = bf16[1728,768]{1,0:T(8,128)(2,1)} async-done(((bf16[864,768]{1,0:T(8,128)(2,1)}), bf16[1728,768]{1,0:T(8,128)(2,1)}) %all-gather.27.cloned.1.call-update) | async-done | bytes 2654224 | tf_op jit(solution)/shard_map/while/body/eval_jaxpr/all_gather | solution.py:161
  206.5 70.6 %while.66 = (s32[]{:T(128)}, bf16[6,864,128]{1,2,0:T(8,128)(2,1)}, f32[6,2,864]{2,1,0:T(2,128)}, s32[6]{0:T(128)S(1)}, bf16[1728,768]{0,1:T(8,128)(2,1)S(1)}, /*...) while((s32[]{:T(128)}, bf16[6,864,128]{1,2,0:T(8,128)(2,1)}, ...), condition=%wide.region_9.9_spmd, body=%wide.region_6.8_spmd.sunk | while | flops 791284032 | bytes 39877056 | solution.py:88
  289.3 31.2 %fusion.214 = (bf16[864,3072]{1,0:T(8,128)(2,1)}, f32[864,3072]{1,0:T(8,128)}) fusion(bf16[768,3072]{1,0:T(8,128)(2,1)} %all-gather.37.cloned.1.call-done, f32[864,768]{1,0:T(8,128)} %copy-done.3, f32[768]{0:T(1024)S(1)} %reshape.235, f32[768]{0:T(1024)S(1)} %reshape.233, f32[864]{0:T(1024)S(1)} %add_rsqrt_fusion.5, ...), kind=kOutput, calls=%fused_computation.31.clone.1 | convolution fusion | flops 4252704768 | bytes 23311104 | tf_op jit(solution)/shard_map/while/body/eval_jaxpr/dot_general | solution.py:16
  320.5 33.1 %all-gather.39.cloned.1.call-done = bf16[3072,768]{1,0:T(8,128)(2,1)} async-done(((bf16[1536,768]{1,0:T(8,128)(2,1)}), bf16[3072,768]{1,0:T(8,128)(2,1)}) %all-gather.39.cloned.1.call-update) | async-done | bytes 4718608 | tf_op jit(solution)/shard_map/while/body/eval_jaxpr/all_gather | solution.py:293
  353.6 9.6 fusion.215
  364.3 10.2 fusion.216
  385.6 166.4 %while.67 = (s32[]{:T(128)}, bf16[6,864,128]{1,2,0:T(8,128)(2,1)}, bf16[6,1728,128]{1,2,0:T(8,128)(2,1)}, bf16[6,1728,128]{1,2,0:T(8,128)(2,1)S(1)}, s32[6]{0:T(...) while((s32[]{:T(128)}, bf16[6,864,128]{1,2,0:T(8,128)(2,1)}, ...), condition=%wide.region_16.16_spmd, body=%wide.region_14.15_spmd.sunk | while | flops 1947523328 | bytes 98328024 | solution.py:131
  396.3 6.1 multiply_reduce_fusion.14
  402.4 6.3 multiply_convert_fusion.5
  424.0 6.1 multiply_reduce_fusion.14
  430.1 6.3 multiply_convert_fusion.5
  451.7 6.1 multiply_reduce_fusion.14
  457.8 6.3 multiply_convert_fusion.5
  479.4 6.1 multiply_reduce_fusion.14
  485.5 6.3 multiply_convert_fusion.5
  507.2 6.1 multiply_reduce_fusion.14
  513.3 6.3 multiply_convert_fusion.5
  534.9 6.1 multiply_reduce_fusion.14
  541.0 6.3 multiply_convert_fusion.5
  573.7 21.1 %reduce-scatter.24.cloned.1.call-done = bf16[864,768]{1,0:T(8,128)(2,1)} async-done(((bf16[1728,768]{1,0:T(8,128)(2,1)}), bf16[864,768]{1,0:T(8,128)(2,1)}) %reduce-scatter.24.cloned.1.call-update) | async-done | bytes 1327120 | tf_op jit(solution)/shard_map/while
  599.3 35.8 %reduce-scatter.22.cloned.1.call-done = bf16[864,768]{1,0:T(8,128)(2,1)} async-done(((bf16[1728,768]{1,0:T(8,128)(2,1)}), bf16[864,768]{1,0:T(8,128)(2,1)}) %reduce-scatter.22.cloned.1.call-update) | async-done | bytes 1327120 | tf_op jit(solution)/shard_map/while
  653.9 8.9 convolution_convert_fusion.29
  664.6 9.7 convolution_convert_fusion.28
  699.3 21.0 %reduce-scatter.30.cloned.1.call-done = bf16[384,768]{1,0:T(8,128)(2,1)} async-done(((bf16[768,768]{1,0:T(8,128)(2,1)}), bf16[384,768]{1,0:T(8,128)(2,1)}) %reduce-scatter.30.cloned.1.call-update) | async-done | bytes 589840 | tf_op jit(solution)/shard_map/while/body/eval_jaxpr/reduce_scatter | solution.py:312
  721.7 22.5 %reduce-scatter.28.cloned.1.call-done = bf16[384,768]{1,0:T(8,128)(2,1)} async-done(((bf16[768,768]{1,0:T(8,128)(2,1)}), bf16[384,768]{1,0:T(8,128)(2,1)}) %reduce-scatter.28.cloned.1.call-update) | async-done | bytes 589840 | tf_op jit(solution)/shard_map/while/body/eval_jaxpr/reduce_scatter | solution.py:309
  745.7 60.8 %reduce-scatter.36.cloned.1.call-done = bf16[1536,768]{1,0:T(8,128)(2,1)} async-done(((bf16[3072,768]{1,0:T(8,128)(2,1)}), bf16[1536,768]{1,0:T(8,128)(2,1)}) %reduce-scatter.36.cloned.1.call-update) | async-done | bytes 2359312 | tf_op jit(solution)/shard_map/while/body/eval_jaxpr/reduce_scatter | solution.py:327
  810.8 57.9 %reduce-scatter.34.cloned.1.call-done = bf16[384,3072]{1,0:T(8,128)(2,1)} async-done(((bf16[768,3072]{1,0:T(8,128)(2,1)}), bf16[384,3072]{1,0:T(8,128)(2,1)}) %reduce-scatter.34.cloned.1.call-update) | async-done | bytes 2359312 | tf_op jit(solution)/shard_map/while/body/eval_jaxpr/reduce_scatter | solution.py:324
  903.2 20.5 all-gather.25.cloned.1.call-done
  939.3 8.7 all-gather.29.cloned.1.call-done
  954.4 34.7 %all-gather.33.cloned.1.call-done = bf16[1728,768]{1,0:T(8,128)(2,1)} async-done(((bf16[864,768]{1,0:T(8,128)(2,1)}), bf16[1728,768]{1,0:T(8,128)(2,1)}) %all-gather.33.cloned.1.call-update) | async-done | bytes 2654224 | tf_op jit(solution)/shard_map/while/body/eval_jaxpr/all_gather | solution.py:162
  992.4 37.8 %all-gather.27.cloned.1.call-done = bf16[1728,768]{1,0:T(8,128)(2,1)} async-done(((bf16[864,768]{1,0:T(8,128)(2,1)}), bf16[1728,768]{1,0:T(8,128)(2,1)}) %all-gather.27.cloned.1.call-update) | async-done | bytes 2654224 | tf_op jit(solution)/shard_map/while/body/eval_jaxpr/all_gather | solution.py:161
  1035.9 70.6 %while.66 = (s32[]{:T(128)}, bf16[6,864,128]{1,2,0:T(8,128)(2,1)}, f32[6,2,864]{2,1,0:T(2,128)}, s32[6]{0:T(128)S(1)}, bf16[1728,768]{0,1:T(8,128)(2,1)S(1)}, /*...) while((s32[]{:T(128)}, bf16[6,864,128]{1,2,0:T(8,128)(2,1)}, ...), condition=%wide.region_9.9_spmd, body=%wide.region_6.8_spmd.sunk | while | flops 791284032 | bytes 39877056 | solution.py:88
  1118.8 31.1 %fusion.214 = (bf16[864,3072]{1,0:T(8,128)(2,1)}, f32[864,3072]{1,0:T(8,128)}) fusion(bf16[768,3072]{1,0:T(8,128)(2,1)} %all-gather.37.cloned.1.call-done, f32[864,768]{1,0:T(8,128)} %copy-done.3, f32[768]{0:T(1024)S(1)} %reshape.235, f32[768]{0:T(1024)S(1)} %reshape.233, f32[864]{0:T(1024)S(1)} %add_rsqrt_fusion.5, ...), kind=kOutput, calls=%fused_computation.31.clone.1 | convolution fusion | flops 4252704768 | bytes 23311104 | tf_op jit(solution)/shard_map/while/body/eval_jaxpr/dot_general | solution.py:16
  1149.8 33.2 %all-gather.39.cloned.1.call-done = bf16[3072,768]{1,0:T(8,128)(2,1)} async-done(((bf16[1536,768]{1,0:T(8,128)(2,1)}), bf16[3072,768]{1,0:T(8,128)(2,1)}) %all-gather.39.cloned.1.call-update) | async-done | bytes 4718608 | tf_op jit(solution)/shard_map/while/body/eval_jaxpr/all_gather | solution.py:293
  1183.1 9.6 fusion.215
  1193.8 10.2 fusion.216
  1215.1 166.4 %while.67 = (s32[]{:T(128)}, bf16[6,864,128]{1,2,0:T(8,128)(2,1)}, bf16[6,1728,128]{1,2,0:T(8,128)(2,1)}, bf16[6,1728,128]{1,2,0:T(8,128)(2,1)S(1)}, s32[6]{0:T(...) while((s32[]{:T(128)}, bf16[6,864,128]{1,2,0:T(8,128)(2,1)}, ...), condition=%wide.region_16.16_spmd, body=%wide.region_14.15_spmd.sunk | while | flops 1947523328 | bytes 98328024 | solution.py:131
  1225.7 6.1 multiply_reduce_fusion.14
  1231.8 6.3 multiply_convert_fusion.5
  1253.4 6.1 multiply_reduce_fusion.14
  1259.6 6.3 multiply_convert_fusion.5
  1281.2 6.1 multiply_reduce_fusion.14
  1287.3 6.3 multiply_convert_fusion.5
  1308.9 6.1 multiply_reduce_fusion.14
  1315.0 6.3 multiply_convert_fusion.5
  1336.6 6.1 multiply_reduce_fusion.14
  1342.8 6.3 multiply_convert_fusion.5
  1370.5 6.3 multiply_convert_fusion.5
  1403.2 21.1 %reduce-scatter.24.cloned.1.call-done = bf16[864,768]{1,0:T(8,128)(2,1)} async-done(((bf16[1728,768]{1,0:T(8,128)(2,1)}), bf16[864,768]{1,0:T(8,128)(2,1)}) %reduce-scatter.24.cloned.1.call-update) | async-done | bytes 1327120 | tf_op jit(solution)/shard_map/while
  1428.8 35.8 %reduce-scatter.22.cloned.1.call-done = bf16[864,768]{1,0:T(8,128)(2,1)} async-done(((bf16[1728,768]{1,0:T(8,128)(2,1)}), bf16[864,768]{1,0:T(8,128)(2,1)}) %reduce-scatter.22.cloned.1.call-update) | async-done | bytes 1327120 | tf_op jit(solution)/shard_map/while
  1483.4 8.9 convolution_convert_fusion.29
  1494.1 9.6 convolution_convert_fusion.28
  1528.8 21.1 %reduce-scatter.30.cloned.1.call-done = bf16[384,768]{1,0:T(8,128)(2,1)} async-done(((bf16[768,768]{1,0:T(8,128)(2,1)}), bf16[384,768]{1,0:T(8,128)(2,1)}) %reduce-scatter.30.cloned.1.call-update) | async-done | bytes 589840 | tf_op jit(solution)/shard_map/while/body/eval_jaxpr/reduce_scatter | solution.py:312
  1551.3 22.6 %reduce-scatter.28.cloned.1.call-done = bf16[384,768]{1,0:T(8,128)(2,1)} async-done(((bf16[768,768]{1,0:T(8,128)(2,1)}), bf16[384,768]{1,0:T(8,128)(2,1)}) %reduce-scatter.28.cloned.1.call-update) | async-done | bytes 589840 | tf_op jit(solution)/shard_map/while/body/eval_jaxpr/reduce_scatter | solution.py:309
  1575.4 60.8 %reduce-scatter.36.cloned.1.call-done = bf16[1536,768]{1,0:T(8,128)(2,1)} async-done(((bf16[3072,768]{1,0:T(8,128)(2,1)}), bf16[1536,768]{1,0:T(8,128)(2,1)}) %reduce-scatter.36.cloned.1.call-update) | async-done | bytes 2359312 | tf_op jit(solution)/shard_map/while/body/eval_jaxpr/reduce_scatter | solution.py:327
  1642.0 56.6 %reduce-scatter.34.cloned.1.call-done = bf16[384,3072]{1,0:T(8,128)(2,1)} async-done(((bf16[768,3072]{1,0:T(8,128)(2,1)}), bf16[384,3072]{1,0:T(8,128)(2,1)}) %reduce-scatter.34.cloned.1.call-update) | async-done | bytes 2359312 | tf_op jit(solution)/shard_map/while/body/eval_jaxpr/reduce_scatter | solution.py:324
  1698.6 6.3 select_add_fusion.26
  1707.3 90.9 %all-reduce.12.cloned.1.call-done = (f32[384]{0:T(512)}, f32[384]{0:T(512)}, f32[384]{0:T(512)}, f32[384]{0:T(512)}, f32[40,384]{1,0:T(8,128)}) async-done(((f32[384]{0:T(512)}, f32[384]{0:T(512)}, f32[384]{0:T(512)}, f32[384]{0:T(512)}, f32[40,384]{1,0:T(8,128)}), (f32[384]{0:T(512)}, f32[384]{0:T(512)}, f32[384]{0:T(512)}, f32[384]{0:T(512)}, f32[40,384]{1,0:T(8,128)})) %all-reduce.12.cloned.1.call-update) | async-done | bytes 67600 | tf_op jit(solution)/shard_map/psum | solution.py:341
  1798.2 267.4 %all-reduce.14.cloned.1.call-done = (f32[384,768]{1,0:T(8,128)}, f32[384,768]{1,0:T(8,128)}, f32[384,768]{1,0:T(8,128)}, f32[384,768]{1,0:T(8,128)}, f32[384,3072]{1,0:T(8,128)}, /*index=5*/f32[1536,768]{1,0:T(8,128)}) async-done(((f32[384,768]{1,0:T(8,128)}, f32[384,768]{1,0:T(8,128)}, f32[384,768]{1,0:T(8,128)}, f32[384,768]{1,0:T(8,128)}, f32[384,3072]{1,0:T(8,128)}, /*index=5*/f32[1536,768]{1,0:T(8,128)}), ...) | async-done | bytes 14155792 | tf_op jit(solution)/shard_map/psum | solution.py:341
  (788 shorter events, 662.8 us)
Async XLA Ops:
  46.8 23.2 %all-gather.31.cloned.1.call-start = ((), (), s32[]{:S(2)}) async-start(), calls=%async_computation.14 | async-start | bytes 1769472 | tf_op jit(solution)/shard_map/while/body/eval_jaxpr/all_gather | solution.py:288
  47.6 46.9 %all-gather.25.cloned.1.call-start = ((), (), s32[]{:S(2)}) async-start(), calls=%async_computation.11 | async-start | bytes 1769472 | tf_op jit(solution)/shard_map/while/body/eval_jaxpr/all_gather | solution.py:287
  48.3 70.6 %all-gather.29.cloned.1.call-start = ((), (), s32[]{:S(2)}) async-start(), calls=%async_computation.13 | async-start | bytes 1769472 | tf_op jit(solution)/shard_map/while/body/eval_jaxpr/all_gather | solution.py:286
  49.1 110.7 %all-gather.33.cloned.1.call-start = ((), (), s32[]{:S(2)}) async-start(), calls=%async_computation.15 | async-start | bytes 3981312 | tf_op jit(solution)/shard_map/while/body/eval_jaxpr/all_gather | solution.py:162
  54.1 64.8 %copy-start.40 = (f32[768]{0:T(1024)}, f32[768]{0:T(1024)S(1)}, u32[]{:S(2)}) copy-start(f32[768]{0:T(1024)S(1)} %reshape.231) | copy-start | bytes 9220 | tf_op jit(solution)/shard_map/while
  59.2 59.7 %copy-start.32 = (f32[768]{0:T(1024)}, f32[768]{0:T(1024)S(1)}, u32[]{:S(2)}) copy-start(f32[768]{0:T(1024)S(1)} %reshape.229) | copy-start | bytes 9220 | tf_op jit(solution)/shard_map/while
  64.8 212.3 %copy-start.23 = (f32[768]{0:T(1024)}, f32[768]{0:T(1024)S(1)}, u32[]{:S(2)}) copy-start(f32[768]{0:T(1024)S(1)} %convolution_reduce_fusion.2) | copy-start | bytes 9220 | tf_op jit(solution)/shard_map/while
  73.9 126.8 %all-gather.27.cloned.1.call-start = ((), (), s32[]{:S(2)}) async-start(), calls=%async_computation.12 | async-start | bytes 3981312 | tf_op jit(solution)/shard_map/while/body/eval_jaxpr/all_gather | solution.py:161
  98.3 178.8 %all-gather.35.cloned.1.call-start = ((), (), s32[]{:S(2)}) async-start(), calls=%async_computation.16 | async-start | bytes 1769472 | tf_op jit(solution)/shard_map/while/body/eval_jaxpr/all_gather | solution.py:289
  98.9 190.4 %all-gather.37.cloned.1.call-start = ((), (), s32[]{:S(2)}) async-start(), calls=%async_computation.17 | async-start | bytes 7077888 | tf_op jit(solution)/shard_map/while/body/eval_jaxpr/all_gather | solution.py:292
  99.6 254.0 %all-gather.39.cloned.1.call-start = ((), (), s32[]{:S(2)}) async-start(), calls=%async_computation.18 | async-start | bytes 7077888 | tf_op jit(solution)/shard_map/while/body/eval_jaxpr/all_gather | solution.py:293
  100.4 494.5 %reduce-scatter.24.cloned.1.call-start = ((), (), s32[]{:S(2)}) async-start(), calls=%async_computation.20 | async-start | bytes 3981312 | tf_op jit(solution)/shard_map/while
  105.4 183.9 %copy-start.42 = (f32[768]{0:T(1024)}, f32[768]{0:T(1024)S(1)}, u32[]{:S(2)}) copy-start(f32[768]{0:T(1024)S(1)} %reshape.235) | copy-start | bytes 9220 | tf_op jit(solution)/shard_map/while
  110.1 269.8 %copy-start.34 = (f32[768]{0:T(1024)}, f32[768]{0:T(1024)S(1)}, u32[]{:S(2)}) copy-start(f32[768]{0:T(1024)S(1)} %reshape.233) | copy-start | bytes 9220 | tf_op jit(solution)/shard_map/while
  281.7 98.3 %copy-start.30 = (f32[864]{0:T(1024)}, f32[864]{0:T(1024)S(1)}, u32[]{:S(2)}) copy-start(f32[864]{0:T(1024)S(1)} %broadcast_multiply_fusion.12) | copy-start | bytes 10372 | tf_op jit(solution)/shard_map/while
  283.6 96.3 %copy-start.38 = (f32[864]{0:T(1024)}, f32[864]{0:T(1024)S(1)}, u32[]{:S(2)}) copy-start(f32[864]{0:T(1024)S(1)} %add_rsqrt_fusion.5) | copy-start | bytes 10372 | tf_op jit(solution)/shard_map/while
  283.7 69.9 %copy-start.4 = (f32[864,768]{1,0:T(8,128)S(1)}, f32[864,768]{1,0:T(8,128)}, u32[]{:S(2)}) copy-start(f32[864,768]{1,0:T(8,128)} %copy-done.3) | copy-start | bytes 7962628 | tf_op jit(solution)/shard_map/while
  556.7 78.3 %reduce-scatter.22.cloned.1.call-start = ((), (), s32[]{:S(2)}) async-start(), calls=%async_computation.19 | async-start | bytes 3981312 | tf_op jit(solution)/shard_map/while
  559.6 117.8 %reduce-scatter.32.cloned.1.call-start = ((), (), s32[]{:S(2)}) async-start(), calls=%async_computation.24 | async-start | bytes 1769472 | tf_op jit(solution)/shard_map/while/body/eval_jaxpr/reduce_scatter | solution.py:315
  565.1 117.9 %reduce-scatter.26.cloned.1.call-start = ((), (), s32[]{:S(2)}) async-start(), calls=%async_computation.21 | async-start | bytes 1769472 | tf_op jit(solution)/shard_map/while/body/eval_jaxpr/reduce_scatter | solution.py:306
  570.0 126.4 %reduce-scatter.38.cloned.1.call-start = ((), (), s32[]{:S(2)}) async-start(), calls=%async_computation.27 | async-start | bytes 294912 | tf_op jit(solution)/shard_map/while
  573.7 61.3 %copy-start.10 = (bf16[2,864,768]{2,1,0:T(8,128)(2,1)S(1)}, bf16[2,864,768]{2,1,0:T(8,128)(2,1)}, u32[]{:S(2)}) copy-start(bf16[2,864,768]{2,1,0:T(8,128)(2,1)} %get-tuple-element.1116) | copy-start | bytes 7962628 | tf_op jit(solution)/shard_map/while
  644.9 75.4 %reduce-scatter.30.cloned.1.call-start = ((), (), s32[]{:S(2)}) async-start(), calls=%async_computation.23 | async-start | bytes 1769472 | tf_op jit(solution)/shard_map/while/body/eval_jaxpr/reduce_scatter | solution.py:312
  649.6 94.6 %reduce-scatter.28.cloned.1.call-start = ((), (), s32[]{:S(2)}) async-start(), calls=%async_computation.22 | async-start | bytes 1769472 | tf_op jit(solution)/shard_map/while/body/eval_jaxpr/reduce_scatter | solution.py:309
  653.9 152.6 %reduce-scatter.36.cloned.1.call-start = ((), (), s32[]{:S(2)}) async-start(), calls=%async_computation.26 | async-start | bytes 7077888 | tf_op jit(solution)/shard_map/while/body/eval_jaxpr/reduce_scatter | solution.py:327
  662.9 205.8 %reduce-scatter.34.cloned.1.call-start = ((), (), s32[]{:S(2)}) async-start(), calls=%async_computation.25 | async-start | bytes 7077888 | tf_op jit(solution)/shard_map/while/body/eval_jaxpr/reduce_scatter | solution.py:324
  683.1 61.1 %copy-start.16 = (f32[384,768]{1,0:T(8,128)S(1)}, f32[384,768]{1,0:T(8,128)}, u32[]{:S(2)}) copy-start(f32[384,768]{1,0:T(8,128)} %get-tuple-element.1063) | copy-start | bytes 3538948 | tf_op jit(solution)/shard_map/while
  684.6 61.0 %copy-start.19 = (f32[384,768]{1,0:T(8,128)}, f32[384,768]{1,0:T(8,128)S(1)}, u32[]{:S(2)}) copy-start(f32[384,768]{1,0:T(8,128)S(1)} %select_add_fusion.21) | copy-start | bytes 3538948 | tf_op jit(solution)/shard_map/while
  721.7 89.1 %copy-start.15 = (f32[384,768]{1,0:T(8,128)}, f32[384,768]{1,0:T(8,128)S(1)}, u32[]{:S(2)}) copy-start(f32[384,768]{1,0:T(8,128)S(1)} %select_add_fusion.23) | copy-start | bytes 3538948 | tf_op jit(solution)/shard_map/while
  745.6 65.2 %copy-start.17 = (f32[384,768]{1,0:T(8,128)}, f32[384,768]{1,0:T(8,128)S(1)}, u32[]{:S(2)}) copy-start(f32[384,768]{1,0:T(8,128)S(1)} %select_add_fusion.22) | copy-start | bytes 3538948 | tf_op jit(solution)/shard_map/while
  873.7 56.1 %copy-start.65 = (f32[2]{0:T(128)}, f32[2]{0:T(128)S(1)}, u32[]{:S(2)}) copy-start(f32[2]{0:T(128)S(1)} %get-tuple-element.1124) | copy-start | bytes 28 | tf_op jit(solution)/shard_map/while
  873.7 25.6 %all-gather.31.cloned.1.call-start = ((), (), s32[]{:S(2)}) async-start(), calls=%async_computation.14 | async-start | bytes 1769472 | tf_op jit(solution)/shard_map/while/body/eval_jaxpr/all_gather | solution.py:288
  874.3 49.5 %all-gather.25.cloned.1.call-start = ((), (), s32[]{:S(2)}) async-start(), calls=%async_computation.11 | async-start | bytes 1769472 | tf_op jit(solution)/shard_map/while/body/eval_jaxpr/all_gather | solution.py:287
  875.0 73.0 %all-gather.29.cloned.1.call-start = ((), (), s32[]{:S(2)}) async-start(), calls=%async_computation.13 | async-start | bytes 1769472 | tf_op jit(solution)/shard_map/while/body/eval_jaxpr/all_gather | solution.py:286
  875.6 113.5 %all-gather.33.cloned.1.call-start = ((), (), s32[]{:S(2)}) async-start(), calls=%async_computation.15 | async-start | bytes 3981312 | tf_op jit(solution)/shard_map/while/body/eval_jaxpr/all_gather | solution.py:162
  880.7 67.4 %copy-start.40 = (f32[768]{0:T(1024)}, f32[768]{0:T(1024)S(1)}, u32[]{:S(2)}) copy-start(f32[768]{0:T(1024)S(1)} %reshape.231) | copy-start | bytes 9220 | tf_op jit(solution)/shard_map/while
  885.8 62.3 %copy-start.32 = (f32[768]{0:T(1024)}, f32[768]{0:T(1024)S(1)}, u32[]{:S(2)}) copy-start(f32[768]{0:T(1024)S(1)} %reshape.229) | copy-start | bytes 9220 | tf_op jit(solution)/shard_map/while
  891.4 215.2 %copy-start.23 = (f32[768]{0:T(1024)}, f32[768]{0:T(1024)S(1)}, u32[]{:S(2)}) copy-start(f32[768]{0:T(1024)S(1)} %convolution_reduce_fusion.2) | copy-start | bytes 9220 | tf_op jit(solution)/shard_map/while
  893.0 55.0 %copy-start.28 = (f32[864]{0:T(1024)}, f32[864]{0:T(1024)S(1)}, u32[]{:S(2)}) copy-start(f32[864]{0:T(1024)S(1)} %broadcast_multiply_fusion.11) | copy-start | bytes 10372 | tf_op jit(solution)/shard_map/while
  903.2 127.0 %all-gather.27.cloned.1.call-start = ((), (), s32[]{:S(2)}) async-start(), calls=%async_computation.12 | async-start | bytes 3981312 | tf_op jit(solution)/shard_map/while/body/eval_jaxpr/all_gather | solution.py:161
  927.6 179.0 %all-gather.35.cloned.1.call-start = ((), (), s32[]{:S(2)}) async-start(), calls=%async_computation.16 | async-start | bytes 1769472 | tf_op jit(solution)/shard_map/while/body/eval_jaxpr/all_gather | solution.py:289
  928.3 190.4 %all-gather.37.cloned.1.call-start = ((), (), s32[]{:S(2)}) async-start(), calls=%async_computation.17 | async-start | bytes 7077888 | tf_op jit(solution)/shard_map/while/body/eval_jaxpr/all_gather | solution.py:292
  928.9 254.1 %all-gather.39.cloned.1.call-start = ((), (), s32[]{:S(2)}) async-start(), calls=%async_computation.18 | async-start | bytes 7077888 | tf_op jit(solution)/shard_map/while/body/eval_jaxpr/all_gather | solution.py:293
  929.7 494.6 %reduce-scatter.24.cloned.1.call-start = ((), (), s32[]{:S(2)}) async-start(), calls=%async_computation.20 | async-start | bytes 3981312 | tf_op jit(solution)/shard_map/while
  934.7 184.1 %copy-start.42 = (f32[768]{0:T(1024)}, f32[768]{0:T(1024)S(1)}, u32[]{:S(2)}) copy-start(f32[768]{0:T(1024)S(1)} %reshape.235) | copy-start | bytes 9220 | tf_op jit(solution)/shard_map/while
  939.3 270.1 %copy-start.34 = (f32[768]{0:T(1024)}, f32[768]{0:T(1024)S(1)}, u32[]{:S(2)}) copy-start(f32[768]{0:T(1024)S(1)} %reshape.233) | copy-start | bytes 9220 | tf_op jit(solution)/shard_map/while
  1111.1 98.3 %copy-start.30 = (f32[864]{0:T(1024)}, f32[864]{0:T(1024)S(1)}, u32[]{:S(2)}) copy-start(f32[864]{0:T(1024)S(1)} %broadcast_multiply_fusion.12) | copy-start | bytes 10372 | tf_op jit(solution)/shard_map/while
  1113.1 96.3 %copy-start.38 = (f32[864]{0:T(1024)}, f32[864]{0:T(1024)S(1)}, u32[]{:S(2)}) copy-start(f32[864]{0:T(1024)S(1)} %add_rsqrt_fusion.5) | copy-start | bytes 10372 | tf_op jit(solution)/shard_map/while
  1113.1 69.9 %copy-start.4 = (f32[864,768]{1,0:T(8,128)S(1)}, f32[864,768]{1,0:T(8,128)}, u32[]{:S(2)}) copy-start(f32[864,768]{1,0:T(8,128)} %copy-done.3) | copy-start | bytes 7962628 | tf_op jit(solution)/shard_map/while
  1386.2 78.3 %reduce-scatter.22.cloned.1.call-start = ((), (), s32[]{:S(2)}) async-start(), calls=%async_computation.19 | async-start | bytes 3981312 | tf_op jit(solution)/shard_map/while
  1389.1 117.8 %reduce-scatter.32.cloned.1.call-start = ((), (), s32[]{:S(2)}) async-start(), calls=%async_computation.24 | async-start | bytes 1769472 | tf_op jit(solution)/shard_map/while/body/eval_jaxpr/reduce_scatter | solution.py:315
  1394.6 118.1 %reduce-scatter.26.cloned.1.call-start = ((), (), s32[]{:S(2)}) async-start(), calls=%async_computation.21 | async-start | bytes 1769472 | tf_op jit(solution)/shard_map/while/body/eval_jaxpr/reduce_scatter | solution.py:306
  1399.4 126.4 %reduce-scatter.38.cloned.1.call-start = ((), (), s32[]{:S(2)}) async-start(), calls=%async_computation.27 | async-start | bytes 294912 | tf_op jit(solution)/shard_map/while
  1403.2 61.3 %copy-start.10 = (bf16[2,864,768]{2,1,0:T(8,128)(2,1)S(1)}, bf16[2,864,768]{2,1,0:T(8,128)(2,1)}, u32[]{:S(2)}) copy-start(bf16[2,864,768]{2,1,0:T(8,128)(2,1)} %get-tuple-element.1116) | copy-start | bytes 7962628 | tf_op jit(solution)/shard_map/while
  1474.4 75.6 %reduce-scatter.30.cloned.1.call-start = ((), (), s32[]{:S(2)}) async-start(), calls=%async_computation.23 | async-start | bytes 1769472 | tf_op jit(solution)/shard_map/while/body/eval_jaxpr/reduce_scatter | solution.py:312
  1479.1 94.9 %reduce-scatter.28.cloned.1.call-start = ((), (), s32[]{:S(2)}) async-start(), calls=%async_computation.22 | async-start | bytes 1769472 | tf_op jit(solution)/shard_map/while/body/eval_jaxpr/reduce_scatter | solution.py:309
  1483.3 152.9 %reduce-scatter.36.cloned.1.call-start = ((), (), s32[]{:S(2)}) async-start(), calls=%async_computation.26 | async-start | bytes 7077888 | tf_op jit(solution)/shard_map/while/body/eval_jaxpr/reduce_scatter | solution.py:327
  1492.4 206.2 %reduce-scatter.34.cloned.1.call-start = ((), (), s32[]{:S(2)}) async-start(), calls=%async_computation.25 | async-start | bytes 7077888 | tf_op jit(solution)/shard_map/while/body/eval_jaxpr/reduce_scatter | solution.py:324
  1512.7 61.3 %copy-start.16 = (f32[384,768]{1,0:T(8,128)S(1)}, f32[384,768]{1,0:T(8,128)}, u32[]{:S(2)}) copy-start(f32[384,768]{1,0:T(8,128)} %get-tuple-element.1063) | copy-start | bytes 3538948 | tf_op jit(solution)/shard_map/while
  1514.2 61.2 %copy-start.19 = (f32[384,768]{1,0:T(8,128)}, f32[384,768]{1,0:T(8,128)S(1)}, u32[]{:S(2)}) copy-start(f32[384,768]{1,0:T(8,128)S(1)} %select_add_fusion.21) | copy-start | bytes 3538948 | tf_op jit(solution)/shard_map/while
  1551.3 90.7 %copy-start.15 = (f32[384,768]{1,0:T(8,128)}, f32[384,768]{1,0:T(8,128)S(1)}, u32[]{:S(2)}) copy-start(f32[384,768]{1,0:T(8,128)S(1)} %select_add_fusion.23) | copy-start | bytes 3538948 | tf_op jit(solution)/shard_map/while
  1575.4 66.6 %copy-start.17 = (f32[384,768]{1,0:T(8,128)}, f32[384,768]{1,0:T(8,128)S(1)}, u32[]{:S(2)}) copy-start(f32[384,768]{1,0:T(8,128)S(1)} %select_add_fusion.22) | copy-start | bytes 3538948 | tf_op jit(solution)/shard_map/while
  1706.2 92.0 %all-reduce.12.cloned.1.call-start = ((), (), s32[]{:S(2)}) async-start(), calls=%async_computation.9 | async-start | bytes 139264 | tf_op jit(solution)/shard_map/psum | solution.py:341
  1706.7 358.9 %all-reduce.14.cloned.1.call-start = ((), (), s32[]{:S(2)}) async-start(), calls=%async_computation.10 | async-start | bytes 28311552 | tf_op jit(solution)/shard_map/psum | solution.py:341
  (109 other events, 1320.2 us)
Sparse Core Ops, SparseCore 0:
  49.3 20.6 all-gather.30
  71.6 22.7 all-gather.24
  96.1 22.8 all-gather.28
  120.4 39.3 all-gather.32
  161.3 39.3 all-gather.26
  202.2 22.7 all-gather.34
  226.6 62.6 all-gather.36
  290.9 62.6 all-gather.38
  556.9 37.9 reduce-scatter.23
  597.0 37.9 reduce-scatter.21
  637.4 21.7 reduce-scatter.31
  661.3 21.7 reduce-scatter.25
  685.4 10.9 reduce-scatter.37
  698.5 21.7 reduce-scatter.29
  722.4 21.7 reduce-scatter.27
  746.5 59.9 reduce-scatter.35
  808.6 59.9 reduce-scatter.33
  875.8 23.4 all-gather.30
  900.9 22.7 all-gather.24
  925.2 22.8 all-gather.28
  949.7 39.3 all-gather.32
  990.7 39.3 all-gather.26
  1031.8 22.7 all-gather.34
  1056.1 62.6 all-gather.36
  1120.4 62.6 all-gather.38
  1386.3 37.9 reduce-scatter.23
  1426.5 37.9 reduce-scatter.21
  1466.8 21.7 reduce-scatter.31
  1490.9 21.7 reduce-scatter.25
  1514.8 10.9 reduce-scatter.37
  1528.1 21.7 reduce-scatter.29
  1552.2 21.7 reduce-scatter.27
  1576.2 59.9 reduce-scatter.35
  1638.6 59.9 reduce-scatter.33
Sparse Core Ops, SparseCore 1:
  1711.8 86.3 all-reduce.11
  1805.2 260.4 all-reduce.13
where the time goes:
time: 2100 us; the launch traced here: 2090 us
  waiting for transfers between devices  1110 us (53%)
  matrix products  471 us (22%)
  local copies, waits for them, and re-layouts  208 us (10%)
  other arithmetic  169 us (8%)
  blocking collectives  92.3 us (4%)
  loops' own time  21.1 us (1%)
    psum x2, waiting for transfers between devices, body(): summed = lax.psum(running, 'dp')  358 us
    while x40, waiting for transfers between devices  131 us
    reduce_scatter x2, waiting for transfers between devices, scan_frame(): lax.psum_scatter(frame_grads[9].astype(jnp.bfloat16), 'seq', scatter_dime...  122 us
    reduce_scatter x2, waiting for transfers between devices, scan_frame(): lax.psum_scatter(frame_grads[8].astype(jnp.bfloat16), 'seq', scatter_dime...  114 us
    dot_general x12, matrix products, matmul(): return jnp.dot(left_side, right_side, preferred_element_type=jnp.float32)  114 us
    convert_element_type x12, other arithmetic, one_pair(): score_grad = (softmaxed * (prob_grad - row_inner)).astype(jnp.bfloat16)  76.2 us
    all_gather x2, waiting for transfers between devices, frame_pass(): lax.all_gather(keys, 'seq', axis=0, tiled=True)  75.3 us
    dynamic_slice x84, local copies, waits for them, and re-layouts, pair_slice(): lax.dynamic_slice_in_dim(matrix, pair_index * PAIR_WIDTH, PAIR_WIDTH, 1)  75.1 us
  transfers between devices with their start and end apart: 36, of which 32 were waited for; matrix products, arithmetic and copies ran while one was open for 19% of the time, Pallas kernels for 0%

commit v1 on v0

v1 whole, which is shorter than its diff:
```python
import functools

import jax
import jax.numpy as jnp
from jax import lax
from jax.experimental import pallas as pl
from jax.experimental.pallas import tpu as pltpu
from jax.sharding import PartitionSpec as P

HEAD_DIM = 64
PAIR = 128
EPSILON = 1e-06
LOG2E = 1.4426950408889634
SCORE_SCALE = HEAD_DIM**-0.5
EXP2_SCALE = SCORE_SCALE * LOG2E
BF = jnp.bfloat16
F32 = jnp.float32
VMEM_BYTES = 61 * 2**20
SAFE_LOG2 = 100.0


def dot(left, right):
    return jnp.dot(left, right, preferred_element_type=F32)


def dot_t(left, right):
    return lax.dot_general(left, right, (((1,), (1,)), ((), ())), preferred_element_type=F32)


def dot_l(left, right):
    return lax.dot_general(left, right, (((0,), (0,)), ((), ())), preferred_element_type=F32)


def row_mean(x):
    return jnp.mean(x, axis=1, keepdims=True)


def norm_rows(hidden):
    center = hidden - row_mean(hidden)
    inv_std = lax.rsqrt(row_mean(center * center) + EPSILON)
    return center * inv_std, inv_std


def norm_rows_back(grad_out, normed, inv_std, gain):
    scaled = grad_out * gain
    return inv_std * (scaled - row_mean(scaled) - normed * row_mean(scaled * normed))


def gelu_pair(u):
    z = jnp.abs(u) * 0.7071067811865476
    t = 1.0 / (1.0 + 0.3275911 * z)
    e = jnp.exp2(u * u * (-0.5 * LOG2E))
    poly = t * (
        0.127414796
        + t * (-0.142248368 + t * (0.7107068705 + t * (-0.7265760135 + t * 0.5307027145)))
    )
    tail = poly * e
    cdf = jnp.where(u >= 0, 1.0 - tail, tail)
    return u * cdf, cdf + u * (e * 0.3989422804014327)


def params(limit=VMEM_BYTES):
    return pltpu.CompilerParams(vmem_limit_bytes=limit)


def qkv_kernel(
    seq_axis, frame_ref, emb_ref, gain_ref, shift_ref, *rest
):
    own, other = rest[0:3], rest[3:6]
    outs = rest[6:9]
    weights, sems = rest[9:11]
    seq = lax.axis_index(seq_axis)
    half = own[0].shape[0]

    @pl.when(pl.program_id(0) == 0)
    def _():
        copies = []
        for n in range(3):
            for m, (src, place) in enumerate(((own[n], seq), (other[n], 1 - seq))):
                rows = pl.ds(pl.multiple_of(place * half, 128), half)
                copies.append(pltpu.make_async_copy(src, weights.at[n, rows, :], sems.at[n, m]))
        for copy in copies:
            copy.start()
        for copy in copies:
            copy.wait()

    hidden = frame_ref[...].astype(F32) + emb_ref[...]
    normed, _ = norm_rows(hidden)
    first_in = (normed * gain_ref[...] + shift_ref[...]).astype(BF)
    for n in range(3):
        outs[n][...] = dot(first_in, weights[n]).astype(BF)


def qkv_call(frame, emb, gain, shift, own, other, block):
    rows, width = frame.shape
    tile = pl.BlockSpec((block, width), lambda i: (i, 0))
    vec = pl.BlockSpec((1, width), lambda i: (0, 0))
    anys = pl.BlockSpec(memory_space=pl.ANY)
    return pl.pallas_call(
        functools.partial(qkv_kernel, "seq"),
        grid=(rows // block,),
        in_specs=[tile, vec, vec, vec] + [anys] * 6,
        out_specs=[tile] * 3,
        out_shape=[jax.ShapeDtypeStruct((rows, width), BF)] * 3,
        scratch_shapes=[
            pltpu.VMEM((3, width, width), BF),
            pltpu.SemaphoreType.DMA((3, 2)),
        ],
        compiler_params=params(),
    )(frame, emb, gain, shift, *own, *other)


def attend_kernel(block, q_ref, k_ref, v_ref, o_ref, l_ref, keys, values):
    rows = q_ref.shape[0]
    low = lax.broadcasted_iota(jnp.int32, (rows, PAIR), 1) < HEAD_DIM
    k = k_ref[...]
    v = v_ref[...]
    keys[0] = jnp.where(low, k, 0).astype(BF)
    keys[1] = jnp.where(low, 0, k).astype(BF)
    values[0] = jnp.where(low, v, 1).astype(BF)
    values[1] = jnp.where(low, 1, v).astype(BF)

    def longest(x):
        square = x.astype(F32) * x.astype(F32)
        first = jnp.max(jnp.sum(jnp.where(low, square, 0.0), axis=1, keepdims=True))
        second = jnp.max(jnp.sum(jnp.where(low, 0.0, square), axis=1, keepdims=True))
        return jnp.maximum(first, second)

    bound = longest(q_ref[...]) * longest(k)
    fast = bound <= (SAFE_LOG2 / EXP2_SCALE) ** 2
    low_block = lax.broadcasted_iota(jnp.int32, (block, PAIR), 1) < HEAD_DIM

    def run(shifted):
        def body(i, _):
            here = pl.ds(pl.multiple_of(i * block, block), block)
            query = q_ref[here, :]
            mixed, logs = [], []
            for h in range(2):
                scores = dot_t(query, keys[h])
                if shifted:
                    peak = jnp.max(scores, axis=1, keepdims=True)
                    scores = scores - peak
                weight = jnp.exp2(scores * EXP2_SCALE).astype(BF)
                total = dot(weight, values[h])
                turned = pltpu.roll(total, HEAD_DIM, 1)
                mixed.append(total / turned)
                log = jnp.log2(turned) * (1.0 / EXP2_SCALE)
                logs.append(log + peak if shifted else log)
            o_ref[here, :] = jnp.where(low_block, mixed[0], mixed[1]).astype(BF)
            l_ref[here, :] = jnp.where(low_block, logs[0], logs[1])
            return 0

        lax.fori_loop(0, rows // block, body, 0)

    @pl.when(fast)
    def _():
        run(False)

    @pl.when(jnp.logical_not(fast))
    def _():
        run(True)


def attend_call(queries, keys, values, block):
    rows, width = queries.shape
    tile = pl.BlockSpec((rows, PAIR), lambda i: (0, i))
    return pl.pallas_call(
        functools.partial(attend_kernel, block),
        grid=(width // PAIR,),
        in_specs=[tile] * 3,
        out_specs=[tile] * 2,
        out_shape=[
            jax.ShapeDtypeStruct((rows, width), BF),
            jax.ShapeDtypeStruct((rows, width), F32),
        ],
        scratch_shapes=[pltpu.VMEM((2, rows, PAIR), BF)] * 2,
        compiler_params=params(),
    )(queries, keys, values)


def feed_kernel(
    block, steps, seq_axis,
    frame_ref, o_ref, o_full, target_ref, emb_ref, gain_ref, shift_ref, weight_ref,
    wo_own, wo_other, wu_own, wu_other, wd_own, wd_other,
    y_ref, gh_ref, go_ref, sg_ref, ss_ref, grads,
    wo, wu, wd, act, slope, second_in, result_grad, hidden_grad, normed_s, hidden_s, acc, stage,
    sems, out_sems,
):
    i = pl.program_id(0)
    seq = lax.axis_index(seq_axis)
    width = wo.shape[0]
    half = width // 2
    chunks = act.shape[0]

    @pl.when(i == 0)
    def _():
        copies = []
        for m, (place, wo_h, wu_h, wd_h) in enumerate(
            ((seq, wo_own, wu_own, wd_own), (1 - seq, wo_other, wu_other, wd_other))
        ):
            rows = pl.ds(pl.multiple_of(place * half, 128), half)
            copies.append(pltpu.make_async_copy(wo_h, wo.at[rows, :], sems.at[m, 0]))
            for c in range(chunks):
                copies.append(
                    pltpu.make_async_copy(
                        wu_h.at[:, pl.ds(c * width, width)], wu.at[c, rows, :], sems.at[m, 1 + c]
                    )
                )
            for c in range(chunks // 2):
                copies.append(
                    pltpu.make_async_copy(
                        wd_h.at[pl.ds(c * width, width), :],
                        wd.at[place * (chunks // 2) + c],
                        sems.at[m, 1 + chunks + c],
                    )
                )
        for copy in copies:
            copy.start()
        for copy in copies:
            copy.wait()
        sg_ref[...] = jnp.zeros_like(sg_ref)
        ss_ref[...] = jnp.zeros_like(ss_ref)

    @pl.when(i < steps)
    def _():
        rows = pl.ds(pl.multiple_of(i * block, block), block)
        hidden = frame_ref[...].astype(F32) + emb_ref[...] + dot(o_ref[...], wo[...])
        normed, inv_std = norm_rows(hidden)
        normed_s[...] = normed
        second_in[rows, :] = (normed * gain_ref[...] + shift_ref[...]).astype(BF)
        acc[...] = hidden

        def forward(c, _):
            a, s = gelu_pair(dot(second_in[rows, :], wu[c]))
            a = a.astype(BF)
            act[c, rows, :] = a
            slope[c, rows, :] = s.astype(BF)
            acc[...] += dot(a, wd[c])
            return 0

        lax.fori_loop(0, chunks, forward, 0)
        result = acc[...]
        y_ref[...] = result.astype(BF)
        grad = weight_ref[0, 0] * (result - target_ref[...].astype(F32))
        result_grad[rows, :] = grad.astype(BF)
        hidden_s[...] = grad
        acc[...] = jnp.zeros_like(acc)

        def backward(c, _):
            back = dot_t(result_grad[rows, :], wd[c])
            back = (back * slope[c, rows, :].astype(F32)).astype(BF)
            slope[c, rows, :] = back
            acc[...] += dot_t(back, wu[c])
            return 0

        lax.fori_loop(0, chunks, backward, 0)
        grad = acc[...]
        normed = normed_s[...]
        ss_ref[...] += jnp.sum(grad, axis=0, keepdims=True)
        sg_ref[...] += jnp.sum(grad * normed, axis=0, keepdims=True)
        grad = hidden_s[...] + norm_rows_back(grad, normed, inv_std, gain_ref[...])
        gh_ref[...] = grad
        grad = grad.astype(BF)
        hidden_grad[rows, :] = grad
        go_ref[...] = dot_t(grad, wo[...]).astype(BF)

    def out_copies(n):
        slot = n % 2
        if n < chunks:
            at = grads.at[n // (chunks // 2), pl.ds((n % (chunks // 2)) * width, width), :]
            return [pltpu.make_async_copy(stage.at[slot], at, out_sems.at[slot, 0])]
        base = (chunks // 2) * width + (n - chunks) * half
        return [
            pltpu.make_async_copy(
                stage.at[slot, pl.ds(h * half, half), :],
                grads.at[h, pl.ds(base, half), :],
                out_sems.at[slot, h],
            )
            for h in range(2)
        ]

    last = 2 * chunks
    for n in range(last + 1):

        @pl.when(i == steps + n)
        def _():
            if n >= 2:
                for copy in out_copies(n - 2):
                    copy.wait()
            if n < chunks:
                term = dot_l(act[n], result_grad[...])
            elif n < last:
                term = dot_l(second_in[...], slope[n - chunks])
            else:
                term = dot_l(o_full[...], hidden_grad[...])
            stage[n % 2] = term.astype(BF)
            for copy in out_copies(n):
                copy.start()
            if n == last:
                for m in (n - 1, n):
                    for copy in out_copies(m):
                        copy.wait()


def feed_call(frame, attended, target, emb, gain, shift, weight, halves, grad_rows, block):
    rows, width = frame.shape
    chunks = halves[2].shape[1] // width
    steps = rows // block
    tile = pl.BlockSpec((block, width), lambda i: (jnp.minimum(i, steps - 1), 0))
    whole = pl.BlockSpec((rows, width), lambda i: (0, 0))
    vec = pl.BlockSpec((1, width), lambda i: (0, 0))
    anys = pl.BlockSpec(memory_space=pl.ANY)
    return pl.pallas_call(
        functools.partial(feed_kernel, block, steps, "seq"),
        grid=(steps + 2 * chunks + 1,),
        in_specs=[tile, tile, whole, tile, vec, vec, vec, pl.BlockSpec(memory_space=pltpu.SMEM)]
        + [anys] * 6,
        out_specs=[tile, tile, tile, vec, vec, anys],
        out_shape=[
            jax.ShapeDtypeStruct((rows, width), BF),
            jax.ShapeDtypeStruct((rows, width), F32),
            jax.ShapeDtypeStruct((rows, width), BF),
            jax.ShapeDtypeStruct((1, width), F32),
            jax.ShapeDtypeStruct((1, width), F32),
            jax.ShapeDtypeStruct((2, grad_rows, width), BF),
        ],
        scratch_shapes=[
            pltpu.VMEM((width, width), BF),
            pltpu.VMEM((chunks, width, width), BF),
            pltpu.VMEM((chunks, width, width), BF),
            pltpu.VMEM((chunks, rows, width), BF),
            pltpu.VMEM((chunks, rows, width), BF),
            pltpu.VMEM((rows, width), BF),
            pltpu.VMEM((rows, width), BF),
            pltpu.VMEM((rows, width), BF),
            pltpu.VMEM((block, width), F32),
            pltpu.VMEM((block, width), F32),
            pltpu.VMEM((block, width), F32),
            pltpu.VMEM((2, width, width), BF),
            pltpu.SemaphoreType.DMA((2, 1 + chunks + chunks // 2)),
            pltpu.SemaphoreType.DMA((2, 2)),
        ],
        compiler_params=params(),
    )(frame, attended, attended, target, emb, gain, shift, weight, *halves)


def split_three(x):
    first = x.astype(BF)
    rest = x - first.astype(F32)
    second = rest.astype(BF)
    rest = rest - second.astype(F32)
    return first, second, rest.astype(BF)


def attend_back_kernel(
    block, q_ref, k_ref, v_ref, g_ref, o_ref, l_ref, gq_ref, gk_ref, gv_ref, qm, km, vm, gm, acc
):
    rows = q_ref.shape[0]
    lane = lax.broadcasted_iota(jnp.int32, (rows, PAIR), 1)
    q, k, v, g = q_ref[...], k_ref[...], v_ref[...], g_ref[...]
    product = g.astype(F32) * o_ref[...].astype(F32)
    logs = l_ref[...]
    for h in range(2):
        inside = (lane < HEAD_DIM) if h == 0 else (lane >= HEAD_DIM)
        base = HEAD_DIM * (1 - h)
        inner = -jnp.sum(jnp.where(inside, product, 0.0), axis=1, keepdims=True)
        log = -jnp.max(jnp.where(inside, logs, -jnp.inf), axis=1, keepdims=True)

        def extend(x, terms):
            tail = jnp.zeros_like(x)
            for n, term in enumerate(terms):
                tail = jnp.where(lane == base + n, term, tail)
            return jnp.where(inside, x, tail)

        ones = jnp.where((lane >= base) & (lane < base + 3), 1.0, 0.0).astype(BF)
        qm[h] = extend(q, split_three(log))
        gm[h] = extend(g, split_three(inner))
        km[h] = jnp.where(inside, k, ones)
        vm[h] = jnp.where(inside, v, ones)
    acc[...] = jnp.zeros_like(acc)
    low_block = lax.broadcasted_iota(jnp.int32, (block, PAIR), 1) < HEAD_DIM

    def body(i, _):
        here = pl.ds(pl.multiple_of(i * block, block), block)
        value_terms, key_terms = [], []
        turned = k_ref[here, :].T
        for h in range(2):
            prob = jnp.exp2(EXP2_SCALE * dot_t(km[h, here, :], qm[h]))
            score = (prob * dot_t(vm[h, here, :], gm[h])).astype(BF)
            value_terms.append(dot(prob.astype(BF), g_ref[...]))
            key_terms.append(dot(score, q_ref[...]))
            acc[h] += dot(turned, score)
        gv_ref[here, :] = jnp.where(low_block, value_terms[0], value_terms[1]).astype(BF)
        gk_ref[here, :] = (
            SCORE_SCALE * jnp.where(low_block, key_terms[0], key_terms[1])
        ).astype(BF)
        return 0

    lax.fori_loop(0, rows // block, body, 0)
    gq_ref[...] = (SCORE_SCALE * jnp.where(lane < HEAD_DIM, acc[0].T, acc[1].T)).astype(BF)


def attend_back_call(queries, keys, values, grad, attended, logs, block):
    rows, width = queries.shape
    tile = pl.BlockSpec((rows, PAIR), lambda i: (0, i))
    return pl.pallas_call(
        functools.partial(attend_back_kernel, block),
        grid=(width // PAIR,),
        in_specs=[tile] * 6,
        out_specs=[tile] * 3,
        out_shape=[jax.ShapeDtypeStruct((rows, width), BF)] * 3,
        scratch_shapes=[pltpu.VMEM((2, rows, PAIR), BF)] * 4 + [pltpu.VMEM((2, PAIR, rows), F32)],
        compiler_params=params(),
    )(queries, keys, values, grad, attended, logs)


def qkv_back_kernel(
    block, steps, seq_axis,
    frame_ref, gh_ref, gq_ref, gk_ref, gv_ref, emb_ref, gain_ref, shift_ref, *rest
):
    own, other = rest[0:3], rest[3:6]
    gi_ref, sg_ref, ss_ref, st_ref, grads = rest[6:11]
    weights, first_in, sems = rest[11:14]
    parts = (gq_ref, gk_ref, gv_ref)
    i = pl.program_id(0)
    seq = lax.axis_index(seq_axis)
    half = own[0].shape[0]

    @pl.when(i == 0)
    def _():
        copies = []
        for n in range(3):
            for m, (src, place) in enumerate(((own[n], seq), (other[n], 1 - seq))):
                rows = pl.ds(pl.multiple_of(place * half, 128), half)
                copies.append(pltpu.make_async_copy(src, weights.at[n, rows, :], sems.at[n, m]))
        for copy in copies:
            copy.start()
        for copy in copies:
            copy.wait()
        for ref in (sg_ref, ss_ref, st_ref):
            ref[...] = jnp.zeros_like(ref)

    @pl.when(i < steps)
    def _():
        rows = pl.ds(pl.multiple_of(i * block, block), block)
        hidden = frame_ref[...].astype(F32) + emb_ref[...]
        normed, inv_std = norm_rows(hidden)
        first_in[rows, :] = (normed * gain_ref[...] + shift_ref[...]).astype(BF)
        grad = dot_t(gq_ref[rows, :], weights[0])
        grad += dot_t(gk_ref[rows, :], weights[1])
        grad += dot_t(gv_ref[rows, :], weights[2])
        ss_ref[...] += jnp.sum(grad, axis=0, keepdims=True)
        sg_ref[...] += jnp.sum(grad * normed, axis=0, keepdims=True)
        grad = gh_ref[...] + norm_rows_back(grad, normed, inv_std, gain_ref[...])
        st_ref[...] += jnp.sum(grad, axis=0, keepdims=True)
        gi_ref[...] = grad.astype(BF)

    for n in range(3):

        @pl.when(i == steps + n)
        def _():
            term = dot_l(first_in[...], parts[n][...]).astype(BF)
            grads[0, pl.ds(n * half, half), :] = term[:half]
            grads[1, pl.ds(n * half, half), :] = term[half:]


def qkv_back_call(frame, hidden_grad, gq, gk, gv, emb, gain, shift, own, other, block):
    rows, width = frame.shape
    steps = rows // block
    tile = pl.BlockSpec((block, width), lambda i: (jnp.minimum(i, steps - 1), 0))
    whole = pl.BlockSpec((rows, width), lambda i: (0, 0))
    vec = pl.BlockSpec((1, width), lambda i: (0, 0))
    anys = pl.BlockSpec(memory_space=pl.ANY)
    grad_shape = (2, 3 * (width // 2), width)
    return pl.pallas_call(
        functools.partial(qkv_back_kernel, block, steps, "seq"),
        grid=(steps + 3,),
        in_specs=[tile, tile, whole, whole, whole, vec, vec, vec] + [anys] * 6,
        out_specs=[tile, vec, vec, vec, pl.BlockSpec(grad_shape, lambda i: (0, 0, 0))],
        out_shape=[jax.ShapeDtypeStruct((rows, width), BF)]
        + [jax.ShapeDtypeStruct((1, width), F32)] * 3
        + [jax.ShapeDtypeStruct(grad_shape, BF)],
        scratch_shapes=[
            pltpu.VMEM((3, width, width), BF),
            pltpu.VMEM((rows, width), BF),
            pltpu.SemaphoreType.DMA((3, 2)),
        ],
        compiler_params=params(),
    )(frame, hidden_grad, gq, gk, gv, emb, gain, shift, *own, *other)


def body(
    frames, targets, lead_index, lead_counts,
    first_gain, first_shift, query_weight, key_weight, value_weight, output_weight,
    second_gain, second_shift, up_weight, down_weight, lead_table,
):
    seq = lax.axis_index("seq")
    swap = [(0, 1), (1, 0)]

    def trade(x):
        return lax.ppermute(x, "seq", swap)

    def pick(x, which):
        return lax.dynamic_index_in_dim(x, which, 0, keepdims=False)

    def order(mine, theirs, axis):
        return jnp.where(
            seq == 0,
            jnp.concatenate([mine, theirs], axis),
            jnp.concatenate([theirs, mine], axis),
        )

    rows, width = frames.shape[1] * 2, frames.shape[2]
    half = width // 2
    rows_here = jnp.take(lead_table, lead_index, axis=0)
    vectors = jnp.stack([first_gain, first_shift, second_gain, second_shift])
    theirs = trade(jnp.concatenate([vectors, pick(rows_here, 1 - seq)[None]]))
    mine = jnp.concatenate([vectors, pick(rows_here, seq)[None]])
    table = order(mine, theirs, 1).astype(F32)
    gain1, shift1, gain2, shift2, emb = (table[n : n + 1] for n in range(5))

    early = (query_weight, key_weight, value_weight)
    late = (output_weight, up_weight, down_weight)
    early_other = tuple(trade(w) for w in early)
    frame = jnp.concatenate([pick(frames, seq), trade(pick(frames, 1 - seq))])
    late_other = tuple(trade(w) for w in late)
    target = jnp.concatenate([pick(targets, seq), trade(pick(targets, 1 - seq))])

    totals = lax.psum(lead_counts[0].astype(F32), "dp")
    lead_weight = jnp.mean(totals) / totals
    lead = pick(lead_index, seq)
    frame_weight = pick(lead_weight, lead).reshape(1, 1)

    queries, keys, values = qkv_call(frame, emb, gain1, shift1, early, early_other, rows // 4)
    attended, logs = attend_call(queries, keys, values, rows // 2)
    halves = tuple(w for pair in zip(late, late_other) for w in pair)
    result, hidden_grad, attended_grad, sg2, ss2, grads = feed_call(
        frame, attended, target, emb, gain2, shift2, frame_weight, halves, 9 * half, rows // 6
    )
    gq, gk, gv = attend_back_call(
        queries, keys, values, attended_grad, attended, logs, rows // 2
    )
    input_grad, sg1, ss1, st, grads_early = qkv_back_call(
        frame, hidden_grad, gq, gk, gv, emb, gain1, shift1, early, early_other, rows // 4
    )

    def place(x):
        mine, theirs = x[: rows // 2], trade(x[rows // 2 :])
        return jnp.where(
            seq == 0, jnp.stack([mine, theirs]), jnp.stack([theirs, mine])
        )

    def reduce(x):
        summed = pick(x, seq).astype(F32) + trade(pick(x, 1 - seq)).astype(F32)
        return lax.psum(summed.astype(BF), "dp")

    late_sum = reduce(grads).astype(F32)
    early_sum = reduce(grads_early).astype(F32)
    rows_ff = 4 * half
    down_grad = late_sum[:rows_ff]
    up_grad = late_sum[rows_ff : 2 * rows_ff].reshape(4, half, width)
    up_grad = jnp.moveaxis(up_grad, 0, 1).reshape(half, 4 * width)
    output_grad = late_sum[2 * rows_ff :]

    hot = (jnp.arange(lead_table.shape[0]) == lead).astype(F32)
    small = jnp.concatenate([sg1, ss1, sg2, ss2, hot[:, None] * st]).reshape(-1, 2, half)
    small = small.transpose(1, 0, 2)
    small = lax.psum(pick(small, seq) + trade(pick(small, 1 - seq)), "dp")
    return (
        place(result), place(input_grad), small[0], small[1],
        early_sum[:half], early_sum[half : 2 * half], early_sum[2 * half :], output_grad,
        small[2], small[3], up_grad, down_grad, small[4:],
    )


def solution(mesh):
    weight = P("seq", None)
    vector = P("seq")
    batch = P("dp", "seq", None)
    table = P(None, "seq")
    return jax.shard_map(
        body,
        mesh=mesh,
        in_specs=(
            batch, batch, P("dp"), P("dp", None), vector, vector, weight, weight, weight, weight,
            vector, vector, weight, weight, table,
        ),
        out_specs=(
            batch, batch, vector, vector, weight, weight, weight, weight, vector, vector, weight,
            weight, table,
        ),
        check_vma=False,
    )
```

time: 2100 us -> 838 us (0.40)
  waiting for transfers between devices: 1110 us -> 396 us
  matrix products: 471 us -> 0 us
  Pallas kernels: 0 us -> 315 us
  local copies, waits for them, and re-layouts: 208 us -> 37.2 us
  other arithmetic: 169 us -> 25.9 us
  blocking collectives: 92.3 us -> 32.4 us
  loops' own time: 21.1 us -> 0 us
    dot_general x122 -> x0, matrix products: 471 us -> none  [the longest x12 114 us: matmul(): return jnp.dot(left_side, right_side, preferred_element_type=jnp.float32)]
    reduce_scatter x12 -> x0, waiting for transfers between devices: 330 us -> none  [the longest x2 122 us: scan_frame(): lax.psum_scatter(frame_grads[9].astype(jnp.bfloat16), 'seq', scatter_dime...]
    pallas_call x0 -> x5, Pallas kernels: none -> 315 us  [the longest x1 116 us: feed_call(): pl.pallas_call(functools.partial(feed_kernel, block, steps, 'seq'), grid=...]
    all_gather x16 -> x0, waiting for transfers between devices: 289 us -> none  [the longest x2 75.3 us: frame_pass(): lax.all_gather(keys, 'seq', axis=0, tiled=True)]
    ppermute x0 -> x14, waiting for transfers between devices: none -> 181 us  [trade(): return lax.ppermute(x, 'seq', swap)]
    psum x2, waiting for transfers between devices: 358 us -> 215 us  [the longest x1 147 us: reduce(): return lax.psum(summed.astype(BF), 'dp')]
    while x40 -> x0, waiting for transfers between devices: 131 us -> none
    dynamic_slice x110 -> x3, local copies, waits for them, and re-layouts: 90.7 us -> 1.18 us  [pick(): return lax.dynamic_index_in_dim(x, which, 0, keepdims=False)]
  transfers between devices with their start and end apart: 36 -> 16, of which waited for: 32 -> 6; matrix products, arithmetic and copies ran while one was open for 19% -> 5% of each run, Pallas kernels for 0% -> 24%
where the time goes in v1:
time: 838 us; the launch traced here: 840 us
  waiting for transfers between devices  396 us (47%)
  Pallas kernels  315 us (38%)
  local copies, waits for them, and re-layouts  37.2 us (4%)
  blocking collectives  32.4 us (4%)
  other arithmetic  25.9 us (3%)
  between operations  17.2 us (2%)
  starting transfers between devices  16.8 us (2%)
    ppermute x14, waiting for transfers between devices, trade(): return lax.ppermute(x, 'seq', swap)  181 us
    psum x1, waiting for transfers between devices, reduce(): return lax.psum(summed.astype(BF), 'dp')  147 us
    pallas_call x1, Pallas kernels, feed_call(): pl.pallas_call(functools.partial(feed_kernel, block, steps, 'seq'), grid=...  116 us
    pallas_call x1, Pallas kernels, attend_back_call(): pl.pallas_call(functools.partial(attend_back_kernel, block), grid=(width...  108 us
    psum x1, waiting for transfers between devices, body(): small = lax.psum(pick(small, seq) + trade(pick(small, 1 - seq)), 'dp')  68.4 us
    pallas_call x1, Pallas kernels, attend_call(): pl.pallas_call(functools.partial(attend_kernel, block), grid=(width // PA...  53.9 us
    psum x1, blocking collectives, body(): totals = lax.psum(lead_counts[0].astype(F32), 'dp')  32.4 us
    pallas_call x1, Pallas kernels, qkv_back_call(): pl.pallas_call(functools.partial(qkv_back_kernel, block, steps, 'seq'), g...  25.2 us
  transfers between devices with their start and end apart: 16, of which 6 were waited for; matrix products, arithmetic and copies ran while one was open for 5% of the time, Pallas kernels for 24%

profile of v1, /device:TPU:0, one launch (start us, length us, event | category | flops | bytes accessed | tf_op | source)
XLA Modules:
  0.0 840.2 jit_solution(14060964997814137645)
XLA Ops:
  7.2 0.0 copy-start
  7.2 0.0 all-reduce.4.cloned.1.call-start
  7.2 3.0 collective-permute-start.2
  10.2 0.1 collective-permute-start.7
  10.3 1.9 collective-permute-start.8
  12.3 3.0 dynamic-slice_bitcast_fusion.5
  15.3 0.1 collective-permute-start
  15.4 0.6 gather_fusion
  16.0 0.1 broadcast_select_fusion
  16.2 0.0 copy-start.16
  16.2 2.0 collective-permute-start.1
  18.2 3.0 dynamic-slice_bitcast_fusion.3
  21.3 132.3 %collective-permute-done.1 = bf16[5,384]{1,0:T(8,128)(2,1)S(1)} collective-permute-done((bf16[5,384]{1,0:T(8,128)(2,1)S(1)}, bf16[5,384]{1,0:T(8,128)(2,1)S(1)}, u32[]{:S(2)}, u32[]{:S(2)}) %collective-permute-start.1) | collective-permute-done | bytes 3872 | tf_op jit(solution)/shard_map/ppermute | solution.py:501
  153.5 1.7 collective-permute-start.5
  155.3 0.3 collective-permute-start.3
  155.6 0.6 dynamic_slice.51
  158.1 32.4 %psum.28 = f32[40]{0:T(128)S(1)} all-reduce(f32[40]{0:T(128)S(1)} %convert_bitcast_fusion), channel_id=1, replica_groups=mesh['dp'=16,'seq'=2] {'dp'}, use_global_device_ids=true, to_apply=%region_0.1 | all-reduce | flops 40 | bytes 320 | tf_op jit(solution)/shard_map/psum | solution.py:529
  190.5 0.6 reduce_sum.9
  191.8 0.6 dynamic_slice.52
  192.4 4.5 collective-permute-done.3.rest_4_
  196.9 1.4 collective-permute-start.4
  198.3 0.6 fusion.5
  198.9 0.6 collective-permute-start.6
  199.5 3.0 pad_maximum_fusion.frame_ref
  202.5 10.8 %collective-permute-done.4.rest_5_ = bf16[384,768]{1,0:T(8,128)(2,1)S(1)} collective-permute-done((bf16[384,768]{1,0:T(8,128)(2,1)}, bf16[384,768]{1,0:T(8,128)(2,1)S(1)}, u32[]{:S(2)}, u32[]{:S(2)}) %collective-permute-start.4) | collective-permute-done | bytes 589856 | tf_op jit(solution)/shard_map/ppermute | solution.py:501
  213.3 0.8 copy-done.5
  214.1 12.3 %shard_map.246 = (bf16[1728,768]{1,0:T(8,128)(2,1)}, bf16[1728,768]{1,0:T(8,128)(2,1)}, bf16[1728,768]{1,0:T(8,128)(2,1)}) custom-call(bf16[1728,768]{1,0:T(8,128)(2,1)} %pad_maximum_fusion.frame_ref, f32[1,768]{1,0:T(1,128)} %get-tuple-element.76.emb_ref, f32[1,768]{1,0:T(1,128)} %get-tuple-element.75.gain_ref, f32[1,768]{1,0:T(1,128)} %get-tuple-element.74.shift_ref, ...), custom_call_target="tpu_custom_call" | custom-call | tf_op jit(solution)/shard_map/pallas_call | solution.py:99
  226.4 53.9 %shard_map.247 = (bf16[1728,768]{1,0:T(8,128)(2,1)}, f32[1728,768]{1,0:T(8,128)}) custom-call(bf16[1728,768]{1,0:T(8,128)(2,1)} %get-tuple-element.32.q_ref, bf16[1728,768]{1,0:T(8,128)(2,1)} %get-tuple-element.33.k_ref, bf16[1728,768]{1,0:T(8,128)(2,1)} %get-tuple-element.34.v_ref), custom_call_target="tpu_custom_call" | custom-call | tf_op jit(solution)/shard_map/pallas_call | solution.py:167
  280.3 3.0 pad_maximum_fusion.1.target_ref
  283.4 115.8 %shard_map.248 = (bf16[1728,768]{1,0:T(8,128)(2,1)}, f32[1728,768]{1,0:T(8,128)}, bf16[1728,768]{1,0:T(8,128)(2,1)}, f32[1,768]{1,0:T(1,128)}, f32[1,768]{1,0:T(1,128)}, /*index=5*/bf16[2,3456,768]{2,1,0:T(8,128)(2,1)}) custom-call(bf16[1728,768]{1,0:T(8,128)(2,1)} %pad_maximum_fusion.frame_ref, bf16[1728,768]{1,0:T(8,128)(2,1)} %get-tuple-element.35.o_ref.o_full, ...), custom_call_target="tpu_custom_call" | custom-call | tf_op jit(solution)/shard_map/pallas_call | solution.py:313
  399.2 5.2 dynamic-slice_bitcast_fusion
  404.4 1.4 collective-permute-start.13
  405.8 108.0 %shard_map.249 = (bf16[1728,768]{1,0:T(8,128)(2,1)}, bf16[1728,768]{1,0:T(8,128)(2,1)}, bf16[1728,768]{1,0:T(8,128)(2,1)}) custom-call(bf16[1728,768]{1,0:T(8,128)(2,1)} %get-tuple-element.32.q_ref, bf16[1728,768]{1,0:T(8,128)(2,1)} %get-tuple-element.33.k_ref, bf16[1728,768]{1,0:T(8,128)(2,1)} %get-tuple-element.34.v_ref, ...), custom_call_target="tpu_custom_call" | custom-call | tf_op jit(solution)/shard_map/pallas_call | solution.py:406
  513.8 25.2 %shard_map.250 = (bf16[1728,768]{1,0:T(8,128)(2,1)}, f32[1,768]{1,0:T(1,128)}, f32[1,768]{1,0:T(1,128)}, f32[1,768]{1,0:T(1,128)}, bf16[2,1152,768]{2,1,0:T(8,128)(2,1)}) custom-call(bf16[1728,768]{1,0:T(8,128)(2,1)} %pad_maximum_fusion.frame_ref, f32[1728,768]{1,0:T(8,128)} %get-tuple-element.37.gh_ref, bf16[1728,768]{1,0:T(8,128)(2,1)} %get-tuple-element.40.gq_ref, ...), custom_call_target="tpu_custom_call" | custom-call | tf_op jit(solution)/shard_map/pallas_call | solution.py:475
  539.1 0.0 copy-start.10
  539.1 2.8 dynamic-slice_bitcast_fusion.1
  541.9 0.6 collective-permute-start.12
  542.6 0.6 compare_convert_fusion
  543.3 0.1 broadcast_multiply_fusion
  543.4 0.2 concatenate.29
  543.6 0.1 reshape.59
  543.6 0.1 constant_dynamic-slice_fusion.1
  543.8 1.5 collective-permute-start.11
  545.3 33.0 %collective-permute-done.11 = f32[44,384]{1,0:T(8,128)S(1)} collective-permute-done((f32[44,384]{1,0:T(8,128)S(1)}, f32[44,384]{1,0:T(8,128)S(1)}, u32[]{:S(2)}, u32[]{:S(2)}) %collective-permute-start.11) | collective-permute-done | bytes 67616 | tf_op jit(solution)/shard_map/ppermute | solution.py:501
  578.2 0.6 bitcast_add_fusion
  578.9 0.0 all-reduce.4.cloned.1.call-update
  578.9 0.0 all-reduce.6.cloned.1.call-start
  579.0 3.1 fusion.1
  582.1 7.8 fusion
  589.9 0.0 all-reduce.6.cloned.1.call-update
  589.9 3.1 slice_bitcast_fusion.1
  593.0 1.3 collective-permute-start.9
  594.3 1.2 slice_bitcast_fusion
  595.5 0.8 collective-permute-start.10
  596.3 68.4 %all-reduce.4.cloned.1.call-done = f32[44,384]{1,0:T(8,128)} async-done(((f32[44,384]{1,0:T(8,128)}), f32[44,384]{1,0:T(8,128)}) %all-reduce.4.cloned.1.call-update) | async-done | bytes 67600 | tf_op jit(solution)/shard_map/psum | solution.py:568
  664.6 1.5 slice.97
  666.1 1.5 slice_reduce_fusion
  667.6 3.5 maximum_select_fusion
  671.1 3.4 maximum_select_fusion.1
  674.5 146.6 %all-reduce.6.cloned.1.call-done = (bf16[1152,768]{1,0:T(8,128)(2,1)}, bf16[3456,768]{1,0:T(8,128)(2,1)}) async-done(((bf16[1152,768]{1,0:T(8,128)(2,1)}, bf16[3456,768]{1,0:T(8,128)(2,1)}), (bf16[1152,768]{1,0:T(8,128)(2,1)}, bf16[3456,768]{1,0:T(8,128)(2,1)})) %all-reduce.6.cloned.1.call-update) | async-done | bytes 7077904 | tf_op jit(solution)/shard_map/psum | solution.py:555
  821.1 2.2 slice.92
  823.3 5.3 fusion.3
  828.6 1.9 fusion.4
  830.5 2.7 copy.32
  (55 shorter events, 0.3 us)
Async XLA Ops:
  7.2 8.2 copy-start
  7.2 657.4 %all-reduce.4.cloned.1.call-start = ((), (), s32[]{:S(2)}) async-start(), calls=%async_computation | async-start | bytes 147456 | tf_op jit(solution)/shard_map/psum | solution.py:568
  7.2 148.0 %collective-permute-start.2 = (bf16[384,768]{1,0:T(8,128)(2,1)}, bf16[384,768]{1,0:T(8,128)(2,1)}, u32[]{:S(2)}, u32[]{:S(2)}) collective-permute-start(bf16[384,768]{1,0:T(8,128)(2,1)} %rest_0_.3), channel_id=1, source_target_pairs={{0,1},{1,0},{2,3},{3,2},{4,5},{5,4},{6,7},{7,6},{8,9},{9,8},{10,11... | collective-permute-start | bytes 1769480 | tf_op jit(solution)/shard_map/ppermute | solution.py:501
  10.2 273.1 %collective-permute-start.7 = (bf16[384,3072]{1,0:T(8,128)(2,1)}, bf16[384,3072]{1,0:T(8,128)(2,1)}, u32[]{:S(2)}, u32[]{:S(2)}) collective-permute-start(bf16[384,3072]{1,0:T(8,128)(2,1)} %wu_own.1), channel_id=1, source_target_pairs={{0,1},{1,0},{2,3},{3,2},{4,5},{5,4},{6,7},{7,6},{8,9},{9,8},{10,11... | collective-permute-start | bytes 7077896 | tf_op jit(solution)/shard_map/ppermute | solution.py:501
  10.3 273.0 %collective-permute-start.8 = (bf16[1536,768]{1,0:T(8,128)(2,1)}, bf16[1536,768]{1,0:T(8,128)(2,1)}, u32[]{:S(2)}, u32[]{:S(2)}) collective-permute-start(bf16[1536,768]{1,0:T(8,128)(2,1)} %wd_own.1), channel_id=1, source_target_pairs={{0,1},{1,0},{2,3},{3,2},{4,5},{5,4},{6,7},{7,6},{8,9},{9,8},{10,11... | collective-permute-start | bytes 7077896 | tf_op jit(solution)/shard_map/ppermute | solution.py:501
  12.3 3.1 copy-start.15
  12.3 3.8 copy-start.11
  12.3 3.8 copy-start.12
  12.3 3.8 copy-start.13
  12.3 3.8 copy-start.14
  15.3 183.6 %collective-permute-start = (bf16[864,768]{1,0:T(8,128)(2,1)}, bf16[864,768]{1,0:T(8,128)(2,1)}, u32[]{:S(2)}, u32[]{:S(2)}) collective-permute-start(bf16[864,768]{1,0:T(8,128)(2,1)} %get-tuple-element.66), channel_id=1, source_target_pairs={{0,1},{1,0},{2,3},{3,2},{4,5},{5,4},{6,7},{7,6},{8,9},{9,8},{10,11... | collective-permute-start | bytes 3981320 | tf_op jit(solution)/shard_map/ppermute | solution.py:501
  16.2 139.1 %copy-start.4 = (bf16[384,768]{1,0:T(8,128)(2,1)S(1)}, bf16[384,768]{1,0:T(8,128)(2,1)}, u32[]{:S(2)}) copy-start(bf16[384,768]{1,0:T(8,128)(2,1)} %rest_1_.3) | copy-start | bytes 1769476
  16.2 141.9 %copy-start.16 = (s32[1,40]{1,0:T(1,128)S(1)}, s32[1,40]{1,0:T(1,128)}, u32[]{:S(2)}) copy-start(s32[1,40]{1,0:T(1,128)} %param.18) | copy-start | bytes 484
  16.2 137.3 %collective-permute-start.1 = (bf16[5,384]{1,0:T(8,128)(2,1)S(1)}, bf16[5,384]{1,0:T(8,128)(2,1)S(1)}, u32[]{:S(2)}, u32[]{:S(2)}) collective-permute-start(bf16[5,384]{1,0:T(8,128)(2,1)S(1)} %concatenate.25), channel_id=1, source_target_pairs={{0,1},{1,0},{2,3},{3,2},{4,5},{5,4},{6,7},{7,6},{8,9},{9,8},{10,11... | collective-permute-start | bytes 11528 | tf_op jit(solution)/shard_map/ppermute | solution.py:501
  153.5 126.8 %collective-permute-start.5 = (bf16[864,768]{1,0:T(8,128)(2,1)}, bf16[864,768]{1,0:T(8,128)(2,1)}, u32[]{:S(2)}, u32[]{:S(2)}) collective-permute-start(bf16[864,768]{1,0:T(8,128)(2,1)} %get-tuple-element.64), channel_id=1, source_target_pairs={{0,1},{1,0},{2,3},{3,2},{4,5},{5,4},{6,7},{7,6},{8,9},{9,8},{10,11... | collective-permute-start | bytes 3981320 | tf_op jit(solution)/shard_map/ppermute | solution.py:501
  155.3 41.6 %collective-permute-start.3 = (bf16[384,768]{1,0:T(8,128)(2,1)S(1)}, bf16[384,768]{1,0:T(8,128)(2,1)}, u32[]{:S(2)}, u32[]{:S(2)}) collective-permute-start(bf16[384,768]{1,0:T(8,128)(2,1)S(1)} %copy-done.4), channel_id=1, source_target_pairs={{0,1},{1,0},{2,3},{3,2},{4,5},{5,4},{6,7},{7,6},{8,9},{9,8},{10,11... | collective-permute-start | bytes 1769480 | tf_op jit(solution)/shard_map/ppermute | solution.py:501
  196.9 16.5 %collective-permute-start.4 = (bf16[384,768]{1,0:T(8,128)(2,1)}, bf16[384,768]{1,0:T(8,128)(2,1)S(1)}, u32[]{:S(2)}, u32[]{:S(2)}) collective-permute-start(bf16[384,768]{1,0:T(8,128)(2,1)} %rest_2_.3), channel_id=1, source_target_pairs={{0,1},{1,0},{2,3},{3,2},{4,5},{5,4},{6,7},{7,6},{8,9},{9,8},{10,11... | collective-permute-start | bytes 1769480 | tf_op jit(solution)/shard_map/ppermute | solution.py:501
  198.9 84.4 %collective-permute-start.6 = (bf16[384,768]{1,0:T(8,128)(2,1)}, bf16[384,768]{1,0:T(8,128)(2,1)}, u32[]{:S(2)}, u32[]{:S(2)}) collective-permute-start(bf16[384,768]{1,0:T(8,128)(2,1)} %wo_own.1), channel_id=1, source_target_pairs={{0,1},{1,0},{2,3},{3,2},{4,5},{5,4},{6,7},{7,6},{8,9},{9,8},{10,11... | collective-permute-start | bytes 1769480 | tf_op jit(solution)/shard_map/ppermute | solution.py:501
  213.3 0.8 copy-start.5
  404.4 177.7 %collective-permute-start.13 = (bf16[3456,768]{1,0:T(8,128)(2,1)}, bf16[3456,768]{1,0:T(8,128)(2,1)}, u32[]{:S(2)}, u32[]{:S(2)}) collective-permute-start(bf16[3456,768]{1,0:T(8,128)(2,1)} %dynamic-slice_bitcast_fusion), channel_id=1, source_target_pairs={{0,1},{1,0},{2,3},{3,2},{4,5},{5,4},{6,7},{7,6},{8,9},{9,8},{10,11... | collective-permute-start | bytes 15925256 | tf_op jit(solution)/shard_map/ppermute | solution.py:501
  539.1 4.1 copy-start.10
  539.1 4.2 copy-start.6
  539.1 4.2 copy-start.7
  539.1 4.2 copy-start.8
  539.1 4.2 copy-start.9
  541.9 37.0 %collective-permute-start.12 = (bf16[1152,768]{1,0:T(8,128)(2,1)}, bf16[1152,768]{1,0:T(8,128)(2,1)S(1)}, u32[]{:S(2)}, u32[]{:S(2)}) collective-permute-start(bf16[1152,768]{1,0:T(8,128)(2,1)} %dynamic-slice_bitcast_fusion.1), channel_id=1, source_target_pairs={{0,1},{1,0},{2,3},{3,2},{4,5},{5,4},{6,7},{7,6},{8,9},{9,8},{10,11... | collective-permute-start | bytes 5308424 | tf_op jit(solution)/shard_map/ppermute | solution.py:501
  543.8 34.4 %collective-permute-start.11 = (f32[44,384]{1,0:T(8,128)S(1)}, f32[44,384]{1,0:T(8,128)S(1)}, u32[]{:S(2)}, u32[]{:S(2)}) collective-permute-start(f32[44,384]{1,0:T(8,128)S(1)} %bitcast.40), channel_id=1, source_target_pairs={{0,1},{1,0},{2,3},{3,2},{4,5},{5,4},{6,7},{7,6},{8,9},{9,8},{10,11... | collective-permute-start | bytes 202760 | tf_op jit(solution)/shard_map/ppermute | solution.py:501
  578.9 242.2 %all-reduce.6.cloned.1.call-start = ((), (), s32[]{:S(2)}) async-start(), calls=%async_computation.1 | async-start | bytes 14155776 | tf_op jit(solution)/shard_map/psum | solution.py:555
  589.9 4.4 copy-start.3
  593.0 74.6 %collective-permute-start.9 = (bf16[864,768]{1,0:T(8,128)(2,1)}, bf16[864,768]{1,0:T(8,128)(2,1)}, u32[]{:S(2)}, u32[]{:S(2)}) collective-permute-start(bf16[864,768]{1,0:T(8,128)(2,1)} %get-tuple-element.62), channel_id=1, source_target_pairs={{0,1},{1,0},{2,3},{3,2},{4,5},{5,4},{6,7},{7,6},{8,9},{9,8},{10,11... | collective-permute-start | bytes 3981320 | tf_op jit(solution)/shard_map/ppermute | solution.py:501
  595.5 75.6 %collective-permute-start.10 = (bf16[864,768]{1,0:T(8,128)(2,1)}, bf16[864,768]{1,0:T(8,128)(2,1)}, u32[]{:S(2)}, u32[]{:S(2)}) collective-permute-start(bf16[864,768]{1,0:T(8,128)(2,1)} %get-tuple-element.60), channel_id=1, source_target_pairs={{0,1},{1,0},{2,3},{3,2},{4,5},{5,4},{6,7},{7,6},{8,9},{9,8},{10,11... | collective-permute-start | bytes 3981320 | tf_op jit(solution)/shard_map/ppermute | solution.py:501
  823.3 5.3 copy-start.2
  830.5 2.7 copy-start.1
Sparse Core Ops, SparseCore 0:
  579.0 85.5 all-reduce.3
  669.5 151.6 all-reduce.5

commit v2 on v1

--- a/solution.py
+++ b/solution.py
@@ -61,6 +61,231 @@
 
 def params(limit=VMEM_BYTES):
     return pltpu.CompilerParams(vmem_limit_bytes=limit)
+
+
+def reduce_parts(rows, dp):
+    bits = dp.bit_length() - 1
+    unit = 16 * dp
+    units = rows // unit
+    middle = list(range(1, bits))
+    orders = [["seq"] + middle, middle + ["seq"], middle[1:] + ["seq"] + middle[:1]]
+    sizes = [(units + 2 - n) // 3 for n in range(3)]
+    parts, base = [], 0
+    for size, order in zip(sizes, orders):
+        if size > 0:
+            parts.append((base, size * unit, [0] + order))
+            base += size * unit
+    return parts
+
+
+def padded_rows(rows, dp):
+    unit = 16 * dp
+    return -(-rows // unit) * unit
+
+
+class Place:
+    def __init__(self, dp):
+        self.bits = dp.bit_length() - 1
+        self.dp = lax.axis_index("dp")
+        self.seq = lax.axis_index("seq")
+
+    def bit(self, key):
+        return self.seq if key == "seq" else (self.dp // (1 << key)) % 2
+
+    def partner(self, key):
+        if key == "seq":
+            return (self.dp, 1 - self.seq)
+        return (self.dp + (1 << key) * (1 - 2 * self.bit(key)), self.seq)
+
+    def meet(self):
+        barrier = pltpu.get_barrier_semaphore()
+        keys = ["seq"] + list(range(self.bits))
+        for key in keys:
+            pl.semaphore_signal(
+                barrier, inc=1, device_id=self.partner(key), device_id_type=pl.DeviceIdType.MESH
+            )
+        pl.semaphore_wait(barrier, len(keys))
+
+
+def reduce_scratch(parts, width):
+    shapes = []
+    for _, rows, order in parts:
+        lead, n = 2, rows // 2
+        shapes += [pltpu.VMEM((2, n, width), BF), pltpu.VMEM((2, n, width), BF)]
+        for key in order[1:]:
+            lead, n = (1, n) if key == "seq" else (lead, n // 2)
+            shapes.append(pltpu.VMEM((lead, n, width), BF))
+    steps = max(len(order) for _, _, order in parts)
+    shapes += [pltpu.SemaphoreType.DMA((len(parts), 2 * steps, 2))]
+    shapes += [pltpu.SemaphoreType.DMA((len(parts), 2))]
+    return shapes
+
+
+class Reducer:
+    def __init__(self, place, part, index, source, out, refs, sems, local_sems):
+        self.place, self.index, self.source, self.out = place, index, source, out
+        self.base, self.rows, self.order = part
+        self.acc, self.landing = refs[0], refs[1:]
+        self.sems, self.local = sems, local_sems
+        self.copies = {}
+        half = self.rows // 2
+        seq = place.seq
+        off, n, cut = 0, half, False
+        self.plan = []
+        for key in self.order[1:]:
+            if key == "seq":
+                leave = (pl.ds(1 - seq, 1), pl.ds(off, n))
+                cut = True
+                stay = (pl.ds(seq, 1), pl.ds(off, n))
+            else:
+                n //= 2
+                bit = place.bit(key)
+                lead = pl.ds(seq, 1) if cut else slice(None)
+                leave = (lead, pl.ds(self.row(off + (1 - bit) * n), n))
+                off = self.row(off + bit * n)
+                stay = (lead, pl.ds(off, n))
+            self.plan.append((key, leave, stay))
+        self.final_off, self.final_rows = off, n
+
+    @staticmethod
+    def row(x):
+        return x if isinstance(x, int) else pl.multiple_of(x, 16)
+
+    def absolute(self, off):
+        return pl.multiple_of(self.base + self.place.bit(0) * (self.rows // 2) + off, 16)
+
+    def remote(self, step, src, dst, key):
+        return pltpu.make_async_remote_copy(
+            src_ref=src,
+            dst_ref=dst,
+            send_sem=self.sems.at[self.index, step, 0],
+            recv_sem=self.sems.at[self.index, step, 1],
+            device_id=self.place.partner(key),
+            device_id_type=pl.DeviceIdType.MESH,
+        )
+
+    def scatter(self, step):
+        if step == 0:
+            half = self.rows // 2
+            there = pl.multiple_of(self.base + (1 - self.place.bit(0)) * half, 16)
+            return self.remote(0, self.source.at[:, pl.ds(there, half), :], self.landing[0], 0)
+        key, leave, _ = self.plan[step - 1]
+        return self.remote(step, self.acc.at[leave[0], leave[1], :], self.landing[step], key)
+
+    def keep_copy(self):
+        half = self.rows // 2
+        here = pl.multiple_of(self.base + self.place.bit(0) * half, 16)
+        return pltpu.make_async_copy(
+            self.source.at[:, pl.ds(here, half), :], self.acc, self.local.at[self.index, 0]
+        )
+
+    def final_copy(self):
+        return pltpu.make_async_copy(
+            self.acc.at[self.place.seq, pl.ds(self.final_off, self.final_rows), :],
+            self.out.at[pl.ds(self.absolute(self.final_off), self.final_rows), :],
+            self.local.at[self.index, 1],
+        )
+
+    def gather(self, j):
+        keys = [key for key in reversed(self.order) if key != "seq"]
+        off, n = self.absolute(self.final_off), self.final_rows
+        for key in keys[:j]:
+            off = off - self.place.bit(key) * n
+            n *= 2
+        off = pl.multiple_of(off, 16)
+        if j == 0:
+            src = self.acc.at[self.place.seq, pl.ds(self.final_off, n), :]
+        else:
+            src = self.out.at[pl.ds(off, n), :]
+        return self.remote(len(self.order) + j, src, self.out.at[pl.ds(off, n), :], keys[j])
+
+    def add(self, step):
+        landing = self.landing[step]
+        if step == 0:
+            lead, rows = (0, 2), pl.ds(0, self.rows // 2)
+            first = 0
+        else:
+            _, _, stay = self.plan[step - 1]
+            first = stay[0].start if isinstance(stay[0], pl.Slice) else 0
+            lead, rows = (0, landing.shape[0]), stay[1]
+        n = landing.shape[1]
+        size = 32 if n % 32 == 0 else 16
+        start = rows.start
+        for m in range(lead[1]):
+
+            def some(i, _):
+                at = pl.multiple_of(i * size, size)
+                here = pl.ds(pl.multiple_of(start + at, 16), size)
+                self.acc[first + m, here, :] = (
+                    self.acc[first + m, here, :] + landing[m, pl.ds(at, size), :]
+                )
+                return 0
+
+            lax.fori_loop(0, n // size, some, 0)
+
+    def events(self):
+        steps = len(self.order)
+        gathers = self.place.bits
+
+        def begin():
+            self.keep_copy().start()
+            self.scatter(0).start()
+
+        def middle(step):
+            def run():
+                if step == 1:
+                    self.keep_copy().wait()
+                self.scatter(step - 1).wait_recv()
+                self.add(step - 1)
+                if step < steps:
+                    self.scatter(step).start()
+                else:
+                    self.final_copy().start()
+                    self.gather(0).start()
+
+            return run
+
+        def onward(j):
+            def run():
+                if j == 1:
+                    self.final_copy().wait()
+                self.gather(j - 1).wait_recv()
+                self.gather(j).start()
+
+            return run
+
+        def finish():
+            self.gather(gathers - 1).wait_recv()
+            for step in range(steps):
+                self.scatter(step).wait_send()
+            for j in range(gathers):
+                self.gather(j).wait_send()
+
+        return (
+            [begin]
+            + [middle(step) for step in range(1, steps + 1)]
+            + [onward(j) for j in range(1, gathers)]
+            + [finish]
+        )
+
+
+def reducers(place, parts, source, out, refs):
+    sems, local_sems = refs[-2:]
+    made, at = [], 0
+    for index, part in enumerate(parts):
+        count = 1 + len(part[2])
+        made.append(Reducer(place, part, index, source, out, refs[at : at + count], sems, local_sems))
+        at += count
+    return made
+
+
+def spread(count, slots, weights=None):
+    weights = weights or [1.0] * (count - 1)
+    total, at, out = sum(weights), 0.0, [0]
+    for weight in weights:
+        at += weight
+        out.append(min(slots - 1, round(at / total * (slots - 1))))
+    return out
 
 
 def qkv_kernel(
@@ -220,6 +445,21 @@
             copy.wait()
         sg_ref[...] = jnp.zeros_like(sg_ref)
         ss_ref[...] = jnp.zeros_like(ss_ref)
+        spare = grads.shape[1] - (2 * chunks + 1) * half
+        if spare > 0:
+            stage[0] = jnp.zeros_like(stage[0])
+            fills = [
+                pltpu.make_async_copy(
+                    stage.at[0, pl.ds(0, spare), :],
+                    grads.at[h, pl.ds((2 * chunks + 1) * half, spare), :],
+                    out_sems.at[0, h],
+                )
+                for h in range(2)
+            ]
+            for fill in fills:
+                fill.start()
+            for fill in fills:
+                fill.wait()
 
     @pl.when(i < steps)
     def _():
@@ -353,65 +593,95 @@
 
 
 def attend_back_kernel(
-    block, q_ref, k_ref, v_ref, g_ref, o_ref, l_ref, gq_ref, gk_ref, gv_ref, qm, km, vm, gm, acc
+    dp, parts, q_ref, k_ref, v_ref, g_ref, o_ref, l_ref, source, gq_ref, gk_ref, gv_ref, out,
+    qm, km, vm, gm, acc, *refs
 ):
     rows = q_ref.shape[0]
+    pair, i = pl.program_id(0), pl.program_id(1)
+    pairs, blocks = pl.num_programs(0), pl.num_programs(1)
+    block = gv_ref.shape[0]
+    slot = pair * blocks + i
+    slots = 6 * (rows // block)
+    place = Place(dp)
+
+    @pl.when(slot == 0)
+    def _():
+        place.meet()
+
+    for reducer in reducers(place, parts, source, out, refs):
+        events = reducer.events()
+        for at, event in zip(spread(len(events), slots, REDUCE_WEIGHTS(len(events))), events):
+            pl.when(slot == at)(event)
+
     lane = lax.broadcasted_iota(jnp.int32, (rows, PAIR), 1)
-    q, k, v, g = q_ref[...], k_ref[...], v_ref[...], g_ref[...]
-    product = g.astype(F32) * o_ref[...].astype(F32)
-    logs = l_ref[...]
+
+    @pl.when(i == 0)
+    def _():
+        q, k, v, g = q_ref[...], k_ref[...], v_ref[...], g_ref[...]
+        product = g.astype(F32) * o_ref[...].astype(F32)
+        logs = l_ref[...]
+        for h in range(2):
+            inside = (lane < HEAD_DIM) if h == 0 else (lane >= HEAD_DIM)
+            base = HEAD_DIM * (1 - h)
+            inner = -jnp.sum(jnp.where(inside, product, 0.0), axis=1, keepdims=True)
+            log = -jnp.max(jnp.where(inside, logs, -jnp.inf), axis=1, keepdims=True)
+
+            def extend(x, terms):
+                tail = jnp.zeros_like(x)
+                for n, term in enumerate(terms):
+                    tail = jnp.where(lane == base + n, term, tail)
+                return jnp.where(inside, x, tail)
+
+            ones = jnp.where((lane >= base) & (lane < base + 3), 1.0, 0.0).astype(BF)
+            qm[h] = extend(q, split_three(log))
+            gm[h] = extend(g, split_three(inner))
+            km[h] = jnp.where(inside, k, ones)
+            vm[h] = jnp.where(inside, v, ones)
+        acc[...] = jnp.zeros_like(acc)
+
+    low_block = lax.broadcasted_iota(jnp.int32, (block, PAIR), 1) < HEAD_DIM
+    here = pl.ds(pl.multiple_of(i * block, block), block)
+    value_terms, key_terms = [], []
+    turned = k_ref[here, :].T
     for h in range(2):
-        inside = (lane < HEAD_DIM) if h == 0 else (lane >= HEAD_DIM)
-        base = HEAD_DIM * (1 - h)
-        inner = -jnp.sum(jnp.where(inside, product, 0.0), axis=1, keepdims=True)
-        log = -jnp.max(jnp.where(inside, logs, -jnp.inf), axis=1, keepdims=True)
-
-        def extend(x, terms):
-            tail = jnp.zeros_like(x)
-            for n, term in enumerate(terms):
-                tail = jnp.where(lane == base + n, term, tail)
-            return jnp.where(inside, x, tail)
-
-        ones = jnp.where((lane >= base) & (lane < base + 3), 1.0, 0.0).astype(BF)
-        qm[h] = extend(q, split_three(log))
-        gm[h] = extend(g, split_three(inner))
-        km[h] = jnp.where(inside, k, ones)
-        vm[h] = jnp.where(inside, v, ones)
-    acc[...] = jnp.zeros_like(acc)
-    low_block = lax.broadcasted_iota(jnp.int32, (block, PAIR), 1) < HEAD_DIM
-
-    def body(i, _):
-        here = pl.ds(pl.multiple_of(i * block, block), block)
-        value_terms, key_terms = [], []
-        turned = k_ref[here, :].T
-        for h in range(2):
-            prob = jnp.exp2(EXP2_SCALE * dot_t(km[h, here, :], qm[h]))
-            score = (prob * dot_t(vm[h, here, :], gm[h])).astype(BF)
-            value_terms.append(dot(prob.astype(BF), g_ref[...]))
-            key_terms.append(dot(score, q_ref[...]))
-            acc[h] += dot(turned, score)
-        gv_ref[here, :] = jnp.where(low_block, value_terms[0], value_terms[1]).astype(BF)
-        gk_ref[here, :] = (
-            SCORE_SCALE * jnp.where(low_block, key_terms[0], key_terms[1])
-        ).astype(BF)
-        return 0
-
-    lax.fori_loop(0, rows // block, body, 0)
-    gq_ref[...] = (SCORE_SCALE * jnp.where(lane < HEAD_DIM, acc[0].T, acc[1].T)).astype(BF)
-
-
-def attend_back_call(queries, keys, values, grad, attended, logs, block):
+        prob = jnp.exp2(EXP2_SCALE * dot_t(km[h, here, :], qm[h]))
+        score = (prob * dot_t(vm[h, here, :], gm[h])).astype(BF)
+        value_terms.append(dot(prob.astype(BF), g_ref[...]))
+        key_terms.append(dot(score, q_ref[...]))
+        acc[h] += dot(turned, score)
+    gv_ref[...] = jnp.where(low_block, value_terms[0], value_terms[1]).astype(BF)
+    gk_ref[...] = (SCORE_SCALE * jnp.where(low_block, key_terms[0], key_terms[1])).astype(BF)
+
+    @pl.when(i == blocks - 1)
+    def _():
+        gq_ref[...] = (SCORE_SCALE * jnp.where(lane < HEAD_DIM, acc[0].T, acc[1].T)).astype(BF)
+
+
+def REDUCE_WEIGHTS(count):
+    known = [1, 5, 3, 2, 2, 2, 2, 3, 2]
+    return known if count == len(known) + 1 else None
+
+
+def attend_back_call(queries, keys, values, grad, attended, logs, source, dp, block):
     rows, width = queries.shape
-    tile = pl.BlockSpec((rows, PAIR), lambda i: (0, i))
+    tile = pl.BlockSpec((rows, PAIR), lambda i, j: (0, i))
+    part_tile = pl.BlockSpec((block, PAIR), lambda i, j: (j, i))
+    anys = pl.BlockSpec(memory_space=pl.ANY)
+    parts = reduce_parts(source.shape[1], dp)
     return pl.pallas_call(
-        functools.partial(attend_back_kernel, block),
-        grid=(width // PAIR,),
-        in_specs=[tile] * 6,
-        out_specs=[tile] * 3,
-        out_shape=[jax.ShapeDtypeStruct((rows, width), BF)] * 3,
-        scratch_shapes=[pltpu.VMEM((2, rows, PAIR), BF)] * 4 + [pltpu.VMEM((2, PAIR, rows), F32)],
-        compiler_params=params(),
-    )(queries, keys, values, grad, attended, logs)
+        functools.partial(attend_back_kernel, dp, parts),
+        grid=(width // PAIR, rows // block),
+        in_specs=[tile] * 6 + [anys],
+        out_specs=[tile, part_tile, part_tile, anys],
+        out_shape=[jax.ShapeDtypeStruct((rows, width), BF)] * 3
+        + [jax.ShapeDtypeStruct(source.shape[1:], BF)],
+        scratch_shapes=[pltpu.VMEM((2, rows, PAIR), BF)] * 4
+        + [pltpu.VMEM((2, PAIR, rows), F32)]
+        + reduce_scratch(parts, width),
+        compiler_params=pltpu.CompilerParams(
+            vmem_limit_bytes=VMEM_BYTES, collective_id=1, has_side_effects=True
+        ),
+    )(queries, keys, values, grad, attended, logs, source)
 
 
 def qkv_back_kernel(
@@ -495,6 +765,7 @@
     second_gain, second_shift, up_weight, down_weight, lead_table,
 ):
     seq = lax.axis_index("seq")
+    dp = lax.axis_size("dp")
     swap = [(0, 1), (1, 0)]
 
     def trade(x):
@@ -535,10 +806,10 @@
     attended, logs = attend_call(queries, keys, values, rows // 2)
     halves = tuple(w for pair in zip(late, late_other) for w in pair)
     result, hidden_grad, attended_grad, sg2, ss2, grads = feed_call(
-        frame, attended, target, emb, gain2, shift2, frame_weight, halves, 9 * half, rows // 6
+        frame, attended, target, emb, gain2, shift2, frame_weight, halves, padded_rows(9 * half, dp), rows // 6
     )
-    gq, gk, gv = attend_back_call(
-        queries, keys, values, attended_grad, attended, logs, rows // 2
+    gq, gk, gv, late_sum = attend_back_call(
+        queries, keys, values, attended_grad, attended, logs, grads, dp, rows // 4
     )
     input_grad, sg1, ss1, st, grads_early = qkv_back_call(
         frame, hidden_grad, gq, gk, gv, emb, gain1, shift1, early, early_other, rows // 4
@@ -554,13 +825,13 @@
         summed = pick(x, seq).astype(F32) + trade(pick(x, 1 - seq)).astype(F32)
         return lax.psum(summed.astype(BF), "dp")
 
-    late_sum = reduce(grads).astype(F32)
+    late_sum = late_sum.astype(F32)
     early_sum = reduce(grads_early).astype(F32)
     rows_ff = 4 * half
     down_grad = late_sum[:rows_ff]
     up_grad = late_sum[rows_ff : 2 * rows_ff].reshape(4, half, width)
     up_grad = jnp.moveaxis(up_grad, 0, 1).reshape(half, 4 * width)
-    output_grad = late_sum[2 * rows_ff :]
+    output_grad = late_sum[2 * rows_ff : 2 * rows_ff + half]
 
     hot = (jnp.arange(lead_table.shape[0]) == lead).astype(F32)
     small = jnp.concatenate([sg1, ss1, sg2, ss2, hot[:, None] * st]).reshape(-1, 2, half)

time: 838 us -> 802 us (0.957)
  waiting for transfers between devices: 396 us -> 345 us
  Pallas kernels: 315 us -> 336 us
    psum x1, waiting for transfers between devices: 147 us -> 91.5 us  [reduce(): return lax.psum(summed.astype(BF), 'dp')]
    pallas_call x1, Pallas kernels: 108 us -> 141 us  [attend_back_call(): pl.pallas_call(functools.partial(attend_back_kernel, dp, parts), grid=(wi...]
    pallas_call x1, Pallas kernels: 116 us -> 105 us  [feed_call(): pl.pallas_call(functools.partial(feed_kernel, block, steps, 'seq'), grid=...]
    ppermute x14 -> x13, waiting for transfers between devices: 181 us -> 181 us  [trade(): return lax.ppermute(x, 'seq', swap)]
  transfers between devices with their start and end apart: 16 -> 15, of which waited for: 6 -> 6; matrix products, arithmetic and copies ran while one was open for 5% -> 6% of each run, Pallas kernels for 24% -> 8%
where the time goes in v2:
time: 802 us; the launch traced here: 798 us
  waiting for transfers between devices  345 us (43%)
  Pallas kernels  336 us (42%)
  local copies, waits for them, and re-layouts  33.2 us (4%)
  blocking collectives  32.4 us (4%)
  other arithmetic  18.6 us (2%)
  between operations  17.2 us (2%)
  starting transfers between devices  15.4 us (2%)
    ppermute x13, waiting for transfers between devices, trade(): return lax.ppermute(x, 'seq', swap)  181 us
    pallas_call x1, Pallas kernels, attend_back_call(): pl.pallas_call(functools.partial(attend_back_kernel, dp, parts), grid=(wi...  141 us
    pallas_call x1, Pallas kernels, feed_call(): pl.pallas_call(functools.partial(feed_kernel, block, steps, 'seq'), grid=...  105 us
    psum x1, waiting for transfers between devices, reduce(): return lax.psum(summed.astype(BF), 'dp')  91.5 us
    psum x1, waiting for transfers between devices, body(): small = lax.psum(pick(small, seq) + trade(pick(small, 1 - seq)), 'dp')  72.4 us
    pallas_call x1, Pallas kernels, attend_call(): pl.pallas_call(functools.partial(attend_kernel, block), grid=(width // PA...  53.6 us
    psum x1, blocking collectives, body(): totals = lax.psum(lead_counts[0].astype(F32), 'dp')  32.4 us
    pallas_call x1, Pallas kernels, qkv_back_call(): pl.pallas_call(functools.partial(qkv_back_kernel, block, steps, 'seq'), g...  25.1 us
  transfers between devices with their start and end apart: 15, of which 6 were waited for; matrix products, arithmetic and copies ran while one was open for 6% of the time, Pallas kernels for 8%

profile of v2, /device:TPU:0, one launch (start us, length us, event | category | flops | bytes accessed | tf_op | source)
XLA Modules:
  0.0 798.2 jit_solution(5344336337640596362)
XLA Ops:
  7.2 0.0 copy-start
  7.2 0.0 all-reduce.3.cloned.1.call-start
  7.2 3.0 collective-permute-start.2
  10.2 0.1 collective-permute-start.7
  10.3 1.9 collective-permute-start.8
  12.3 3.0 dynamic-slice_bitcast_fusion.4
  15.3 0.1 collective-permute-start
  15.4 0.6 gather_fusion
  16.0 0.1 broadcast_select_fusion
  16.2 0.0 copy-start.15
  16.2 2.0 collective-permute-start.1
  18.2 3.0 dynamic-slice_bitcast_fusion.2
  21.2 132.3 %collective-permute-done.1 = bf16[5,384]{1,0:T(8,128)(2,1)S(1)} collective-permute-done((bf16[5,384]{1,0:T(8,128)(2,1)S(1)}, bf16[5,384]{1,0:T(8,128)(2,1)S(1)}, u32[]{:S(2)}, u32[]{:S(2)}) %collective-permute-start.1) | collective-permute-done | bytes 3872 | tf_op jit(solution)/shard_map/ppermute | solution.py:772
  153.5 1.7 collective-permute-start.5
  155.3 0.3 collective-permute-start.3
  155.6 0.6 dynamic_slice.44
  158.1 32.4 %psum.21 = f32[40]{0:T(128)S(1)} all-reduce(f32[40]{0:T(128)S(1)} %convert_bitcast_fusion), channel_id=1, replica_groups=mesh['dp'=16,'seq'=2] {'dp'}, use_global_device_ids=true, to_apply=%region_0.1 | all-reduce | flops 40 | bytes 320 | tf_op jit(solution)/shard_map/psum | solution.py:800
  190.5 0.6 reduce_sum.9
  191.8 0.6 dynamic_slice.45
  192.4 4.5 collective-permute-done.3.rest_4_
  196.9 1.4 collective-permute-start.4
  198.3 0.6 fusion.4
  198.9 0.6 collective-permute-start.6
  199.5 3.0 pad_maximum_fusion.frame_ref
  202.5 10.8 %collective-permute-done.4.rest_5_ = bf16[384,768]{1,0:T(8,128)(2,1)S(1)} collective-permute-done((bf16[384,768]{1,0:T(8,128)(2,1)}, bf16[384,768]{1,0:T(8,128)(2,1)S(1)}, u32[]{:S(2)}, u32[]{:S(2)}) %collective-permute-start.4) | collective-permute-done | bytes 589856 | tf_op jit(solution)/shard_map/ppermute | solution.py:772
  213.3 0.8 copy-done.4
  214.1 12.3 %shard_map.246 = (bf16[1728,768]{1,0:T(8,128)(2,1)}, bf16[1728,768]{1,0:T(8,128)(2,1)}, bf16[1728,768]{1,0:T(8,128)(2,1)}) custom-call(bf16[1728,768]{1,0:T(8,128)(2,1)} %pad_maximum_fusion.frame_ref, f32[1,768]{1,0:T(1,128)} %get-tuple-element.76.emb_ref, f32[1,768]{1,0:T(1,128)} %get-tuple-element.75.gain_ref, f32[1,768]{1,0:T(1,128)} %get-tuple-element.74.shift_ref, ...), custom_call_target="tpu_custom_call" | custom-call | tf_op jit(solution)/shard_map/pallas_call | solution.py:324
  226.4 53.6 %shard_map.247 = (bf16[1728,768]{1,0:T(8,128)(2,1)}, f32[1728,768]{1,0:T(8,128)}) custom-call(bf16[1728,768]{1,0:T(8,128)(2,1)} %get-tuple-element.33.q_ref, bf16[1728,768]{1,0:T(8,128)(2,1)} %get-tuple-element.34.k_ref, bf16[1728,768]{1,0:T(8,128)(2,1)} %get-tuple-element.35.v_ref), custom_call_target="tpu_custom_call" | custom-call | tf_op jit(solution)/shard_map/pallas_call | solution.py:392
  280.1 0.0 collective-permute-done.5
  280.1 3.1 pad_maximum_fusion.1.target_ref
  283.2 104.6 %shard_map.248 = (bf16[1728,768]{1,0:T(8,128)(2,1)}, f32[1728,768]{1,0:T(8,128)}, bf16[1728,768]{1,0:T(8,128)(2,1)}, f32[1,768]{1,0:T(1,128)}, f32[1,768]{1,0:T(1,128)}, /*index=5*/bf16[2,3584,768]{2,1,0:T(8,128)(2,1)}) custom-call(bf16[1728,768]{1,0:T(8,128)(2,1)} %pad_maximum_fusion.frame_ref, bf16[1728,768]{1,0:T(8,128)(2,1)} %get-tuple-element.36.o_ref.o_full, ...), custom_call_target="tpu_custom_call" | custom-call | tf_op jit(solution)/shard_map/pallas_call | solution.py:553
  387.8 140.8 %shard_map.249 = (bf16[1728,768]{1,0:T(8,128)(2,1)}, bf16[1728,768]{1,0:T(8,128)(2,1)}, bf16[1728,768]{1,0:T(8,128)(2,1)}, bf16[3584,768]{1,0:T(8,128)(2,1)}) custom-call(bf16[1728,768]{1,0:T(8,128)(2,1)} %get-tuple-element.33.q_ref, bf16[1728,768]{1,0:T(8,128)(2,1)} %get-tuple-element.34.k_ref, bf16[1728,768]{1,0:T(8,128)(2,1)} %get-tuple-element.35.v_ref, ...), custom_call_target="tpu_custom_call" | custom-call | tf_op jit(solution)/shard_map/pallas_call | solution.py:671
  528.6 25.1 %shard_map.250 = (bf16[1728,768]{1,0:T(8,128)(2,1)}, f32[1,768]{1,0:T(1,128)}, f32[1,768]{1,0:T(1,128)}, f32[1,768]{1,0:T(1,128)}, bf16[2,1152,768]{2,1,0:T(8,128)(2,1)}) custom-call(bf16[1728,768]{1,0:T(8,128)(2,1)} %pad_maximum_fusion.frame_ref, f32[1728,768]{1,0:T(8,128)} %get-tuple-element.38.gh_ref, bf16[1728,768]{1,0:T(8,128)(2,1)} %get-tuple-element.42.gq_ref, ...), custom_call_target="tpu_custom_call" | custom-call | tf_op jit(solution)/shard_map/pallas_call | solution.py:745
  553.7 0.0 copy-start.9
  553.7 0.0 copy-start.7
  553.7 0.0 copy-start.8
  553.7 2.8 dynamic-slice_bitcast_fusion
  556.5 1.8 collective-permute-start.12
  558.3 0.6 compare_convert_fusion
  559.0 0.1 broadcast_multiply_fusion
  559.1 0.2 concatenate.29
  559.3 0.1 reshape.57
  559.4 0.1 constant_dynamic-slice_fusion.1
  559.5 0.3 collective-permute-start.11
  559.8 3.1 slice_bitcast_fusion
  563.0 1.2 slice_bitcast_fusion.1
  564.2 1.8 collective-permute-start.9
  566.0 0.3 collective-permute-start.10
  566.2 33.5 %collective-permute-done.11 = f32[44,384]{1,0:T(8,128)S(1)} collective-permute-done((f32[44,384]{1,0:T(8,128)S(1)}, f32[44,384]{1,0:T(8,128)S(1)}, u32[]{:S(2)}, u32[]{:S(2)}) %collective-permute-start.11) | collective-permute-done | bytes 67616 | tf_op jit(solution)/shard_map/ppermute | solution.py:772
  599.7 0.6 bitcast_add_fusion
  600.3 0.0 all-reduce.3.cloned.1.call-update
  600.4 0.0 all-reduce.5.cloned.1.call-start
  600.4 3.7 fusion
  604.1 0.0 all-reduce.5.cloned.1.call-update
  604.1 5.2 fusion.2
  609.3 2.2 slice.92
  611.5 2.7 copy.32
  614.2 72.4 %all-reduce.3.cloned.1.call-done = f32[44,384]{1,0:T(8,128)} async-done(((f32[44,384]{1,0:T(8,128)}), f32[44,384]{1,0:T(8,128)}) %all-reduce.3.cloned.1.call-update) | async-done | bytes 67600 | tf_op jit(solution)/shard_map/psum | solution.py:839
  686.6 1.5 slice.97
  688.1 1.5 slice_reduce_fusion
  689.6 3.4 maximum_select_fusion
  693.0 3.4 maximum_select_fusion.1
  696.4 91.5 %all-reduce.5.cloned.1.call-done = bf16[1152,768]{1,0:T(8,128)(2,1)} async-done(((bf16[1152,768]{1,0:T(8,128)(2,1)}), bf16[1152,768]{1,0:T(8,128)(2,1)}) %all-reduce.5.cloned.1.call-update) | async-done | bytes 1769488 | tf_op jit(solution)/shard_map/psum | solution.py:826
  787.8 3.3 fusion.3
  (49 shorter events, 0.2 us)
Async XLA Ops:
  7.2 8.2 %copy-start = (bf16[40,384]{1,0:T(8,128)(2,1)S(1)}, bf16[40,384]{1,0:T(8,128)(2,1)}, u32[]{:S(2)}) copy-start(bf16[40,384]{1,0:T(8,128)(2,1)} %param.29) | copy-start | bytes 92164
  7.2 679.4 %all-reduce.3.cloned.1.call-start = ((), (), s32[]{:S(2)}) async-start(), calls=%async_computation | async-start | bytes 147456 | tf_op jit(solution)/shard_map/psum | solution.py:839
  7.2 148.0 %collective-permute-start.2 = (bf16[384,768]{1,0:T(8,128)(2,1)}, bf16[384,768]{1,0:T(8,128)(2,1)}, u32[]{:S(2)}, u32[]{:S(2)}) collective-permute-start(bf16[384,768]{1,0:T(8,128)(2,1)} %rest_0_.3), channel_id=1, source_target_pairs={{0,1},{1,0},{2,3},{3,2},{4,5},{5,4},{6,7},{7,6},{8,9},{9,8},{10,11... | collective-permute-start | bytes 1769480 | tf_op jit(solution)/shard_map/ppermute | solution.py:772
  10.2 273.0 %collective-permute-start.7 = (bf16[384,3072]{1,0:T(8,128)(2,1)}, bf16[384,3072]{1,0:T(8,128)(2,1)}, u32[]{:S(2)}, u32[]{:S(2)}) collective-permute-start(bf16[384,3072]{1,0:T(8,128)(2,1)} %wu_own.1), channel_id=1, source_target_pairs={{0,1},{1,0},{2,3},{3,2},{4,5},{5,4},{6,7},{7,6},{8,9},{9,8},{10,11... | collective-permute-start | bytes 7077896 | tf_op jit(solution)/shard_map/ppermute | solution.py:772
  10.3 272.9 %collective-permute-start.8 = (bf16[1536,768]{1,0:T(8,128)(2,1)}, bf16[1536,768]{1,0:T(8,128)(2,1)}, u32[]{:S(2)}, u32[]{:S(2)}) collective-permute-start(bf16[1536,768]{1,0:T(8,128)(2,1)} %wd_own.1), channel_id=1, source_target_pairs={{0,1},{1,0},{2,3},{3,2},{4,5},{5,4},{6,7},{7,6},{8,9},{9,8},{10,11... | collective-permute-start | bytes 7077896 | tf_op jit(solution)/shard_map/ppermute | solution.py:772
  12.3 3.1 copy-start.14
  12.3 3.8 copy-start.10
  12.3 3.8 copy-start.11
  12.3 3.8 copy-start.12
  12.3 3.8 copy-start.13
  15.3 183.6 %collective-permute-start = (bf16[864,768]{1,0:T(8,128)(2,1)}, bf16[864,768]{1,0:T(8,128)(2,1)}, u32[]{:S(2)}, u32[]{:S(2)}) collective-permute-start(bf16[864,768]{1,0:T(8,128)(2,1)} %get-tuple-element.66), channel_id=1, source_target_pairs={{0,1},{1,0},{2,3},{3,2},{4,5},{5,4},{6,7},{7,6},{8,9},{9,8},{10,11... | collective-permute-start | bytes 3981320 | tf_op jit(solution)/shard_map/ppermute | solution.py:772
  16.2 139.1 %copy-start.3 = (bf16[384,768]{1,0:T(8,128)(2,1)S(1)}, bf16[384,768]{1,0:T(8,128)(2,1)}, u32[]{:S(2)}) copy-start(bf16[384,768]{1,0:T(8,128)(2,1)} %rest_1_.3) | copy-start | bytes 1769476
  16.2 141.9 %copy-start.15 = (s32[1,40]{1,0:T(1,128)S(1)}, s32[1,40]{1,0:T(1,128)}, u32[]{:S(2)}) copy-start(s32[1,40]{1,0:T(1,128)} %param.18) | copy-start | bytes 484
  16.2 137.3 %collective-permute-start.1 = (bf16[5,384]{1,0:T(8,128)(2,1)S(1)}, bf16[5,384]{1,0:T(8,128)(2,1)S(1)}, u32[]{:S(2)}, u32[]{:S(2)}) collective-permute-start(bf16[5,384]{1,0:T(8,128)(2,1)S(1)} %concatenate.25), channel_id=1, source_target_pairs={{0,1},{1,0},{2,3},{3,2},{4,5},{5,4},{6,7},{7,6},{8,9},{9,8},{10,11... | collective-permute-start | bytes 11528 | tf_op jit(solution)/shard_map/ppermute | solution.py:772
  153.5 126.6 %collective-permute-start.5 = (bf16[864,768]{1,0:T(8,128)(2,1)}, bf16[864,768]{1,0:T(8,128)(2,1)}, u32[]{:S(2)}, u32[]{:S(2)}) collective-permute-start(bf16[864,768]{1,0:T(8,128)(2,1)} %get-tuple-element.64), channel_id=1, source_target_pairs={{0,1},{1,0},{2,3},{3,2},{4,5},{5,4},{6,7},{7,6},{8,9},{9,8},{10,11... | collective-permute-start | bytes 3981320 | tf_op jit(solution)/shard_map/ppermute | solution.py:772
  155.3 41.6 %collective-permute-start.3 = (bf16[384,768]{1,0:T(8,128)(2,1)S(1)}, bf16[384,768]{1,0:T(8,128)(2,1)}, u32[]{:S(2)}, u32[]{:S(2)}) collective-permute-start(bf16[384,768]{1,0:T(8,128)(2,1)S(1)} %copy-done.3), channel_id=1, source_target_pairs={{0,1},{1,0},{2,3},{3,2},{4,5},{5,4},{6,7},{7,6},{8,9},{9,8},{10,11... | collective-permute-start | bytes 1769480 | tf_op jit(solution)/shard_map/ppermute | solution.py:772
  196.9 16.5 %collective-permute-start.4 = (bf16[384,768]{1,0:T(8,128)(2,1)}, bf16[384,768]{1,0:T(8,128)(2,1)S(1)}, u32[]{:S(2)}, u32[]{:S(2)}) collective-permute-start(bf16[384,768]{1,0:T(8,128)(2,1)} %rest_2_.3), channel_id=1, source_target_pairs={{0,1},{1,0},{2,3},{3,2},{4,5},{5,4},{6,7},{7,6},{8,9},{9,8},{10,11... | collective-permute-start | bytes 1769480 | tf_op jit(solution)/shard_map/ppermute | solution.py:772
  198.9 84.3 %collective-permute-start.6 = (bf16[384,768]{1,0:T(8,128)(2,1)}, bf16[384,768]{1,0:T(8,128)(2,1)}, u32[]{:S(2)}, u32[]{:S(2)}) collective-permute-start(bf16[384,768]{1,0:T(8,128)(2,1)} %wo_own.1), channel_id=1, source_target_pairs={{0,1},{1,0},{2,3},{3,2},{4,5},{5,4},{6,7},{7,6},{8,9},{9,8},{10,11... | collective-permute-start | bytes 1769480 | tf_op jit(solution)/shard_map/ppermute | solution.py:772
  213.3 0.8 copy-start.4
  553.7 5.3 copy-start.9
  553.7 5.4 copy-start.5
  553.7 5.4 copy-start.6
  553.7 5.4 copy-start.7
  553.7 5.4 copy-start.8
  556.5 43.9 %collective-permute-start.12 = (bf16[1152,768]{1,0:T(8,128)(2,1)}, bf16[1152,768]{1,0:T(8,128)(2,1)}, u32[]{:S(2)}, u32[]{:S(2)}) collective-permute-start(bf16[1152,768]{1,0:T(8,128)(2,1)} %dynamic-slice_bitcast_fusion), channel_id=1, source_target_pairs={{0,1},{1,0},{2,3},{3,2},{4,5},{5,4},{6,7},{7,6},{8,9},{9,8},{10,11... | collective-permute-start | bytes 5308424 | tf_op jit(solution)/shard_map/ppermute | solution.py:772
  559.5 40.2 %collective-permute-start.11 = (f32[44,384]{1,0:T(8,128)S(1)}, f32[44,384]{1,0:T(8,128)S(1)}, u32[]{:S(2)}, u32[]{:S(2)}) collective-permute-start(f32[44,384]{1,0:T(8,128)S(1)} %bitcast.35), channel_id=1, source_target_pairs={{0,1},{1,0},{2,3},{3,2},{4,5},{5,4},{6,7},{7,6},{8,9},{9,8},{10,11... | collective-permute-start | bytes 202760 | tf_op jit(solution)/shard_map/ppermute | solution.py:772
  559.8 3.1 copy-start.2
  564.2 125.4 %collective-permute-start.9 = (bf16[864,768]{1,0:T(8,128)(2,1)}, bf16[864,768]{1,0:T(8,128)(2,1)}, u32[]{:S(2)}, u32[]{:S(2)}) collective-permute-start(bf16[864,768]{1,0:T(8,128)(2,1)} %get-tuple-element.62), channel_id=1, source_target_pairs={{0,1},{1,0},{2,3},{3,2},{4,5},{5,4},{6,7},{7,6},{8,9},{9,8},{10,11... | collective-permute-start | bytes 3981320 | tf_op jit(solution)/shard_map/ppermute | solution.py:772
  566.0 127.0 %collective-permute-start.10 = (bf16[864,768]{1,0:T(8,128)(2,1)}, bf16[864,768]{1,0:T(8,128)(2,1)}, u32[]{:S(2)}, u32[]{:S(2)}) collective-permute-start(bf16[864,768]{1,0:T(8,128)(2,1)} %get-tuple-element.60), channel_id=1, source_target_pairs={{0,1},{1,0},{2,3},{3,2},{4,5},{5,4},{6,7},{7,6},{8,9},{9,8},{10,11... | collective-permute-start | bytes 3981320 | tf_op jit(solution)/shard_map/ppermute | solution.py:772
  600.4 187.5 %all-reduce.5.cloned.1.call-start = ((), (), s32[]{:S(2)}) async-start(), calls=%async_computation.1 | async-start | bytes 3538944 | tf_op jit(solution)/shard_map/psum | solution.py:826
  693.0 98.1 %copy-start.1 = (bf16[40,384]{1,0:T(8,128)(2,1)S(1)}, bf16[40,384]{1,0:T(8,128)(2,1)}, u32[]{:S(2)}) copy-start(bf16[40,384]{1,0:T(8,128)(2,1)} %param.29) | copy-start | bytes 92164
Sparse Core Ops, SparseCore 0:
  600.5 86.0 all-reduce.2
  690.5 97.2 all-reduce.4

commit v3 on v2

--- a/solution.py
+++ b/solution.py
@@ -97,14 +97,43 @@
             return (self.dp, 1 - self.seq)
         return (self.dp + (1 << key) * (1 - 2 * self.bit(key)), self.seq)
 
-    def meet(self):
+    def meet(self, keys=None):
         barrier = pltpu.get_barrier_semaphore()
-        keys = ["seq"] + list(range(self.bits))
+        keys = keys or ["seq"] + list(range(self.bits))
         for key in keys:
             pl.semaphore_signal(
                 barrier, inc=1, device_id=self.partner(key), device_id_type=pl.DeviceIdType.MESH
             )
         pl.semaphore_wait(barrier, len(keys))
+
+
+def send(place, key, src, dst, sems):
+    return pltpu.make_async_remote_copy(
+        src_ref=src,
+        dst_ref=dst,
+        send_sem=sems.at[0],
+        recv_sem=sems.at[1],
+        device_id=place.partner(key),
+        device_id_type=pl.DeviceIdType.MESH,
+    )
+
+
+def fetch_other(place, own, full, base, sems):
+    quarter = own.shape[0] // 4
+    mine, theirs = base
+    b0, b1 = place.bit(0), place.bit(1)
+    at = (b0 * 2 + b1) * quarter
+
+    def rows(start, n):
+        return pl.ds(pl.multiple_of(start, 16), n)
+
+    there = full.at[rows(theirs + at, quarter), :]
+    pair = full.at[rows(theirs + b0 * 2 * quarter, 2 * quarter), :]
+    return (
+        send(place, "seq", own.at[rows(at, quarter), :], full.at[rows(mine + at, quarter), :], sems.at[0]),
+        send(place, 1, there, there, sems.at[1]),
+        send(place, 0, pair, pair, sems.at[2]),
+    )
 
 
 def reduce_scratch(parts, width):
@@ -288,119 +317,303 @@
     return out
 
 
-def qkv_kernel(
-    seq_axis, frame_ref, emb_ref, gain_ref, shift_ref, *rest
+def start_kernel(
+    dp, frames, pack_ref, wq, wk, wv,
+    q_ref, k_ref, v_ref, frame_out, weight_out, table_ref,
+    weights, frame, pack_in, weight_sems, frame_sems, pack_sems, local_sems,
 ):
-    own, other = rest[0:3], rest[3:6]
-    outs = rest[6:9]
-    weights, sems = rest[9:11]
-    seq = lax.axis_index(seq_axis)
-    half = own[0].shape[0]
-
-    @pl.when(pl.program_id(0) == 0)
-    def _():
-        copies = []
-        for n in range(3):
-            for m, (src, place) in enumerate(((own[n], seq), (other[n], 1 - seq))):
-                rows = pl.ds(pl.multiple_of(place * half, 128), half)
-                copies.append(pltpu.make_async_copy(src, weights.at[n, rows, :], sems.at[n, m]))
-        for copy in copies:
+    i = pl.program_id(0)
+    steps = pl.num_programs(0)
+    place = Place(dp)
+    seq = place.seq
+    rows = frame.shape[0] // 2
+    half = wq.shape[0]
+    block = q_ref.shape[0]
+    pieces = rows // block
+    own = (wq, wk, wv)
+    chains = [
+        fetch_other(place, own[n], weights.at[n], (seq * half, (1 - seq) * half), weight_sems.at[n])
+        for n in range(3)
+    ]
+    pack_copy = send(place, "seq", pack_ref, pack_in, pack_sems)
+    frame_copies = [
+        send(
+            place, "seq",
+            frames.at[1 - seq, pl.ds(c * block, block), :],
+            frame.at[pl.ds(rows + c * block, block), :],
+            frame_sems.at[c],
+        )
+        for c in range(pieces)
+    ]
+    keep = [
+        pltpu.make_async_copy(
+            own[n], weights.at[n, pl.ds(pl.multiple_of(seq * half, 128), half), :], local_sems.at[n]
+        )
+        for n in range(3)
+    ] + [pltpu.make_async_copy(frames.at[seq], frame.at[pl.ds(0, rows), :], local_sems.at[3])]
+    weights_back = pltpu.make_async_copy(weights, weight_out, local_sems.at[4])
+    frame_back = pltpu.make_async_copy(frame, frame_out, local_sems.at[5])
+
+    @pl.when(i == 0)
+    def _():
+        place.meet(["seq", 0, 1])
+        pack_copy.start()
+        for chain in chains:
+            chain[0].start()
+        for copy in frame_copies:
             copy.start()
-        for copy in copies:
+        for copy in keep:
+            copy.start()
+        for step in range(2):
+            for chain in chains:
+                chain[step].wait_recv()
+                chain[step + 1].start()
+        pack_copy.wait()
+        here = pl.ds(pl.multiple_of(seq * half, 128), half)
+        there = pl.ds(pl.multiple_of((1 - seq) * half, 128), half)
+        table_ref[:, here] = pack_ref[...]
+        table_ref[:, there] = pack_in[...]
+        table_ref[4:5, there] = pack_in[5:6, :]
+        for copy in keep:
             copy.wait()
-
-    hidden = frame_ref[...].astype(F32) + emb_ref[...]
-    normed, _ = norm_rows(hidden)
-    first_in = (normed * gain_ref[...] + shift_ref[...]).astype(BF)
-    for n in range(3):
-        outs[n][...] = dot(first_in, weights[n]).astype(BF)
-
-
-def qkv_call(frame, emb, gain, shift, own, other, block):
-    rows, width = frame.shape
+        for chain in chains:
+            chain[2].wait_recv()
+            for step in range(3):
+                chain[step].wait_send()
+        weights_back.start()
+
+    for c in range(pieces):
+
+        @pl.when(i == pieces + c)
+        def _():
+            frame_copies[c].wait()
+
+    @pl.when(i == steps - 1)
+    def _():
+        frame_back.start()
+
+    hidden = frame[pl.ds(pl.multiple_of(i * block, block), block), :].astype(F32)
+    normed, _ = norm_rows(hidden + table_ref[4:5, :])
+    first_in = (normed * table_ref[0:1, :] + table_ref[1:2, :]).astype(BF)
+    for n, ref in enumerate((q_ref, k_ref, v_ref)):
+        ref[...] = dot(first_in, weights[n]).astype(BF)
+
+    @pl.when(i == steps - 1)
+    def _():
+        weights_back.wait()
+        frame_back.wait()
+
+
+def start_call(frames, pack, own, dp, block):
+    rows, width = 2 * frames.shape[1], frames.shape[2]
+    pieces = frames.shape[1] // block
     tile = pl.BlockSpec((block, width), lambda i: (i, 0))
-    vec = pl.BlockSpec((1, width), lambda i: (0, 0))
     anys = pl.BlockSpec(memory_space=pl.ANY)
     return pl.pallas_call(
-        functools.partial(qkv_kernel, "seq"),
+        functools.partial(start_kernel, dp),
         grid=(rows // block,),
-        in_specs=[tile, vec, vec, vec] + [anys] * 6,
-        out_specs=[tile] * 3,
-        out_shape=[jax.ShapeDtypeStruct((rows, width), BF)] * 3,
+        in_specs=[anys, pl.BlockSpec(memory_space=pltpu.VMEM)] + [anys] * 3,
+        out_specs=[tile] * 3 + [anys, anys, pl.BlockSpec((8, width), lambda i: (0, 0))],
+        out_shape=[jax.ShapeDtypeStruct((rows, width), BF)] * 4
+        + [
+            jax.ShapeDtypeStruct((3, width, width), BF),
+            jax.ShapeDtypeStruct((8, width), F32),
+        ],
         scratch_shapes=[
             pltpu.VMEM((3, width, width), BF),
-            pltpu.SemaphoreType.DMA((3, 2)),
+            pltpu.VMEM((rows, width), BF),
+            pltpu.VMEM((8, width // 2), F32),
+            pltpu.SemaphoreType.DMA((3, 3, 2)),
+            pltpu.SemaphoreType.DMA((pieces, 2)),
+            pltpu.SemaphoreType.DMA((2,)),
+            pltpu.SemaphoreType.DMA((6,)),
         ],
-        compiler_params=params(),
-    )(frame, emb, gain, shift, *own, *other)
-
-
-def attend_kernel(block, q_ref, k_ref, v_ref, o_ref, l_ref, keys, values):
-    rows = q_ref.shape[0]
-    low = lax.broadcasted_iota(jnp.int32, (rows, PAIR), 1) < HEAD_DIM
-    k = k_ref[...]
-    v = v_ref[...]
-    keys[0] = jnp.where(low, k, 0).astype(BF)
-    keys[1] = jnp.where(low, 0, k).astype(BF)
-    values[0] = jnp.where(low, v, 1).astype(BF)
-    values[1] = jnp.where(low, 1, v).astype(BF)
-
-    def longest(x):
-        square = x.astype(F32) * x.astype(F32)
-        first = jnp.max(jnp.sum(jnp.where(low, square, 0.0), axis=1, keepdims=True))
-        second = jnp.max(jnp.sum(jnp.where(low, 0.0, square), axis=1, keepdims=True))
-        return jnp.maximum(first, second)
-
-    bound = longest(q_ref[...]) * longest(k)
-    fast = bound <= (SAFE_LOG2 / EXP2_SCALE) ** 2
-    low_block = lax.broadcasted_iota(jnp.int32, (block, PAIR), 1) < HEAD_DIM
-
-    def run(shifted):
-        def body(i, _):
-            here = pl.ds(pl.multiple_of(i * block, block), block)
-            query = q_ref[here, :]
-            mixed, logs = [], []
-            for h in range(2):
-                scores = dot_t(query, keys[h])
-                if shifted:
-                    peak = jnp.max(scores, axis=1, keepdims=True)
-                    scores = scores - peak
-                weight = jnp.exp2(scores * EXP2_SCALE).astype(BF)
-                total = dot(weight, values[h])
-                turned = pltpu.roll(total, HEAD_DIM, 1)
-                mixed.append(total / turned)
-                log = jnp.log2(turned) * (1.0 / EXP2_SCALE)
-                logs.append(log + peak if shifted else log)
-            o_ref[here, :] = jnp.where(low_block, mixed[0], mixed[1]).astype(BF)
-            l_ref[here, :] = jnp.where(low_block, logs[0], logs[1])
+        compiler_params=pltpu.CompilerParams(
+            vmem_limit_bytes=VMEM_BYTES, collective_id=2, has_side_effects=True
+        ),
+    )(frames, pack, *own)
+
+
+def masked_pair(k, v):
+    low = lax.broadcasted_iota(jnp.int32, k.shape, 1) < HEAD_DIM
+    return (
+        (jnp.where(low, k, 0).astype(BF), jnp.where(low, 0, k).astype(BF)),
+        (jnp.where(low, v, 1).astype(BF), jnp.where(low, 1, v).astype(BF)),
+    )
+
+
+def attend_rows(query, keys, values, shifted):
+    mixed, logs = [], []
+    for h in range(2):
+        scores = dot_t(query, keys[h])
+        if shifted:
+            peak = jnp.max(scores, axis=1, keepdims=True)
+            scores = scores - peak
+        weight = jnp.exp2(scores * EXP2_SCALE).astype(BF)
+        total = dot(weight, values[h])
+        turned = pltpu.roll(total, HEAD_DIM, 1)
+        mixed.append(total / turned)
+        log = jnp.log2(turned) * (1.0 / EXP2_SCALE)
+        logs.append(log + peak if shifted else log)
+    low = lax.broadcasted_iota(jnp.int32, mixed[0].shape, 1) < HEAD_DIM
+    return jnp.where(low, mixed[0], mixed[1]).astype(BF), jnp.where(low, logs[0], logs[1])
+
+
+def longest(x):
+    square = x.astype(F32) * x.astype(F32)
+    low = lax.broadcasted_iota(jnp.int32, x.shape, 1) < HEAD_DIM
+    first = jnp.sum(jnp.where(low, square, 0.0), axis=1, keepdims=True)
+    second = jnp.sum(jnp.where(low, 0.0, square), axis=1, keepdims=True)
+    return jnp.max(jnp.maximum(first, second), axis=0, keepdims=True)
+
+
+def attend_kernel(
+    dp, q_ref, k_ref, v_ref, targets, wu_own, wd_own, wo_own,
+    o_ref, l_ref, bound_ref, target, wu_other, wd_other, wo_other,
+    keys, values, chain_sems, target_sems, local_sem,
+):
+    pair, i = pl.program_id(0), pl.program_id(1)
+    pairs, blocks = pl.num_programs(0), pl.num_programs(1)
+    slot = pair * blocks + i
+    rows, block = k_ref.shape[0], q_ref.shape[0]
+    slots = 6 * (rows // block)
+    place = Place(dp)
+    wu, wd, wo = (
+        fetch_other(place, own, other, (0, 0), chain_sems.at[n])
+        for n, (own, other) in enumerate(((wu_own, wu_other), (wd_own, wd_other), (wo_own, wo_other)))
+    )
+    near = targets.shape[1]
+    trade = send(
+        place, "seq", targets.at[1 - place.seq], target.at[pl.ds(near, near), :], target_sems
+    )
+    keep = pltpu.make_async_copy(targets.at[place.seq], target.at[pl.ds(0, near), :], local_sem)
+
+    def begin():
+        place.meet(["seq", 0, 1])
+        wu[0].start()
+        wd[0].start()
+        keep.start()
+
+    def step_on(chain, step):
+        chain[step].wait_recv()
+        chain[step + 1].start()
+
+    def third():
+        step_on(wu, 0)
+        wo[0].start()
+        trade.start()
+
+    def last_step():
+        step_on(wd, 1)
+        step_on(wo, 1)
+
+    def end():
+        for chain in (wu, wd, wo):
+            chain[2].wait_recv()
+            for copy in chain:
+                copy.wait_send()
+        trade.wait()
+        keep.wait()
+
+    events = [
+        (0, begin),
+        (3, third),
+        (5, lambda: step_on(wd, 0)),
+        (6, lambda: step_on(wu, 1)),
+        (7, lambda: step_on(wo, 0)),
+        (9, last_step),
+    ]
+    for at, event in events:
+        pl.when(slot == (at * slots) // 12)(event)
+
+    @pl.when(i == 0)
+    def _():
+        ks, vs = masked_pair(k_ref[...], v_ref[...])
+        for h in range(2):
+            keys[h] = ks[h]
+            values[h] = vs[h]
+
+    @pl.when(slot == 0)
+    def _():
+        bound_ref[...] = jnp.zeros_like(bound_ref)
+
+    query = q_ref[...]
+    bound = longest(query) * longest(k_ref[...])
+    bound_ref[...] = jnp.maximum(bound_ref[...], bound)
+    o_ref[...], l_ref[...] = attend_rows(query, keys, values, False)
+
+    pl.when(slot == slots - 1)(end)
+
+
+def attend_call(queries, keys, values, targets, late, dp, block):
+    rows, width = queries.shape
+    tile = pl.BlockSpec((block, PAIR), lambda i, j: (j, i))
+    whole = pl.BlockSpec((rows, PAIR), lambda i, j: (0, i))
+    anys = pl.BlockSpec(memory_space=pl.ANY)
+    wo, wu, wd = late
+    return pl.pallas_call(
+        functools.partial(attend_kernel, dp),
+        grid=(width // PAIR, rows // block),
+        in_specs=[tile, whole, whole] + [anys] * 4,
+        out_specs=[tile] * 2 + [pl.BlockSpec((1, PAIR), lambda i, j: (0, 0))] + [anys] * 4,
+        out_shape=[
+            jax.ShapeDtypeStruct((rows, width), BF),
+            jax.ShapeDtypeStruct((rows, width), F32),
+            jax.ShapeDtypeStruct((1, PAIR), F32),
+            jax.ShapeDtypeStruct((rows, width), BF),
+        ]
+        + [jax.ShapeDtypeStruct(w.shape, BF) for w in (wu, wd, wo)],
+        scratch_shapes=[pltpu.VMEM((2, rows, PAIR), BF)] * 2
+        + [
+            pltpu.SemaphoreType.DMA((3, 3, 2)),
+            pltpu.SemaphoreType.DMA((2,)),
+            pltpu.SemaphoreType.DMA,
+        ],
+        compiler_params=pltpu.CompilerParams(
+            vmem_limit_bytes=VMEM_BYTES, collective_id=3, has_side_effects=True
+        ),
+    )(queries, keys, values, targets, wu, wd, wo)
+
+
+def shifted_kernel(block, bound_ref, q_ref, k_ref, v_ref, o_in, l_in, o_ref, l_ref, q, k, v, o, log):
+    @pl.when(jnp.logical_not(bound_ref[0, 0] <= (SAFE_LOG2 / EXP2_SCALE) ** 2))
+    def _():
+        rows, width = q_ref.shape
+
+        def one_pair(n, _):
+            columns = pl.ds(pl.multiple_of(n * PAIR, PAIR), PAIR)
+            for src, dst in ((q_ref, q), (k_ref, k), (v_ref, v)):
+                pltpu.sync_copy(src.at[:, columns], dst)
+            keys, values = masked_pair(k[...], v[...])
+
+            def some(i, _):
+                here = pl.ds(pl.multiple_of(i * block, block), block)
+                o[here, :], log[here, :] = attend_rows(q[here, :], keys, values, True)
+                return 0
+
+            lax.fori_loop(0, rows // block, some, 0)
+            pltpu.sync_copy(o, o_ref.at[:, columns])
+            pltpu.sync_copy(log, l_ref.at[:, columns])
             return 0
 
-        lax.fori_loop(0, rows // block, body, 0)
-
-    @pl.when(fast)
-    def _():
-        run(False)
-
-    @pl.when(jnp.logical_not(fast))
-    def _():
-        run(True)
-
-
-def attend_call(queries, keys, values, block):
+        lax.fori_loop(0, width // PAIR, one_pair, 0)
+
+
+def shifted_call(bound, queries, keys, values, attended, logs, block):
     rows, width = queries.shape
-    tile = pl.BlockSpec((rows, PAIR), lambda i: (0, i))
+    anys = pl.BlockSpec(memory_space=pl.ANY)
     return pl.pallas_call(
-        functools.partial(attend_kernel, block),
-        grid=(width // PAIR,),
-        in_specs=[tile] * 3,
-        out_specs=[tile] * 2,
+        functools.partial(shifted_kernel, block),
+        in_specs=[pl.BlockSpec(memory_space=pltpu.SMEM)] + [anys] * 5,
+        out_specs=[anys] * 2,
         out_shape=[
             jax.ShapeDtypeStruct((rows, width), BF),
             jax.ShapeDtypeStruct((rows, width), F32),
         ],
-        scratch_shapes=[pltpu.VMEM((2, rows, PAIR), BF)] * 2,
+        input_output_aliases={4: 0, 5: 1},
+        scratch_shapes=[pltpu.VMEM((rows, PAIR), BF)] * 4 + [pltpu.VMEM((rows, PAIR), F32)],
         compiler_params=params(),
-    )(queries, keys, values)
+    )(bound, queries, keys, values, attended, logs)
 
 
 def feed_kernel(
@@ -593,8 +806,9 @@
 
 
 def attend_back_kernel(
-    dp, parts, q_ref, k_ref, v_ref, g_ref, o_ref, l_ref, source, gq_ref, gk_ref, gv_ref, out,
-    qm, km, vm, gm, acc, *refs
+    dp, parts, q_ref, k_ref, v_ref, g_ref, o_ref, l_ref, source, result,
+    gq_ref, gk_ref, gv_ref, out, result_out,
+    qm, km, vm, gm, acc, trade_sems, *refs
 ):
     rows = q_ref.shape[0]
     pair, i = pl.program_id(0), pl.program_id(1)
@@ -604,9 +818,28 @@
     slots = 6 * (rows // block)
     place = Place(dp)
 
+    near = result_out.shape[1]
+    seq = place.seq
+    trade = send(
+        place, "seq", result.at[pl.ds(near, near), :], result_out.at[seq], trade_sems
+    )
+    keep = pltpu.make_async_copy(
+        result.at[pl.ds(0, near), :], result_out.at[seq], trade_sems.at[2]
+    )
+
     @pl.when(slot == 0)
     def _():
         place.meet()
+        keep.start()
+
+    @pl.when(slot == slots // 2)
+    def _():
+        trade.start()
+
+    @pl.when(slot == slots - 1)
+    def _():
+        trade.wait()
+        keep.wait()
 
     for reducer in reducers(place, parts, source, out, refs):
         events = reducer.events()
@@ -662,7 +895,7 @@
     return known if count == len(known) + 1 else None
 
 
-def attend_back_call(queries, keys, values, grad, attended, logs, source, dp, block):
+def attend_back_call(queries, keys, values, grad, attended, logs, source, result, dp, block):
     rows, width = queries.shape
     tile = pl.BlockSpec((rows, PAIR), lambda i, j: (0, i))
     part_tile = pl.BlockSpec((block, PAIR), lambda i, j: (j, i))
@@ -671,92 +904,215 @@
     return pl.pallas_call(
         functools.partial(attend_back_kernel, dp, parts),
         grid=(width // PAIR, rows // block),
-        in_specs=[tile] * 6 + [anys],
-        out_specs=[tile, part_tile, part_tile, anys],
+        in_specs=[tile] * 6 + [anys] * 2,
+        out_specs=[tile, part_tile, part_tile, anys, anys],
         out_shape=[jax.ShapeDtypeStruct((rows, width), BF)] * 3
-        + [jax.ShapeDtypeStruct(source.shape[1:], BF)],
+        + [
+            jax.ShapeDtypeStruct(source.shape[1:], BF),
+            jax.ShapeDtypeStruct((2, rows // 2, width), BF),
+        ],
         scratch_shapes=[pltpu.VMEM((2, rows, PAIR), BF)] * 4
-        + [pltpu.VMEM((2, PAIR, rows), F32)]
+        + [pltpu.VMEM((2, PAIR, rows), F32), pltpu.SemaphoreType.DMA((3,))]
         + reduce_scratch(parts, width),
         compiler_params=pltpu.CompilerParams(
             vmem_limit_bytes=VMEM_BYTES, collective_id=1, has_side_effects=True
         ),
-    )(queries, keys, values, grad, attended, logs, source)
-
-
-def qkv_back_kernel(
-    block, steps, seq_axis,
-    frame_ref, gh_ref, gq_ref, gk_ref, gv_ref, emb_ref, gain_ref, shift_ref, *rest
+    )(queries, keys, values, grad, attended, logs, source, result)
+
+
+def last_kernel(
+    dp, parts, block, count,
+    frame_ref, gh_ref, gq_ref, gk_ref, gv_ref, table_ref, sg2_ref, ss2_ref, leads_ref, weight_ref,
+    out, gi_out, small_ref, lead_ref,
+    weights, first_in, source, gi, sums, trade, gathered, weight_sem, gi_sems, keep_sems, small_sems,
+    *refs,
 ):
-    own, other = rest[0:3], rest[3:6]
-    gi_ref, sg_ref, ss_ref, st_ref, grads = rest[6:11]
-    weights, first_in, sems = rest[11:14]
-    parts = (gq_ref, gk_ref, gv_ref)
+    parts_in = (gq_ref, gk_ref, gv_ref)
     i = pl.program_id(0)
-    seq = lax.axis_index(seq_axis)
-    half = own[0].shape[0]
+    place = Place(dp)
+    seq = place.seq
+    rows, width = gq_ref.shape
+    half = width // 2
+    near = rows // 2
+    steps = rows // block
+    pieces = near // block
+    emb, gain, shift = table_ref[4:5, :], table_ref[0:1, :], table_ref[1:2, :]
+    fetch = pltpu.make_async_copy(weight_ref, weights, weight_sem)
+    made = [r.events() for r in reducers(place, parts, source, out, refs)]
+
+    def normed_rows(at):
+        hidden = frame_ref[pl.ds(at, block), :].astype(F32) + emb
+        return norm_rows(hidden)
 
     @pl.when(i == 0)
     def _():
-        copies = []
-        for n in range(3):
-            for m, (src, place) in enumerate(((own[n], seq), (other[n], 1 - seq))):
-                rows = pl.ds(pl.multiple_of(place * half, 128), half)
-                copies.append(pltpu.make_async_copy(src, weights.at[n, rows, :], sems.at[n, m]))
-        for copy in copies:
-            copy.start()
-        for copy in copies:
-            copy.wait()
-        for ref in (sg_ref, ss_ref, st_ref):
-            ref[...] = jnp.zeros_like(ref)
-
-    @pl.when(i < steps)
-    def _():
-        rows = pl.ds(pl.multiple_of(i * block, block), block)
-        hidden = frame_ref[...].astype(F32) + emb_ref[...]
-        normed, inv_std = norm_rows(hidden)
-        first_in[rows, :] = (normed * gain_ref[...] + shift_ref[...]).astype(BF)
-        grad = dot_t(gq_ref[rows, :], weights[0])
-        grad += dot_t(gk_ref[rows, :], weights[1])
-        grad += dot_t(gv_ref[rows, :], weights[2])
-        ss_ref[...] += jnp.sum(grad, axis=0, keepdims=True)
-        sg_ref[...] += jnp.sum(grad * normed, axis=0, keepdims=True)
-        grad = gh_ref[...] + norm_rows_back(grad, normed, inv_std, gain_ref[...])
-        st_ref[...] += jnp.sum(grad, axis=0, keepdims=True)
-        gi_ref[...] = grad.astype(BF)
+        place.meet()
+        fetch.start()
+        sums[...] = jnp.zeros_like(sums)
+        if source.shape[1] > 3 * width:
+            source[...] = jnp.zeros_like(source)
+
+        def some(n, _):
+            at = pl.multiple_of(n * block, block)
+            normed, _ = normed_rows(at)
+            first_in[pl.ds(at, block), :] = (normed * gain + shift).astype(BF)
+            return 0
+
+        lax.fori_loop(0, steps, some, 0)
 
     for n in range(3):
 
-        @pl.when(i == steps + n)
+        @pl.when(i == 1 + n)
         def _():
-            term = dot_l(first_in[...], parts[n][...]).astype(BF)
-            grads[0, pl.ds(n * half, half), :] = term[:half]
-            grads[1, pl.ds(n * half, half), :] = term[half:]
-
-
-def qkv_back_call(frame, hidden_grad, gq, gk, gv, emb, gain, shift, own, other, block):
+            term = dot_l(first_in[...], parts_in[n][...]).astype(BF)
+            base = parts[n][0]
+            for h in range(2):
+                for m in range(2):
+                    source[h, pl.ds(base + m * half, half), :] = term[
+                        h * half : (h + 1) * half, m * half : (m + 1) * half
+                    ]
+            made[n][0]()
+
+    def gi_copies(n):
+        if n < pieces:
+            src = gi.at[pl.ds(n * block, block), :]
+            return send(place, "seq", src, gi_out.at[seq, pl.ds(n * block, block), :], gi_sems.at[n])
+        n -= pieces
+        return pltpu.make_async_copy(
+            gi.at[pl.ds(near + n * block, block), :],
+            gi_out.at[seq, pl.ds(n * block, block), :],
+            keep_sems.at[n],
+        )
+
+    first = 4
+    for n in range(steps):
+
+        @pl.when(i == first + n)
+        def _():
+            if n == 0:
+                fetch.wait()
+            at = n * block + (near if n < pieces else -near)
+            here = pl.ds(at, block)
+            grad = dot_t(gq_ref[here, :], weights[0])
+            grad += dot_t(gk_ref[here, :], weights[1])
+            grad += dot_t(gv_ref[here, :], weights[2])
+            normed, inv_std = normed_rows(at)
+            sums[1:2, :] += jnp.sum(grad, axis=0, keepdims=True)
+            sums[0:1, :] += jnp.sum(grad * normed, axis=0, keepdims=True)
+            grad = gh_ref[...] + norm_rows_back(grad, normed, inv_std, gain)
+            sums[4:5, :] += jnp.sum(grad, axis=0, keepdims=True)
+            gi[pl.ds(n * block, block), :] = grad.astype(BF)
+            gi_copies(n).start()
+            if 0 < n:
+                for events in made:
+                    events[n]()
+
+    def small_copy(step):
+        if step == 0:
+            return send(place, "seq", trade.at[0], trade.at[1], small_sems.at[0])
+        b = step - 1
+        start = (place.dp // (1 << b)) * (1 << b)
+        group = gathered.at[pl.ds(start, 1 << b)]
+        return send(place, b, group, group, small_sems.at[step])
+
+    @pl.when(i == first + steps)
+    def _():
+        sums[2:3, :] = sg2_ref[...]
+        sums[3:4, :] = ss2_ref[...]
+        here = pl.ds(pl.multiple_of(seq * half, 128), half)
+        there = pl.ds(pl.multiple_of((1 - seq) * half, 128), half)
+        trade[0] = sums[:, there]
+        small_copy(0).start()
+        left = [events[steps:] for events in made]
+        todo = [events[n] for n in range(len(left[0])) for events in left]
+        share = -(-len(todo) // (place.bits + 2))
+        for event in todo[:share]:
+            event()
+        small_copy(0).wait()
+        mine, theirs = sums[:, here], trade[1]
+        line = lax.broadcasted_iota(jnp.int32, (8, half), 0)
+        turned = jnp.broadcast_to(theirs[4:5, :], (8, half))
+        value = jnp.where(line < 4, mine + theirs, jnp.where(line == 4, mine, turned))
+        value = jnp.where(line == 6, leads_ref[0:1, :], value)
+        value = jnp.where(line == 7, leads_ref[1:2, :], value)
+        gathered[place.dp] = value
+        for step in range(1, place.bits + 1):
+            small_copy(step).start()
+            for event in todo[step * share : (step + 1) * share]:
+                event()
+            small_copy(step).wait()
+        for event in todo[(place.bits + 1) * share :]:
+            event()
+        index = lax.broadcasted_iota(jnp.int32, lead_ref.shape, 0).astype(F32)
+        small_ref[...] = jnp.zeros_like(small_ref)
+        lead_ref[...] = jnp.zeros_like(lead_ref)
+
+        def add_device(d, _):
+            value = gathered[d]
+            small_ref[...] += value
+            lead_ref[...] += jnp.where(index == value[6:7, :], value[4:5, :], 0.0) + jnp.where(
+                index == value[7:8, :], value[5:6, :], 0.0
+            )
+            return 0
+
+        lax.fori_loop(0, dp, add_device, 0)
+        for n in range(steps):
+            gi_copies(n).wait()
+
+
+def last_call(
+    frame, hidden_grad, gq, gk, gv, table, sg2, ss2, leads, weights, dp, lead_count, block
+):
     rows, width = frame.shape
+    half = width // 2
     steps = rows // block
-    tile = pl.BlockSpec((block, width), lambda i: (jnp.minimum(i, steps - 1), 0))
+    pieces = steps // 2
+    size = padded_rows(width, dp)
+    bits = dp.bit_length() - 1
+    middle = list(range(1, bits))
+    orders = [["seq"] + middle, middle + ["seq"], middle[1:] + ["seq"] + middle[:1]]
+    parts = [(n * size, size, [0] + order) for n, order in enumerate(orders)]
     whole = pl.BlockSpec((rows, width), lambda i: (0, 0))
-    vec = pl.BlockSpec((1, width), lambda i: (0, 0))
+
+    def turn(i):
+        n = jnp.clip(i - 4, 0, steps - 1)
+        return (jnp.where(n < pieces, n + pieces, n - pieces), 0)
+
+    def fixed(*shape):
+        return pl.BlockSpec(shape, lambda i: (0,) * len(shape))
+
+    vec = fixed(1, width)
     anys = pl.BlockSpec(memory_space=pl.ANY)
-    grad_shape = (2, 3 * (width // 2), width)
     return pl.pallas_call(
-        functools.partial(qkv_back_kernel, block, steps, "seq"),
-        grid=(steps + 3,),
-        in_specs=[tile, tile, whole, whole, whole, vec, vec, vec] + [anys] * 6,
-        out_specs=[tile, vec, vec, vec, pl.BlockSpec(grad_shape, lambda i: (0, 0, 0))],
-        out_shape=[jax.ShapeDtypeStruct((rows, width), BF)]
-        + [jax.ShapeDtypeStruct((1, width), F32)] * 3
-        + [jax.ShapeDtypeStruct(grad_shape, BF)],
+        functools.partial(last_kernel, dp, parts, block, lead_count),
+        grid=(5 + steps,),
+        in_specs=[whole, pl.BlockSpec((block, width), turn), whole, whole, whole]
+        + [fixed(8, width), vec, vec, fixed(2, half), anys],
+        out_specs=[anys, anys, fixed(8, half), fixed(lead_count, half)],
+        out_shape=[
+            jax.ShapeDtypeStruct((3 * size, half), BF),
+            jax.ShapeDtypeStruct((2, rows // 2, width), BF),
+            jax.ShapeDtypeStruct((8, half), F32),
+            jax.ShapeDtypeStruct((lead_count, half), F32),
+        ],
         scratch_shapes=[
             pltpu.VMEM((3, width, width), BF),
             pltpu.VMEM((rows, width), BF),
-            pltpu.SemaphoreType.DMA((3, 2)),
-        ],
-        compiler_params=params(),
-    )(frame, hidden_grad, gq, gk, gv, emb, gain, shift, *own, *other)
+            pltpu.VMEM((2, 3 * size, half), BF),
+            pltpu.VMEM((rows, width), BF),
+            pltpu.VMEM((8, width), F32),
+            pltpu.VMEM((2, 8, half), F32),
+            pltpu.VMEM((dp, 8, half), F32),
+            pltpu.SemaphoreType.DMA,
+            pltpu.SemaphoreType.DMA((pieces, 2)),
+            pltpu.SemaphoreType.DMA((pieces,)),
+            pltpu.SemaphoreType.DMA((bits + 1, 2)),
+        ]
+        + reduce_scratch(parts, half),
+        compiler_params=pltpu.CompilerParams(
+            vmem_limit_bytes=VMEM_BYTES, collective_id=4, has_side_effects=True
+        ),
+    )(frame, hidden_grad, gq, gk, gv, table, sg2, ss2, leads, weights)
 
 
 def body(
@@ -766,81 +1122,62 @@
 ):
     seq = lax.axis_index("seq")
     dp = lax.axis_size("dp")
-    swap = [(0, 1), (1, 0)]
-
-    def trade(x):
-        return lax.ppermute(x, "seq", swap)
 
     def pick(x, which):
         return lax.dynamic_index_in_dim(x, which, 0, keepdims=False)
 
-    def order(mine, theirs, axis):
-        return jnp.where(
-            seq == 0,
-            jnp.concatenate([mine, theirs], axis),
-            jnp.concatenate([theirs, mine], axis),
-        )
-
     rows, width = frames.shape[1] * 2, frames.shape[2]
     half = width // 2
-    rows_here = jnp.take(lead_table, lead_index, axis=0)
-    vectors = jnp.stack([first_gain, first_shift, second_gain, second_shift])
-    theirs = trade(jnp.concatenate([vectors, pick(rows_here, 1 - seq)[None]]))
-    mine = jnp.concatenate([vectors, pick(rows_here, seq)[None]])
-    table = order(mine, theirs, 1).astype(F32)
-    gain1, shift1, gain2, shift2, emb = (table[n : n + 1] for n in range(5))
-
-    early = (query_weight, key_weight, value_weight)
-    late = (output_weight, up_weight, down_weight)
-    early_other = tuple(trade(w) for w in early)
-    frame = jnp.concatenate([pick(frames, seq), trade(pick(frames, 1 - seq))])
-    late_other = tuple(trade(w) for w in late)
-    target = jnp.concatenate([pick(targets, seq), trade(pick(targets, 1 - seq))])
+    lead_rows = jnp.take(lead_table, lead_index, axis=0)
+    pack = jnp.stack(
+        [
+            first_gain, first_shift, second_gain, second_shift,
+            pick(lead_rows, seq), pick(lead_rows, 1 - seq), first_gain, first_gain,
+        ]
+    ).astype(F32)
 
     totals = lax.psum(lead_counts[0].astype(F32), "dp")
     lead_weight = jnp.mean(totals) / totals
     lead = pick(lead_index, seq)
     frame_weight = pick(lead_weight, lead).reshape(1, 1)
-
-    queries, keys, values = qkv_call(frame, emb, gain1, shift1, early, early_other, rows // 4)
-    attended, logs = attend_call(queries, keys, values, rows // 2)
-    halves = tuple(w for pair in zip(late, late_other) for w in pair)
+    leads = jnp.stack([lead, pick(lead_index, 1 - seq)]).astype(F32)
+    leads = jnp.broadcast_to(leads[:, None], (2, half))
+
+    early = (query_weight, key_weight, value_weight)
+    late = (output_weight, up_weight, down_weight)
+    queries, keys, values, frame, weights, table = start_call(frames, pack, early, dp, rows // 4)
+    gain2, shift2, emb = (table[n : n + 1] for n in (2, 3, 4))
+    attended, logs, bound, target, wu_other, wd_other, wo_other = attend_call(
+        queries, keys, values, targets, late, dp, rows // 2
+    )
+    attended, logs = shifted_call(bound, queries, keys, values, attended, logs, rows // 4)
+    halves = (output_weight, wo_other, up_weight, wu_other, down_weight, wd_other)
     result, hidden_grad, attended_grad, sg2, ss2, grads = feed_call(
-        frame, attended, target, emb, gain2, shift2, frame_weight, halves, padded_rows(9 * half, dp), rows // 6
-    )
-    gq, gk, gv, late_sum = attend_back_call(
-        queries, keys, values, attended_grad, attended, logs, grads, dp, rows // 4
-    )
-    input_grad, sg1, ss1, st, grads_early = qkv_back_call(
-        frame, hidden_grad, gq, gk, gv, emb, gain1, shift1, early, early_other, rows // 4
-    )
-
-    def place(x):
-        mine, theirs = x[: rows // 2], trade(x[rows // 2 :])
-        return jnp.where(
-            seq == 0, jnp.stack([mine, theirs]), jnp.stack([theirs, mine])
-        )
-
-    def reduce(x):
-        summed = pick(x, seq).astype(F32) + trade(pick(x, 1 - seq)).astype(F32)
-        return lax.psum(summed.astype(BF), "dp")
-
+        frame, attended, target, emb, gain2, shift2, frame_weight, halves,
+        padded_rows(9 * half, dp), rows // 6,
+    )
+    gq, gk, gv, late_sum, output = attend_back_call(
+        queries, keys, values, attended_grad, attended, logs, grads, result, dp, rows // 4
+    )
+    early_sum, input_grad, small, lead_grad = last_call(
+        frame, hidden_grad, gq, gk, gv, table, sg2, ss2, leads, weights, dp,
+        lead_table.shape[0], rows // 6,
+    )
+
+    rows_ff = 4 * half
     late_sum = late_sum.astype(F32)
-    early_sum = reduce(grads_early).astype(F32)
-    rows_ff = 4 * half
     down_grad = late_sum[:rows_ff]
     up_grad = late_sum[rows_ff : 2 * rows_ff].reshape(4, half, width)
     up_grad = jnp.moveaxis(up_grad, 0, 1).reshape(half, 4 * width)
     output_grad = late_sum[2 * rows_ff : 2 * rows_ff + half]
-
-    hot = (jnp.arange(lead_table.shape[0]) == lead).astype(F32)
-    small = jnp.concatenate([sg1, ss1, sg2, ss2, hot[:, None] * st]).reshape(-1, 2, half)
-    small = small.transpose(1, 0, 2)
-    small = lax.psum(pick(small, seq) + trade(pick(small, 1 - seq)), "dp")
+    size = early_sum.shape[0] // 3
+    early_grads = [
+        jnp.concatenate([early_sum[at : at + half], early_sum[at + half : at + 2 * half]], 1).astype(F32)
+        for at in (0, size, 2 * size)
+    ]
     return (
-        place(result), place(input_grad), small[0], small[1],
-        early_sum[:half], early_sum[half : 2 * half], early_sum[2 * half :], output_grad,
-        small[2], small[3], up_grad, down_grad, small[4:],
+        output, input_grad, small[0], small[1], *early_grads, output_grad,
+        small[2], small[3], up_grad, down_grad, lead_grad,
     )
 
 

time: 802 us -> 542 us (0.68)
  waiting for transfers between devices: 345 us -> 0 us
  Pallas kernels: 336 us -> 468 us
  starting transfers between devices: 15.4 us -> 0 us
  between operations: 17.2 us -> 3.56 us
  other arithmetic: 18.6 us -> 6.66 us
  local copies, waits for them, and re-layouts: 33.2 us -> 23.8 us
    ppermute x13 -> x0, waiting for transfers between devices: 181 us -> none  [trade(): return lax.ppermute(x, 'seq', swap)]
    psum x2 -> x0, waiting for transfers between devices: 164 us -> none  [the longest x1 91.5 us: reduce(): return lax.psum(summed.astype(BF), 'dp')]
    pallas_call x3 -> x4, Pallas kernels: 91 us -> 197 us  [the longest x1 86.8 us: last_call(): pl.pallas_call(functools.partial(last_kernel, dp, parts, block, lead_coun...]
    ppermute x13 -> x0, starting transfers between devices: 15.3 us -> none  [trade(): return lax.ppermute(x, 'seq', swap)]
    pallas_call x1, Pallas kernels: 141 us -> 155 us  [attend_back_call(): pl.pallas_call(functools.partial(attend_back_kernel, dp, parts), grid=(wi...]
    pallas_call x1, Pallas kernels: 105 us -> 117 us  [feed_call(): pl.pallas_call(functools.partial(feed_kernel, block, steps, 'seq'), grid=...]
    squeeze x3 -> x0, local copies, waits for them, and re-layouts: 8.78 us -> none  [pick(): return lax.dynamic_index_in_dim(x, which, 0, keepdims=False)]
  transfers between devices with their start and end apart: 15 -> 0, of which waited for: 6 -> 0; matrix products, arithmetic and copies ran while one was open for 6% -> 0% of each run, Pallas kernels for 8% -> 0%
where the time goes in v3:
time: 542 us; the launch traced here: 534 us
  Pallas kernels  468 us (86%)
  blocking collectives  32.6 us (6%)
  local copies, waits for them, and re-layouts  23.8 us (4%)
  other arithmetic  6.66 us (1%)
    pallas_call x1, Pallas kernels, attend_back_call(): pl.pallas_call(functools.partial(attend_back_kernel, dp, parts), grid=(wi...  155 us
    pallas_call x1, Pallas kernels, feed_call(): pl.pallas_call(functools.partial(feed_kernel, block, steps, 'seq'), grid=...  117 us
    pallas_call x1, Pallas kernels, last_call(): pl.pallas_call(functools.partial(last_kernel, dp, parts, block, lead_coun...  86.8 us
    pallas_call x1, Pallas kernels, attend_call(): pl.pallas_call(functools.partial(attend_kernel, dp), grid=(width // PAIR,...  61.5 us
    pallas_call x1, Pallas kernels, start_call(): pl.pallas_call(functools.partial(start_kernel, dp), grid=(rows // block,)...  47.4 us
    psum x1, blocking collectives, body(): totals = lax.psum(lead_counts[0].astype(F32), 'dp')  32.6 us

profile of v3, /device:TPU:0, one launch (start us, length us, event | category | flops | bytes accessed | tf_op | source)
XLA Modules:
  0.0 534.2 jit_solution(13763329157812427022)
XLA Ops:
  0.6 0.0 copy-start
  0.7 0.7 compare_select_fusion
  1.3 0.1 copy-done
  1.4 0.6 gather_fusion
  2.0 0.7 compare_and_fusion
  2.6 0.1 broadcast_select_fusion
  2.7 0.7 stack.24
  3.4 0.7 stack.25
  4.1 0.7 stack.26
  4.8 0.7 stack.27
  5.5 0.6 convert_element_type.28.pack_ref
  6.1 47.4 %shard_map.246 = (bf16[1728,768]{1,0:T(8,128)(2,1)}, bf16[1728,768]{1,0:T(8,128)(2,1)}, bf16[1728,768]{1,0:T(8,128)(2,1)}, bf16[1728,768]{1,0:T(8,128)(2,1)}, bf...) custom-call(bf16[2,864,768]{2,1,0:T(8,128)(2,1)} %frames.1, f32[8,384]{1,0:T(8,128)} %convert_element_type.28.pack_ref, ...), custom_call_target="tpu_custom_call" | custom-call | tf_op jit(solution)/shard_map/pallas_call | solution.py:412
  53.5 61.5 %shard_map.247 = (bf16[1728,768]{1,0:T(8,128)(2,1)}, f32[1728,768]{1,0:T(8,128)}, f32[1,128]{1,0:T(1,128)}, bf16[1728,768]{1,0:T(8,128)(2,1)}, bf16[384,3072]{1,...) custom-call(bf16[1728,768]{1,0:T(8,128)(2,1)} %get-tuple-element.43.q_ref, ...), custom_call_target="tpu_custom_call" | custom-call | tf_op jit(solution)/shard_map/pallas_call | solution.py:554
  115.0 0.0 copy-start.6
  115.0 0.0 copy-start.7
  115.1 0.8 shard_map.248
  115.9 0.0 copy-done.6
  115.9 0.6 fusion.3
  118.4 0.0 copy-done.7
  118.4 32.6 %psum.7 = f32[40]{0:T(128)S(1)} all-reduce(f32[40]{0:T(128)S(1)} %convert_bitcast_fusion), channel_id=1, replica_groups=mesh['dp'=16,'seq'=2] {'dp'}, use_global_device_ids=true, to_apply=%region_0.1 | all-reduce | flops 40 | bytes 320 | tf_op jit(solution)/shard_map/psum | solution.py:1139
  151.0 0.6 reduce_sum.9
  152.3 0.6 dynamic_slice.21
  152.9 1.4 fusion.2
  154.3 116.5 %shard_map.249 = (bf16[1728,768]{1,0:T(8,128)(2,1)}, f32[1728,768]{1,0:T(8,128)}, bf16[1728,768]{1,0:T(8,128)(2,1)}, f32[1,768]{1,0:T(1,128)}, f32[1,768]{1,0:T(1,128)}, /*index=5*/bf16[2,3584,768]{2,1,0:T(8,128)(2,1)}) custom-call(bf16[1728,768]{1,0:T(8,128)(2,1)} %get-tuple-element.46.frame_ref, bf16[1728,768]{1,0:T(8,128)(2,1)} %get-tuple-element.50.o_ref.o_full, ...), custom_call_target="tpu_custom_call" | custom-call | tf_op jit(solution)/shard_map/pallas_call | solution.py:766
  270.8 154.5 %shard_map.250 = (bf16[1728,768]{1,0:T(8,128)(2,1)}, bf16[1728,768]{1,0:T(8,128)(2,1)}, bf16[1728,768]{1,0:T(8,128)(2,1)}, bf16[3584,768]{1,0:T(8,128)(2,1)}, bf16[2,864,768]{2,1,0:T(8,128)(2,1)}) custom-call(bf16[1728,768]{1,0:T(8,128)(2,1)} %get-tuple-element.43.q_ref, bf16[1728,768]{1,0:T(8,128)(2,1)} %get-tuple-element.44.k_ref, ...), custom_call_target="tpu_custom_call" | custom-call | tf_op jit(solution)/shard_map/pallas_call | solution.py:904
  425.4 1.4 add_convert_fusion
  426.8 0.7 broadcast_in_dim.21.leads_ref
  427.4 86.8 %shard_map.251 = (bf16[2304,384]{1,0:T(8,128)(2,1)}, bf16[2,864,768]{2,1,0:T(8,128)(2,1)}, f32[8,384]{1,0:T(8,128)}, f32[40,384]{1,0:T(8,128)}) custom-call(bf16[1728,768]{1,0:T(8,128)(2,1)} %get-tuple-element.46.frame_ref, f32[1728,768]{1,0:T(8,128)} %get-tuple-element.61.gh_ref, bf16[1728,768]{1,0:T(8,128)(2,1)} %get-tuple-element.62.gq_ref, ...), custom_call_target="tpu_custom_call" | custom-call | tf_op jit(solution)/shard_map/pallas_call | solution.py:1086
  514.2 1.6 fusion.1
  515.8 1.1 maximum_convert_fusion.2
  516.9 5.2 fusion
  522.1 2.7 copy.31
  524.8 0.0 copy-start.5
  524.8 0.0 copy-start.2
  524.8 1.6 maximum_convert_fusion
  526.4 0.0 copy-done.5
  526.4 0.6 slice_reduce_fusion
  527.0 2.2 slice.66
  529.2 0.0 copy-done.2
  529.2 0.0 copy-start.3
  529.2 0.0 copy-start.1
  529.2 1.5 copy.37
  530.7 1.2 copy-done.3
  531.9 0.0 copy-start.4
  531.9 1.5 copy.38
  533.4 0.0 copy-done.4
  533.4 0.6 copy.39
  534.0 0.0 copy-done.1
  (5 shorter events, 0.1 us)
Async XLA Ops:
  0.6 0.8 copy-start
  115.0 0.8 copy-start.6
  115.0 3.4 copy-start.7
  524.8 1.6 copy-start.5
  524.8 4.3 copy-start.2
  529.2 2.7 copy-start.3
  529.2 4.8 copy-start.1
  531.9 1.5 copy-start.4

commit v4 on v3

--- a/solution.py
+++ b/solution.py
@@ -48,7 +48,9 @@
 
 def gelu_pair(u):
     z = jnp.abs(u) * 0.7071067811865476
-    t = 1.0 / (1.0 + 0.3275911 * z)
+    d = 1.0 + 0.3275911 * z
+    t = pl.reciprocal(d, approx=True)
+    t = t * (2.0 - d * t)
     e = jnp.exp2(u * u * (-0.5 * LOG2E))
     poly = t * (
         0.127414796
@@ -68,8 +70,8 @@
     unit = 16 * dp
     units = rows // unit
     middle = list(range(1, bits))
-    orders = [["seq"] + middle, middle + ["seq"], middle[1:] + ["seq"] + middle[:1]]
-    sizes = [(units + 2 - n) // 3 for n in range(3)]
+    orders = [["seq"] + middle, middle + ["seq"]] * 2
+    sizes = [(units + 3 - n) // 4 for n in range(4)]
     parts, base = [], 0
     for size, order in zip(sizes, orders):
         if size > 0:
@@ -308,19 +310,11 @@
     return made
 
 
-def spread(count, slots, weights=None):
-    weights = weights or [1.0] * (count - 1)
-    total, at, out = sum(weights), 0.0, [0]
-    for weight in weights:
-        at += weight
-        out.append(min(slots - 1, round(at / total * (slots - 1))))
-    return out
-
-
 def start_kernel(
-    dp, frames, pack_ref, wq, wk, wv,
+    dp, frames, leads_ref, counts_ref, vectors_ref, lead_table, wq, wk, wv,
     q_ref, k_ref, v_ref, frame_out, weight_out, table_ref,
-    weights, frame, pack_in, weight_sems, frame_sems, pack_sems, local_sems,
+    weights, frame, pack, pack_in, counts, counts_in,
+    weight_sems, frame_sems, pack_sems, count_sems, local_sems,
 ):
     i = pl.program_id(0)
     steps = pl.num_programs(0)
@@ -335,7 +329,17 @@
         fetch_other(place, own[n], weights.at[n], (seq * half, (1 - seq) * half), weight_sems.at[n])
         for n in range(3)
     ]
-    pack_copy = send(place, "seq", pack_ref, pack_in, pack_sems)
+    pack_copy = send(place, "seq", pack, pack_in, pack_sems)
+    count_copies = [
+        send(place, b, counts.at[b], counts_in.at[b], count_sems.at[b]) for b in range(place.bits)
+    ]
+
+    def count_on(b):
+        if b > 0:
+            count_copies[b - 1].wait()
+            counts[b] = counts[b - 1] + counts_in[b - 1]
+        if b < place.bits:
+            count_copies[b].start()
     frame_copies = [
         send(
             place, "seq",
@@ -356,7 +360,16 @@
 
     @pl.when(i == 0)
     def _():
-        place.meet(["seq", 0, 1])
+        lead, other = leads_ref[seq], leads_ref[1 - seq]
+        leads = lead_table.shape[0]
+        line = lax.broadcasted_iota(jnp.int32, (8, leads), 0)
+        index = lax.broadcasted_iota(jnp.int32, (8, leads), 1)
+        hot = jnp.where(line == 4, lead, jnp.where(line == 5, other, -1)) == index
+        pack[...] = dot(jnp.where(hot, 1.0, 0.0).astype(BF), lead_table[...])
+        pack[0:4, :] = vectors_ref[...].astype(F32)
+        counts[0] = jnp.zeros_like(counts[0])
+        counts[0, 0:1, 0:leads] = counts_ref[...].astype(F32)
+        place.meet()
         pack_copy.start()
         for chain in chains:
             chain[0].start()
@@ -364,16 +377,20 @@
             copy.start()
         for copy in keep:
             copy.start()
+        count_on(0)
         for step in range(2):
             for chain in chains:
                 chain[step].wait_recv()
                 chain[step + 1].start()
+            count_on(step + 1)
         pack_copy.wait()
         here = pl.ds(pl.multiple_of(seq * half, 128), half)
         there = pl.ds(pl.multiple_of((1 - seq) * half, 128), half)
-        table_ref[:, here] = pack_ref[...]
+        table_ref[:, here] = pack[...]
         table_ref[:, there] = pack_in[...]
         table_ref[4:5, there] = pack_in[5:6, :]
+        table_ref[6:7, :] = jnp.full((1, 2 * half), lead.astype(F32))
+        table_ref[7:8, :] = jnp.full((1, 2 * half), other.astype(F32))
         for copy in keep:
             copy.wait()
         for chain in chains:
@@ -391,6 +408,15 @@
     @pl.when(i == steps - 1)
     def _():
         frame_back.start()
+        for b in range(3, place.bits + 1):
+            count_on(b)
+        totals = counts[place.bits, 0:1, :]
+        lane = lax.broadcasted_iota(jnp.int32, totals.shape, 1)
+        leads = lead_table.shape[0]
+        mean = jnp.sum(jnp.where(lane < leads, totals, 0.0), axis=1, keepdims=True) / leads
+        share = mean / jnp.where(lane < leads, totals, 1.0)
+        weight = jnp.sum(jnp.where(lane == leads_ref[seq], share, 0.0), axis=1, keepdims=True)
+        table_ref[5:6, :] = jnp.broadcast_to(weight, (1, 2 * half))
 
     hidden = frame[pl.ds(pl.multiple_of(i * block, block), block), :].astype(F32)
     normed, _ = norm_rows(hidden + table_ref[4:5, :])
@@ -404,15 +430,18 @@
         frame_back.wait()
 
 
-def start_call(frames, pack, own, dp, block):
+def start_call(frames, lead_index, lead_counts, vectors, lead_table, own, dp, block):
     rows, width = 2 * frames.shape[1], frames.shape[2]
     pieces = frames.shape[1] // block
+    bits = dp.bit_length() - 1
     tile = pl.BlockSpec((block, width), lambda i: (i, 0))
     anys = pl.BlockSpec(memory_space=pl.ANY)
     return pl.pallas_call(
         functools.partial(start_kernel, dp),
         grid=(rows // block,),
-        in_specs=[anys, pl.BlockSpec(memory_space=pltpu.VMEM)] + [anys] * 3,
+        in_specs=[anys, pl.BlockSpec(memory_space=pltpu.SMEM)]
+        + [pl.BlockSpec(memory_space=pltpu.VMEM)] * 3
+        + [anys] * 3,
         out_specs=[tile] * 3 + [anys, anys, pl.BlockSpec((8, width), lambda i: (0, 0))],
         out_shape=[jax.ShapeDtypeStruct((rows, width), BF)] * 4
         + [
@@ -423,15 +452,19 @@
             pltpu.VMEM((3, width, width), BF),
             pltpu.VMEM((rows, width), BF),
             pltpu.VMEM((8, width // 2), F32),
+            pltpu.VMEM((8, width // 2), F32),
+            pltpu.VMEM((bits + 1, 8, PAIR), F32),
+            pltpu.VMEM((bits, 8, PAIR), F32),
             pltpu.SemaphoreType.DMA((3, 3, 2)),
             pltpu.SemaphoreType.DMA((pieces, 2)),
             pltpu.SemaphoreType.DMA((2,)),
+            pltpu.SemaphoreType.DMA((bits, 2)),
             pltpu.SemaphoreType.DMA((6,)),
         ],
         compiler_params=pltpu.CompilerParams(
             vmem_limit_bytes=VMEM_BYTES, collective_id=2, has_side_effects=True
         ),
-    )(frames, pack, *own)
+    )(frames, lead_index, lead_counts, vectors, lead_table, *own)
 
 
 def masked_pair(k, v):
@@ -683,30 +716,29 @@
         second_in[rows, :] = (normed * gain_ref[...] + shift_ref[...]).astype(BF)
         acc[...] = hidden
 
-        def forward(c, _):
-            a, s = gelu_pair(dot(second_in[rows, :], wu[c]))
+        u = dot(second_in[rows, :], wu[0])
+        for c in range(chunks):
+            later = dot(second_in[rows, :], wu[c + 1]) if c + 1 < chunks else None
+            a, s = gelu_pair(u)
             a = a.astype(BF)
             act[c, rows, :] = a
             slope[c, rows, :] = s.astype(BF)
             acc[...] += dot(a, wd[c])
-            return 0
-
-        lax.fori_loop(0, chunks, forward, 0)
+            u = later
         result = acc[...]
         y_ref[...] = result.astype(BF)
-        grad = weight_ref[0, 0] * (result - target_ref[...].astype(F32))
+        grad = weight_ref[...] * (result - target_ref[...].astype(F32))
         result_grad[rows, :] = grad.astype(BF)
         hidden_s[...] = grad
         acc[...] = jnp.zeros_like(acc)
 
-        def backward(c, _):
-            back = dot_t(result_grad[rows, :], wd[c])
+        back = dot_t(result_grad[rows, :], wd[0])
+        for c in range(chunks):
+            later = dot_t(result_grad[rows, :], wd[c + 1]) if c + 1 < chunks else None
             back = (back * slope[c, rows, :].astype(F32)).astype(BF)
             slope[c, rows, :] = back
             acc[...] += dot_t(back, wu[c])
-            return 0
-
-        lax.fori_loop(0, chunks, backward, 0)
+            back = later
         grad = acc[...]
         normed = normed_s[...]
         ss_ref[...] += jnp.sum(grad, axis=0, keepdims=True)
@@ -760,13 +792,13 @@
     chunks = halves[2].shape[1] // width
     steps = rows // block
     tile = pl.BlockSpec((block, width), lambda i: (jnp.minimum(i, steps - 1), 0))
-    whole = pl.BlockSpec((rows, width), lambda i: (0, 0))
+    whole = pl.BlockSpec((rows, width), lambda i: (0, 0), pipeline_mode=pl.Buffered(1))
     vec = pl.BlockSpec((1, width), lambda i: (0, 0))
     anys = pl.BlockSpec(memory_space=pl.ANY)
     return pl.pallas_call(
         functools.partial(feed_kernel, block, steps, "seq"),
         grid=(steps + 2 * chunks + 1,),
-        in_specs=[tile, tile, whole, tile, vec, vec, vec, pl.BlockSpec(memory_space=pltpu.SMEM)]
+        in_specs=[tile, tile, whole, tile, vec, vec, vec, vec]
         + [anys] * 6,
         out_specs=[tile, tile, tile, vec, vec, anys],
         out_shape=[
@@ -841,9 +873,9 @@
         trade.wait()
         keep.wait()
 
-    for reducer in reducers(place, parts, source, out, refs):
+    for n, reducer in enumerate(reducers(place, parts, source, out, refs)):
         events = reducer.events()
-        for at, event in zip(spread(len(events), slots, REDUCE_WEIGHTS(len(events))), events):
+        for at, event in zip(reduce_slots(len(events), slots, n), events):
             pl.when(slot == at)(event)
 
     lane = lax.broadcasted_iota(jnp.int32, (rows, PAIR), 1)
@@ -890,9 +922,19 @@
         gq_ref[...] = (SCORE_SCALE * jnp.where(lane < HEAD_DIM, acc[0].T, acc[1].T)).astype(BF)
 
 
-def REDUCE_WEIGHTS(count):
-    known = [1, 5, 3, 2, 2, 2, 2, 3, 2]
-    return known if count == len(known) + 1 else None
+REDUCE_SLOTS = (
+    (0, 1, 5, 8, 10, 12, 14, 16, 19, 21),
+    (0, 1, 5, 8, 10, 12, 14, 16, 19, 21),
+    (3, 5, 9, 11, 13, 15, 17, 19, 21, 23),
+    (3, 5, 9, 11, 13, 15, 17, 19, 21, 23),
+)
+
+
+def reduce_slots(count, slots, part):
+    known = REDUCE_SLOTS[part]
+    if len(known) == count:
+        return [at * (slots - 1) // known[-1] if slots != 24 else at for at in known]
+    return [n * (slots - 1) // (count - 1) for n in range(count)]
 
 
 def attend_back_call(queries, keys, values, grad, attended, logs, source, result, dp, block):
@@ -922,7 +964,7 @@
 
 def last_kernel(
     dp, parts, block, count,
-    frame_ref, gh_ref, gq_ref, gk_ref, gv_ref, table_ref, sg2_ref, ss2_ref, leads_ref, weight_ref,
+    frame_ref, gh_ref, gq_ref, gk_ref, gv_ref, table_ref, sg2_ref, ss2_ref, weight_ref,
     out, gi_out, small_ref, lead_ref,
     weights, first_in, source, gi, sums, trade, gathered, weight_sem, gi_sems, keep_sems, small_sems,
     *refs,
@@ -1033,8 +1075,8 @@
         line = lax.broadcasted_iota(jnp.int32, (8, half), 0)
         turned = jnp.broadcast_to(theirs[4:5, :], (8, half))
         value = jnp.where(line < 4, mine + theirs, jnp.where(line == 4, mine, turned))
-        value = jnp.where(line == 6, leads_ref[0:1, :], value)
-        value = jnp.where(line == 7, leads_ref[1:2, :], value)
+        value = jnp.where(line == 6, table_ref[6:7, 0:half], value)
+        value = jnp.where(line == 7, table_ref[7:8, 0:half], value)
         gathered[place.dp] = value
         for step in range(1, place.bits + 1):
             small_copy(step).start()
@@ -1061,7 +1103,7 @@
 
 
 def last_call(
-    frame, hidden_grad, gq, gk, gv, table, sg2, ss2, leads, weights, dp, lead_count, block
+    frame, hidden_grad, gq, gk, gv, table, sg2, ss2, weights, dp, lead_count, block
 ):
     rows, width = frame.shape
     half = width // 2
@@ -1087,7 +1129,7 @@
         functools.partial(last_kernel, dp, parts, block, lead_count),
         grid=(5 + steps,),
         in_specs=[whole, pl.BlockSpec((block, width), turn), whole, whole, whole]
-        + [fixed(8, width), vec, vec, fixed(2, half), anys],
+        + [fixed(8, width), vec, vec, anys],
         out_specs=[anys, anys, fixed(8, half), fixed(lead_count, half)],
         out_shape=[
             jax.ShapeDtypeStruct((3 * size, half), BF),
@@ -1112,7 +1154,7 @@
         compiler_params=pltpu.CompilerParams(
             vmem_limit_bytes=VMEM_BYTES, collective_id=4, has_side_effects=True
         ),
-    )(frame, hidden_grad, gq, gk, gv, table, sg2, ss2, leads, weights)
+    )(frame, hidden_grad, gq, gk, gv, table, sg2, ss2, weights)
 
 
 def body(
@@ -1120,33 +1162,17 @@
     first_gain, first_shift, query_weight, key_weight, value_weight, output_weight,
     second_gain, second_shift, up_weight, down_weight, lead_table,
 ):
-    seq = lax.axis_index("seq")
     dp = lax.axis_size("dp")
-
-    def pick(x, which):
-        return lax.dynamic_index_in_dim(x, which, 0, keepdims=False)
-
     rows, width = frames.shape[1] * 2, frames.shape[2]
     half = width // 2
-    lead_rows = jnp.take(lead_table, lead_index, axis=0)
-    pack = jnp.stack(
-        [
-            first_gain, first_shift, second_gain, second_shift,
-            pick(lead_rows, seq), pick(lead_rows, 1 - seq), first_gain, first_gain,
-        ]
-    ).astype(F32)
-
-    totals = lax.psum(lead_counts[0].astype(F32), "dp")
-    lead_weight = jnp.mean(totals) / totals
-    lead = pick(lead_index, seq)
-    frame_weight = pick(lead_weight, lead).reshape(1, 1)
-    leads = jnp.stack([lead, pick(lead_index, 1 - seq)]).astype(F32)
-    leads = jnp.broadcast_to(leads[:, None], (2, half))
+    vectors = jnp.concatenate([first_gain, first_shift, second_gain, second_shift]).reshape(4, half)
 
     early = (query_weight, key_weight, value_weight)
     late = (output_weight, up_weight, down_weight)
-    queries, keys, values, frame, weights, table = start_call(frames, pack, early, dp, rows // 4)
-    gain2, shift2, emb = (table[n : n + 1] for n in (2, 3, 4))
+    queries, keys, values, frame, weights, table = start_call(
+        frames, lead_index, lead_counts, vectors, lead_table, early, dp, rows // 4
+    )
+    gain2, shift2, emb, frame_weight = (table[n : n + 1] for n in (2, 3, 4, 5))
     attended, logs, bound, target, wu_other, wd_other, wo_other = attend_call(
         queries, keys, values, targets, late, dp, rows // 2
     )
@@ -1160,7 +1186,7 @@
         queries, keys, values, attended_grad, attended, logs, grads, result, dp, rows // 4
     )
     early_sum, input_grad, small, lead_grad = last_call(
-        frame, hidden_grad, gq, gk, gv, table, sg2, ss2, leads, weights, dp,
+        frame, hidden_grad, gq, gk, gv, table, sg2, ss2, weights, dp,
         lead_table.shape[0], rows // 6,
     )
 

time: 542 us -> 469 us (0.87); the launches traced: 534 us -> 470 us
  blocking collectives: 32.6 us -> 0 us
  Pallas kernels: 468 us -> 449 us
  local copies, waits for them, and re-layouts: 23.8 us -> 16.4 us
    psum x1 -> x0, blocking collectives: 32.6 us -> none  [body(): totals = lax.psum(lead_counts[0].astype(F32), 'dp')]
    pallas_call x1, Pallas kernels: 117 us -> 104 us  [feed_call(): pl.pallas_call(functools.partial(feed_kernel, block, steps, 'seq'), grid=...]
    pallas_call x1, Pallas kernels: 155 us -> 148 us  [attend_back_call(): pl.pallas_call(functools.partial(attend_back_kernel, dp, parts), grid=(wi...]
where the time goes in v4:
time: 469 us; the launch traced here: 470 us
  Pallas kernels  449 us (96%)
  local copies, waits for them, and re-layouts  16.4 us (3%)
    pallas_call x1, Pallas kernels, attend_back_call(): pl.pallas_call(functools.partial(attend_back_kernel, dp, parts), grid=(wi...  148 us
    pallas_call x1, Pallas kernels, feed_call(): pl.pallas_call(functools.partial(feed_kernel, block, steps, 'seq'), grid=...  104 us
    pallas_call x1, Pallas kernels, last_call(): pl.pallas_call(functools.partial(last_kernel, dp, parts, block, lead_coun...  82.5 us
    pallas_call x1, Pallas kernels, attend_call(): pl.pallas_call(functools.partial(attend_kernel, dp), grid=(width // PAIR,...  61.5 us
    pallas_call x1, Pallas kernels, start_call(): pl.pallas_call(functools.partial(start_kernel, dp), grid=(rows // block,)...  52.1 us

profile of v4, /device:TPU:0, one launch (start us, length us, event | category | flops | bytes accessed | tf_op | source)
XLA Modules:
  0.0 469.7 jit_solution(7520547050495169659)
XLA Ops:
  0.6 0.7 pad_maximum_fusion
  1.4 0.6 reshape.35.vectors_ref
  2.0 52.1 %shard_map.246 = (bf16[1728,768]{1,0:T(8,128)(2,1)}, bf16[1728,768]{1,0:T(8,128)(2,1)}, bf16[1728,768]{1,0:T(8,128)(2,1)}, bf16[1728,768]{1,0:T(8,128)(2,1)}, bf...) custom-call(bf16[2,864,768]{2,1,0:T(8,128)(2,1)} %frames.1, s32[2]{0:T(128)} %leads_ref.1, s32[1,40]{1,0:T(1,128)} %counts_ref.1, ...), custom_call_target="tpu_custom_call" | custom-call | tf_op jit(solution)/shard_map/pallas_call | solution.py:439
  54.1 1.5 fusion.2
  55.6 61.5 %shard_map.247 = (bf16[1728,768]{1,0:T(8,128)(2,1)}, f32[1728,768]{1,0:T(8,128)}, f32[1,128]{1,0:T(1,128)}, bf16[1728,768]{1,0:T(8,128)(2,1)}, bf16[384,3072]{1,...) custom-call(bf16[1728,768]{1,0:T(8,128)(2,1)} %get-tuple-element.43.q_ref, ...), custom_call_target="tpu_custom_call" | custom-call | tf_op jit(solution)/shard_map/pallas_call | solution.py:587
  117.1 0.7 shard_map.248
  117.7 103.8 %shard_map.249 = (bf16[1728,768]{1,0:T(8,128)(2,1)}, f32[1728,768]{1,0:T(8,128)}, bf16[1728,768]{1,0:T(8,128)(2,1)}, f32[1,768]{1,0:T(1,128)}, f32[1,768]{1,0:T(1,128)}, /*index=5*/bf16[2,3584,768]{2,1,0:T(8,128)(2,1)}) custom-call(bf16[1728,768]{1,0:T(8,128)(2,1)} %get-tuple-element.46.frame_ref, bf16[1728,768]{1,0:T(8,128)(2,1)} %get-tuple-element.50.o_ref.o_full, ...), custom_call_target="tpu_custom_call" | custom-call | tf_op jit(solution)/shard_map/pallas_call | solution.py:798
  221.6 148.3 %shard_map.250 = (bf16[1728,768]{1,0:T(8,128)(2,1)}, bf16[1728,768]{1,0:T(8,128)(2,1)}, bf16[1728,768]{1,0:T(8,128)(2,1)}, bf16[3584,768]{1,0:T(8,128)(2,1)}, bf16[2,864,768]{2,1,0:T(8,128)(2,1)}) custom-call(bf16[1728,768]{1,0:T(8,128)(2,1)} %get-tuple-element.43.q_ref, bf16[1728,768]{1,0:T(8,128)(2,1)} %get-tuple-element.44.k_ref, ...), custom_call_target="tpu_custom_call" | custom-call | tf_op jit(solution)/shard_map/pallas_call | solution.py:946
  369.9 82.5 %shard_map.251 = (bf16[2304,384]{1,0:T(8,128)(2,1)}, bf16[2,864,768]{2,1,0:T(8,128)(2,1)}, f32[8,384]{1,0:T(8,128)}, f32[40,384]{1,0:T(8,128)}) custom-call(bf16[1728,768]{1,0:T(8,128)(2,1)} %get-tuple-element.46.frame_ref, f32[1728,768]{1,0:T(8,128)} %get-tuple-element.61.gh_ref, bf16[1728,768]{1,0:T(8,128)(2,1)} %get-tuple-element.62.gq_ref, ...), custom_call_target="tpu_custom_call" | custom-call | tf_op jit(solution)/shard_map/pallas_call | solution.py:1128
  452.4 0.0 copy-start.2
  452.4 1.5 slice_reduce_fusion
  453.9 0.0 slice-start
  453.9 2.3 slice.68
  456.2 0.0 copy-done.2
  456.2 0.0 slice-start.1
  456.2 0.2 fusion.1
  456.4 1.1 maximum_convert_fusion.2
  457.5 1.6 maximum_convert_fusion
  459.1 0.0 slice-done
  459.1 0.0 slice-done.1
  459.1 2.8 fusion
  461.9 0.0 copy-start
  461.9 2.7 copy.31
  464.6 0.0 copy-done
  464.6 0.0 copy-start.1
  464.6 1.5 copy.37
  466.1 1.2 copy-done.1
  467.3 0.0 copy-start.3
  467.3 1.5 copy.38
  468.8 0.0 copy-done.3
  468.9 0.6 copy.39
  (1 shorter events, 0.0 us)
Async XLA Ops:
  452.4 3.8 copy-start.2
  453.9 5.2 %slice-start = ((s8[5505024]{0:T(1024)(128)(4,1)}), s8[4194304]{0:T(1024)(128)(4,1)S(1)}, s32[]{:S(2)}) async-start(s8[5505024]{0:T(1024)(128)(4,1)} %bitcast.5), calls=%async_computation | async-start | bytes 8388608
  456.2 2.9 slice-start.1
  461.9 2.7 copy-start
  464.6 2.7 copy-start.1
  467.3 1.5 copy-start.3

commit v5 on v4

--- a/solution.py
+++ b/solution.py
@@ -121,21 +121,25 @@
 
 
 def fetch_other(place, own, full, base, sems):
-    quarter = own.shape[0] // 4
+    eighth = own.shape[0] // 8
     mine, theirs = base
-    b0, b1 = place.bit(0), place.bit(1)
-    at = (b0 * 2 + b1) * quarter
+    at = [0]
+    for b in range(3):
+        at.append(at[-1] + place.bit(b) * (4 * eighth // (1 << b)))
 
     def rows(start, n):
         return pl.ds(pl.multiple_of(start, 16), n)
 
-    there = full.at[rows(theirs + at, quarter), :]
-    pair = full.at[rows(theirs + b0 * 2 * quarter, 2 * quarter), :]
-    return (
-        send(place, "seq", own.at[rows(at, quarter), :], full.at[rows(mine + at, quarter), :], sems.at[0]),
-        send(place, 1, there, there, sems.at[1]),
-        send(place, 0, pair, pair, sems.at[2]),
-    )
+    copies = [
+        send(
+            place, "seq", own.at[rows(at[3], eighth), :], full.at[rows(mine + at[3], eighth), :],
+            sems.at[0],
+        )
+    ]
+    for n, b in enumerate((2, 1, 0)):
+        there = full.at[rows(theirs + at[b + 1], eighth << n), :]
+        copies.append(send(place, b, there, there, sems.at[1 + n]))
+    return copies
 
 
 def reduce_scratch(parts, width):
@@ -156,7 +160,7 @@
     def __init__(self, place, part, index, source, out, refs, sems, local_sems):
         self.place, self.index, self.source, self.out = place, index, source, out
         self.base, self.rows, self.order = part
-        self.acc, self.landing = refs[0], refs[1:]
+        self.acc, self.landing = (refs[0], refs[1:]) if refs else (None, None)
         self.sems, self.local = sems, local_sems
         self.copies = {}
         half = self.rows // 2
@@ -224,11 +228,11 @@
             off = off - self.place.bit(key) * n
             n *= 2
         off = pl.multiple_of(off, 16)
-        if j == 0:
+        here = self.out.at[pl.ds(off, n), :]
+        src = here
+        if j == 0 and self.acc is not None:
             src = self.acc.at[self.place.seq, pl.ds(self.final_off, n), :]
-        else:
-            src = self.out.at[pl.ds(off, n), :]
-        return self.remote(len(self.order) + j, src, self.out.at[pl.ds(off, n), :], keys[j])
+        return self.remote(len(self.order) + j, src, here, keys[j])
 
     def add(self, step):
         landing = self.landing[step]
@@ -254,7 +258,25 @@
 
             lax.fori_loop(0, n // size, some, 0)
 
-    def events(self):
+    def gather_events(self):
+        last = self.place.bits - 1
+
+        def onward(j):
+            def run():
+                if j > 0:
+                    self.gather(j - 1).wait_recv()
+                self.gather(j).start()
+
+            return run
+
+        def finish():
+            self.gather(last).wait_recv()
+            for j in range(last + 1):
+                self.gather(j).wait_send()
+
+        return [onward(j) for j in range(last + 1)] + [finish]
+
+    def events(self, gathered=True):
         steps = len(self.order)
         gathers = self.place.bits
 
@@ -272,9 +294,15 @@
                     self.scatter(step).start()
                 else:
                     self.final_copy().start()
-                    self.gather(0).start()
+                    if gathered:
+                        self.gather(0).start()
 
             return run
+
+        def end_scatter():
+            self.final_copy().wait()
+            for step in range(steps):
+                self.scatter(step).wait_send()
 
         def onward(j):
             def run():
@@ -292,6 +320,8 @@
             for j in range(gathers):
                 self.gather(j).wait_send()
 
+        if not gathered:
+            return [begin] + [middle(step) for step in range(1, steps + 1)] + [end_scatter]
         return (
             [begin]
             + [middle(step) for step in range(1, steps + 1)]
@@ -312,8 +342,8 @@
 
 def start_kernel(
     dp, frames, leads_ref, counts_ref, vectors_ref, lead_table, wq, wk, wv,
-    q_ref, k_ref, v_ref, frame_out, weight_out, table_ref,
-    weights, frame, pack, pack_in, counts, counts_in,
+    q_ref, k_ref, v_ref, frame_out, weight_out, table_ref, bound_ref,
+    weights, frame, longest, pack, pack_in, counts, counts_in,
     weight_sems, frame_sems, pack_sems, count_sems, local_sems,
 ):
     i = pl.program_id(0)
@@ -360,6 +390,7 @@
 
     @pl.when(i == 0)
     def _():
+        longest[...] = jnp.zeros_like(longest)
         lead, other = leads_ref[seq], leads_ref[1 - seq]
         leads = lead_table.shape[0]
         line = lax.broadcasted_iota(jnp.int32, (8, leads), 0)
@@ -373,15 +404,15 @@
         pack_copy.start()
         for chain in chains:
             chain[0].start()
-        for copy in frame_copies:
-            copy.start()
         for copy in keep:
             copy.start()
         count_on(0)
-        for step in range(2):
+        for step in range(3):
             for chain in chains:
                 chain[step].wait_recv()
                 chain[step + 1].start()
+            if step < pieces:
+                frame_copies[step].start()
             count_on(step + 1)
         pack_copy.wait()
         here = pl.ds(pl.multiple_of(seq * half, 128), half)
@@ -394,10 +425,12 @@
         for copy in keep:
             copy.wait()
         for chain in chains:
-            chain[2].wait_recv()
-            for step in range(3):
+            chain[3].wait_recv()
+            for step in range(4):
                 chain[step].wait_send()
         weights_back.start()
+        for copy in frame_copies[3:]:
+            copy.start()
 
     for c in range(pieces):
 
@@ -408,7 +441,7 @@
     @pl.when(i == steps - 1)
     def _():
         frame_back.start()
-        for b in range(3, place.bits + 1):
+        for b in range(4, place.bits + 1):
             count_on(b)
         totals = counts[place.bits, 0:1, :]
         lane = lax.broadcasted_iota(jnp.int32, totals.shape, 1)
@@ -421,11 +454,20 @@
     hidden = frame[pl.ds(pl.multiple_of(i * block, block), block), :].astype(F32)
     normed, _ = norm_rows(hidden + table_ref[4:5, :])
     first_in = (normed * table_ref[0:1, :] + table_ref[1:2, :]).astype(BF)
+    line = lax.broadcasted_iota(jnp.int32, (2 * half, PAIR), 0)
+    column = lax.broadcasted_iota(jnp.int32, (2 * half, PAIR), 1)
+    heads = jnp.where(line // HEAD_DIM == column, 1.0, 0.0).astype(BF)
     for n, ref in enumerate((q_ref, k_ref, v_ref)):
-        ref[...] = dot(first_in, weights[n]).astype(BF)
+        made = dot(first_in, weights[n]).astype(BF)
+        ref[...] = made
+        if n < 2:
+            square = (made.astype(F32) * made.astype(F32)).astype(BF)
+            most = jnp.max(dot(square, heads), axis=0, keepdims=True) * 1.02
+            longest[n : n + 1, :] = jnp.maximum(longest[n : n + 1, :], most)
 
     @pl.when(i == steps - 1)
     def _():
+        bound_ref[...] = jnp.max(longest[0:1, :] * longest[1:2, :], axis=1, keepdims=True)
         weights_back.wait()
         frame_back.wait()
 
@@ -442,20 +484,26 @@
         in_specs=[anys, pl.BlockSpec(memory_space=pltpu.SMEM)]
         + [pl.BlockSpec(memory_space=pltpu.VMEM)] * 3
         + [anys] * 3,
-        out_specs=[tile] * 3 + [anys, anys, pl.BlockSpec((8, width), lambda i: (0, 0))],
+        out_specs=[tile] * 3 + [
+            anys, anys,
+            pl.BlockSpec((8, width), lambda i: (0, 0)),
+            pl.BlockSpec((1, 1), lambda i: (0, 0)),
+        ],
         out_shape=[jax.ShapeDtypeStruct((rows, width), BF)] * 4
         + [
             jax.ShapeDtypeStruct((3, width, width), BF),
             jax.ShapeDtypeStruct((8, width), F32),
+            jax.ShapeDtypeStruct((1, 1), F32),
         ],
         scratch_shapes=[
             pltpu.VMEM((3, width, width), BF),
             pltpu.VMEM((rows, width), BF),
+            pltpu.VMEM((8, PAIR), F32),
             pltpu.VMEM((8, width // 2), F32),
             pltpu.VMEM((8, width // 2), F32),
             pltpu.VMEM((bits + 1, 8, PAIR), F32),
             pltpu.VMEM((bits, 8, PAIR), F32),
-            pltpu.SemaphoreType.DMA((3, 3, 2)),
+            pltpu.SemaphoreType.DMA((3, 4, 2)),
             pltpu.SemaphoreType.DMA((pieces, 2)),
             pltpu.SemaphoreType.DMA((2,)),
             pltpu.SemaphoreType.DMA((bits, 2)),
@@ -492,17 +540,9 @@
     return jnp.where(low, mixed[0], mixed[1]).astype(BF), jnp.where(low, logs[0], logs[1])
 
 
-def longest(x):
-    square = x.astype(F32) * x.astype(F32)
-    low = lax.broadcasted_iota(jnp.int32, x.shape, 1) < HEAD_DIM
-    first = jnp.sum(jnp.where(low, square, 0.0), axis=1, keepdims=True)
-    second = jnp.sum(jnp.where(low, 0.0, square), axis=1, keepdims=True)
-    return jnp.max(jnp.maximum(first, second), axis=0, keepdims=True)
-
-
 def attend_kernel(
     dp, q_ref, k_ref, v_ref, targets, wu_own, wd_own, wo_own,
-    o_ref, l_ref, bound_ref, target, wu_other, wd_other, wo_other,
+    o_ref, l_ref, target, wu_other, wd_other, wo_other,
     keys, values, chain_sems, target_sems, local_sem,
 ):
     pair, i = pl.program_id(0), pl.program_id(1)
@@ -522,27 +562,36 @@
     keep = pltpu.make_async_copy(targets.at[place.seq], target.at[pl.ds(0, near), :], local_sem)
 
     def begin():
-        place.meet(["seq", 0, 1])
+        place.meet(["seq", 0, 1, 2])
         wu[0].start()
-        wd[0].start()
         keep.start()
 
     def step_on(chain, step):
         chain[step].wait_recv()
         chain[step + 1].start()
 
+    def first():
+        step_on(wu, 0)
+        wd[0].start()
+        wo[0].start()
+
+    def second():
+        step_on(wu, 1)
+        step_on(wd, 0)
+        step_on(wo, 0)
+        trade.start()
+
     def third():
-        step_on(wu, 0)
-        wo[0].start()
-        trade.start()
-
-    def last_step():
         step_on(wd, 1)
         step_on(wo, 1)
 
+    def fourth():
+        step_on(wd, 2)
+        step_on(wo, 2)
+
     def end():
         for chain in (wu, wd, wo):
-            chain[2].wait_recv()
+            chain[3].wait_recv()
             for copy in chain:
                 copy.wait_send()
         trade.wait()
@@ -550,11 +599,11 @@
 
     events = [
         (0, begin),
-        (3, third),
-        (5, lambda: step_on(wd, 0)),
-        (6, lambda: step_on(wu, 1)),
-        (7, lambda: step_on(wo, 0)),
-        (9, last_step),
+        (2, first),
+        (4, second),
+        (6, third),
+        (8, lambda: step_on(wu, 2)),
+        (11, fourth),
     ]
     for at, event in events:
         pl.when(slot == (at * slots) // 12)(event)
@@ -566,14 +615,7 @@
             keys[h] = ks[h]
             values[h] = vs[h]
 
-    @pl.when(slot == 0)
-    def _():
-        bound_ref[...] = jnp.zeros_like(bound_ref)
-
-    query = q_ref[...]
-    bound = longest(query) * longest(k_ref[...])
-    bound_ref[...] = jnp.maximum(bound_ref[...], bound)
-    o_ref[...], l_ref[...] = attend_rows(query, keys, values, False)
+    o_ref[...], l_ref[...] = attend_rows(q_ref[...], keys, values, False)
 
     pl.when(slot == slots - 1)(end)
 
@@ -588,17 +630,16 @@
         functools.partial(attend_kernel, dp),
         grid=(width // PAIR, rows // block),
         in_specs=[tile, whole, whole] + [anys] * 4,
-        out_specs=[tile] * 2 + [pl.BlockSpec((1, PAIR), lambda i, j: (0, 0))] + [anys] * 4,
+        out_specs=[tile] * 2 + [anys] * 4,
         out_shape=[
             jax.ShapeDtypeStruct((rows, width), BF),
             jax.ShapeDtypeStruct((rows, width), F32),
-            jax.ShapeDtypeStruct((1, PAIR), F32),
             jax.ShapeDtypeStruct((rows, width), BF),
         ]
         + [jax.ShapeDtypeStruct(w.shape, BF) for w in (wu, wd, wo)],
         scratch_shapes=[pltpu.VMEM((2, rows, PAIR), BF)] * 2
         + [
-            pltpu.SemaphoreType.DMA((3, 3, 2)),
+            pltpu.SemaphoreType.DMA((3, 4, 2)),
             pltpu.SemaphoreType.DMA((2,)),
             pltpu.SemaphoreType.DMA,
         ],
@@ -874,7 +915,7 @@
         keep.wait()
 
     for n, reducer in enumerate(reducers(place, parts, source, out, refs)):
-        events = reducer.events()
+        events = reducer.events(n < WHOLE_PARTS)
         for at, event in zip(reduce_slots(len(events), slots, n), events):
             pl.when(slot == at)(event)
 
@@ -882,26 +923,31 @@
 
     @pl.when(i == 0)
     def _():
-        q, k, v, g = q_ref[...], k_ref[...], v_ref[...], g_ref[...]
-        product = g.astype(F32) * o_ref[...].astype(F32)
-        logs = l_ref[...]
-        for h in range(2):
-            inside = (lane < HEAD_DIM) if h == 0 else (lane >= HEAD_DIM)
-            base = HEAD_DIM * (1 - h)
-            inner = -jnp.sum(jnp.where(inside, product, 0.0), axis=1, keepdims=True)
-            log = -jnp.max(jnp.where(inside, logs, -jnp.inf), axis=1, keepdims=True)
-
-            def extend(x, terms):
-                tail = jnp.zeros_like(x)
-                for n, term in enumerate(terms):
-                    tail = jnp.where(lane == base + n, term, tail)
-                return jnp.where(inside, x, tail)
-
-            ones = jnp.where((lane >= base) & (lane < base + 3), 1.0, 0.0).astype(BF)
-            qm[h] = extend(q, split_three(log))
-            gm[h] = extend(g, split_three(inner))
-            km[h] = jnp.where(inside, k, ones)
-            vm[h] = jnp.where(inside, v, ones)
+        low = lane < HEAD_DIM
+        sub = lane % HEAD_DIM
+        product = g_ref[...].astype(F32) * o_ref[...].astype(F32)
+        first = product.astype(BF)
+        line = lax.broadcasted_iota(jnp.int32, (PAIR, PAIR), 0)
+        column = lax.broadcasted_iota(jnp.int32, (PAIR, PAIR), 1)
+        cross = jnp.where((line < HEAD_DIM) != (column < HEAD_DIM), -1.0, 0.0).astype(BF)
+        inner = dot(first, cross) + dot((product - first.astype(F32)).astype(BF), cross)
+
+        def tail(x):
+            terms = split_three(x)
+            zero = jnp.zeros_like(terms[0])
+            return jnp.where(
+                sub == 0, terms[0], jnp.where(sub == 1, terms[1], jnp.where(sub == 2, terms[2], zero))
+            )
+
+        log_tail = tail(-pltpu.roll(l_ref[...], HEAD_DIM, 1))
+        inner_tail = tail(inner)
+        ones = jnp.where(sub < 3, 1.0, 0.0).astype(BF)
+        for ref, x, extra in (
+            (qm, q_ref[...], log_tail), (gm, g_ref[...], inner_tail),
+            (km, k_ref[...], ones), (vm, v_ref[...], ones),
+        ):
+            ref[0] = jnp.where(low, x, extra)
+            ref[1] = jnp.where(low, extra, x)
         acc[...] = jnp.zeros_like(acc)
 
     low_block = lax.broadcasted_iota(jnp.int32, (block, PAIR), 1) < HEAD_DIM
@@ -922,11 +968,12 @@
         gq_ref[...] = (SCORE_SCALE * jnp.where(lane < HEAD_DIM, acc[0].T, acc[1].T)).astype(BF)
 
 
+WHOLE_PARTS = 2
 REDUCE_SLOTS = (
-    (0, 1, 5, 8, 10, 12, 14, 16, 19, 21),
-    (0, 1, 5, 8, 10, 12, 14, 16, 19, 21),
-    (3, 5, 9, 11, 13, 15, 17, 19, 21, 23),
-    (3, 5, 9, 11, 13, 15, 17, 19, 21, 23),
+    (0, 2, 6, 9, 11, 13, 15, 17, 20, 22),
+    (0, 2, 6, 9, 11, 13, 15, 17, 20, 22),
+    (3, 6, 10, 13, 16, 19, 23),
+    (3, 6, 10, 13, 16, 19, 23),
 )
 
 
@@ -963,10 +1010,10 @@
 
 
 def last_kernel(
-    dp, parts, block, count,
-    frame_ref, gh_ref, gq_ref, gk_ref, gv_ref, table_ref, sg2_ref, ss2_ref, weight_ref,
-    out, gi_out, small_ref, lead_ref,
-    weights, first_in, source, gi, sums, trade, gathered, weight_sem, gi_sems, keep_sems, small_sems,
+    dp, parts, late_parts, block,
+    frame_ref, gh_ref, gq_ref, gk_ref, gv_ref, table_ref, sg2_ref, ss2_ref, weight_ref, late_in,
+    out, gi_out, small_ref, lead_ref, late,
+    weights, first_in, source, gi, sums, trade, gathered, weight_sem, gi_sems, keep_sems, small_sems, late_sems,
     *refs,
 ):
     parts_in = (gq_ref, gk_ref, gv_ref)
@@ -981,6 +1028,15 @@
     emb, gain, shift = table_ref[4:5, :], table_ref[0:1, :], table_ref[1:2, :]
     fetch = pltpu.make_async_copy(weight_ref, weights, weight_sem)
     made = [r.events() for r in reducers(place, parts, source, out, refs)]
+    late_made = [
+        Reducer(place, part, n, None, late, (), late_sems, None).gather_events()
+        for n, part in enumerate(late_parts)
+    ]
+
+    def late_on(n):
+        for events in late_made:
+            if n < len(events) - 1:
+                events[n]()
 
     def normed_rows(at):
         hidden = frame_ref[pl.ds(at, block), :].astype(F32) + emb
@@ -990,22 +1046,25 @@
     def _():
         place.meet()
         fetch.start()
+        late_on(0)
         sums[...] = jnp.zeros_like(sums)
         if source.shape[1] > 3 * width:
             source[...] = jnp.zeros_like(source)
-
-        def some(n, _):
-            at = pl.multiple_of(n * block, block)
-            normed, _ = normed_rows(at)
-            first_in[pl.ds(at, block), :] = (normed * gain + shift).astype(BF)
-            return 0
-
-        lax.fori_loop(0, steps, some, 0)
+        fetch.wait()
 
     for n in range(3):
 
-        @pl.when(i == 1 + n)
+        @pl.when(i == pieces + n)
         def _():
+            if n == 0:
+
+                def some(m, _):
+                    at = pl.multiple_of(m * block, block)
+                    normed, _ = normed_rows(at)
+                    first_in[pl.ds(at, block), :] = (normed * gain + shift).astype(BF)
+                    return 0
+
+                lax.fori_loop(0, pieces, some, 0)
             term = dot_l(first_in[...], parts_in[n][...]).astype(BF)
             base = parts[n][0]
             for h in range(2):
@@ -1014,6 +1073,7 @@
                         h * half : (h + 1) * half, m * half : (m + 1) * half
                     ]
             made[n][0]()
+            late_on(2 + n)
 
     def gi_copies(n):
         if n < pieces:
@@ -1026,28 +1086,29 @@
             keep_sems.at[n],
         )
 
-    first = 4
     for n in range(steps):
 
-        @pl.when(i == first + n)
+        @pl.when(i == (n if n < pieces else n + 3))
         def _():
-            if n == 0:
-                fetch.wait()
             at = n * block + (near if n < pieces else -near)
             here = pl.ds(at, block)
             grad = dot_t(gq_ref[here, :], weights[0])
             grad += dot_t(gk_ref[here, :], weights[1])
             grad += dot_t(gv_ref[here, :], weights[2])
             normed, inv_std = normed_rows(at)
+            if n < pieces:
+                first_in[here, :] = (normed * gain + shift).astype(BF)
             sums[1:2, :] += jnp.sum(grad, axis=0, keepdims=True)
             sums[0:1, :] += jnp.sum(grad * normed, axis=0, keepdims=True)
             grad = gh_ref[...] + norm_rows_back(grad, normed, inv_std, gain)
             sums[4:5, :] += jnp.sum(grad, axis=0, keepdims=True)
             gi[pl.ds(n * block, block), :] = grad.astype(BF)
             gi_copies(n).start()
-            if 0 < n:
+            if n == pieces - 1:
+                late_on(1)
+            if n >= pieces:
                 for events in made:
-                    events[n]()
+                    events[n - pieces + 1]()
 
     def small_copy(step):
         if step == 0:
@@ -1057,7 +1118,7 @@
         group = gathered.at[pl.ds(start, 1 << b)]
         return send(place, b, group, group, small_sems.at[step])
 
-    @pl.when(i == first + steps)
+    @pl.when(i == 3 + steps)
     def _():
         sums[2:3, :] = sg2_ref[...]
         sums[3:4, :] = ss2_ref[...]
@@ -1065,7 +1126,7 @@
         there = pl.ds(pl.multiple_of((1 - seq) * half, 128), half)
         trade[0] = sums[:, there]
         small_copy(0).start()
-        left = [events[steps:] for events in made]
+        left = [events[pieces + 1 :] for events in made]
         todo = [events[n] for n in range(len(left[0])) for events in left]
         share = -(-len(todo) // (place.bits + 2))
         for event in todo[:share]:
@@ -1100,10 +1161,14 @@
         lax.fori_loop(0, dp, add_device, 0)
         for n in range(steps):
             gi_copies(n).wait()
+        for n in range(5, place.bits):
+            late_on(n)
+        for events in late_made:
+            events[-1]()
 
 
 def last_call(
-    frame, hidden_grad, gq, gk, gv, table, sg2, ss2, weights, dp, lead_count, block
+    frame, hidden_grad, gq, gk, gv, table, sg2, ss2, weights, late, dp, lead_count, block
 ):
     rows, width = frame.shape
     half = width // 2
@@ -1112,13 +1177,13 @@
     size = padded_rows(width, dp)
     bits = dp.bit_length() - 1
     middle = list(range(1, bits))
-    orders = [["seq"] + middle, middle + ["seq"], middle[1:] + ["seq"] + middle[:1]]
+    orders = [middle + ["seq"], middle[1:] + ["seq"] + middle[:1], ["seq"] + middle]
+    late_parts = reduce_parts(late.shape[0], dp)[WHOLE_PARTS:]
     parts = [(n * size, size, [0] + order) for n, order in enumerate(orders)]
     whole = pl.BlockSpec((rows, width), lambda i: (0, 0))
 
     def turn(i):
-        n = jnp.clip(i - 4, 0, steps - 1)
-        return (jnp.where(n < pieces, n + pieces, n - pieces), 0)
+        return (jnp.where(i < pieces, i + pieces, jnp.clip(i - 3 - pieces, 0, pieces - 1)), 0)
 
     def fixed(*shape):
         return pl.BlockSpec(shape, lambda i: (0,) * len(shape))
@@ -1126,16 +1191,18 @@
     vec = fixed(1, width)
     anys = pl.BlockSpec(memory_space=pl.ANY)
     return pl.pallas_call(
-        functools.partial(last_kernel, dp, parts, block, lead_count),
-        grid=(5 + steps,),
+        functools.partial(last_kernel, dp, parts, late_parts, block),
+        grid=(4 + steps,),
         in_specs=[whole, pl.BlockSpec((block, width), turn), whole, whole, whole]
-        + [fixed(8, width), vec, vec, anys],
-        out_specs=[anys, anys, fixed(8, half), fixed(lead_count, half)],
+        + [fixed(8, width), vec, vec, anys, anys],
+        out_specs=[anys, anys, fixed(8, half), fixed(lead_count, half), anys],
+        input_output_aliases={9: 4},
         out_shape=[
             jax.ShapeDtypeStruct((3 * size, half), BF),
             jax.ShapeDtypeStruct((2, rows // 2, width), BF),
             jax.ShapeDtypeStruct((8, half), F32),
             jax.ShapeDtypeStruct((lead_count, half), F32),
+            jax.ShapeDtypeStruct(late.shape, BF),
         ],
         scratch_shapes=[
             pltpu.VMEM((3, width, width), BF),
@@ -1149,12 +1216,13 @@
             pltpu.SemaphoreType.DMA((pieces, 2)),
             pltpu.SemaphoreType.DMA((pieces,)),
             pltpu.SemaphoreType.DMA((bits + 1, 2)),
+            pltpu.SemaphoreType.DMA((max(len(late_parts), 1), 2 * (bits + 1), 2)),
         ]
         + reduce_scratch(parts, half),
         compiler_params=pltpu.CompilerParams(
             vmem_limit_bytes=VMEM_BYTES, collective_id=4, has_side_effects=True
         ),
-    )(frame, hidden_grad, gq, gk, gv, table, sg2, ss2, weights)
+    )(frame, hidden_grad, gq, gk, gv, table, sg2, ss2, weights, late)
 
 
 def body(
@@ -1169,11 +1237,11 @@
 
     early = (query_weight, key_weight, value_weight)
     late = (output_weight, up_weight, down_weight)
-    queries, keys, values, frame, weights, table = start_call(
-        frames, lead_index, lead_counts, vectors, lead_table, early, dp, rows // 4
+    queries, keys, values, frame, weights, table, bound = start_call(
+        frames, lead_index, lead_counts, vectors, lead_table, early, dp, rows // 6
     )
     gain2, shift2, emb, frame_weight = (table[n : n + 1] for n in (2, 3, 4, 5))
-    attended, logs, bound, target, wu_other, wd_other, wo_other = attend_call(
+    attended, logs, target, wu_other, wd_other, wo_other = attend_call(
         queries, keys, values, targets, late, dp, rows // 2
     )
     attended, logs = shifted_call(bound, queries, keys, values, attended, logs, rows // 4)
@@ -1185,8 +1253,8 @@
     gq, gk, gv, late_sum, output = attend_back_call(
         queries, keys, values, attended_grad, attended, logs, grads, result, dp, rows // 4
     )
-    early_sum, input_grad, small, lead_grad = last_call(
-        frame, hidden_grad, gq, gk, gv, table, sg2, ss2, weights, dp,
+    early_sum, input_grad, small, lead_grad, late_sum = last_call(
+        frame, hidden_grad, gq, gk, gv, table, sg2, ss2, weights, late_sum, dp,
         lead_table.shape[0], rows // 6,
     )
 

time: 469 us -> 432 us (0.921)
  Pallas kernels: 449 us -> 411 us
    pallas_call x1, Pallas kernels: 148 us -> 132 us  [attend_back_call(): pl.pallas_call(functools.partial(attend_back_kernel, dp, parts), grid=(wi...]
    pallas_call x1, Pallas kernels: 52.1 us -> 44.5 us  [start_call(): pl.pallas_call(functools.partial(start_kernel, dp), grid=(rows // block,)...]
    pallas_call x1, Pallas kernels: 61.5 us -> 54 us  [attend_call(): pl.pallas_call(functools.partial(attend_kernel, dp), grid=(width // PAIR,...]
    pallas_call x1, Pallas kernels: 82.5 us -> 76.4 us  [last_call(): pl.pallas_call(functools.partial(last_kernel, dp, parts, late_parts, bloc...]
where the time goes in v5:
time: 432 us
  Pallas kernels  411 us (95%)
  local copies, waits for them, and re-layouts  16.4 us (4%)
    pallas_call x1, Pallas kernels, attend_back_call(): pl.pallas_call(functools.partial(attend_back_kernel, dp, parts), grid=(wi...  132 us
    pallas_call x1, Pallas kernels, feed_call(): pl.pallas_call(functools.partial(feed_kernel, block, steps, 'seq'), grid=...  104 us
    pallas_call x1, Pallas kernels, last_call(): pl.pallas_call(functools.partial(last_kernel, dp, parts, late_parts, bloc...  76.4 us
    pallas_call x1, Pallas kernels, attend_call(): pl.pallas_call(functools.partial(attend_kernel, dp), grid=(width // PAIR,...  54 us
    pallas_call x1, Pallas kernels, start_call(): pl.pallas_call(functools.partial(start_kernel, dp), grid=(rows // block,)...  44.5 us

profile of v5, /device:TPU:0, one launch (start us, length us, event | category | flops | bytes accessed | tf_op | source)
XLA Modules:
  0.0 432.1 jit_solution(5834528005089997650)
XLA Ops:
  0.6 0.7 pad_maximum_fusion
  1.4 0.6 reshape.35.vectors_ref
  2.0 44.5 %shard_map.246 = (bf16[1728,768]{1,0:T(8,128)(2,1)}, bf16[1728,768]{1,0:T(8,128)(2,1)}, bf16[1728,768]{1,0:T(8,128)(2,1)}, bf16[1728,768]{1,0:T(8,128)(2,1)}, bf...) custom-call(bf16[2,864,768]{2,1,0:T(8,128)(2,1)} %frames.1, s32[2]{0:T(128)} %leads_ref.1, ...), custom_call_target="tpu_custom_call" | custom-call | tf_op jit(solution)/shard_map/pallas_call | solution.py:481
  46.5 1.5 fusion.2
  47.9 54.0 %shard_map.247 = (bf16[1728,768]{1,0:T(8,128)(2,1)}, f32[1728,768]{1,0:T(8,128)}, bf16[1728,768]{1,0:T(8,128)(2,1)}, bf16[384,3072]{1,0:T(8,128)(2,1)}, bf16[153...) custom-call(bf16[1728,768]{1,0:T(8,128)(2,1)} %get-tuple-element.44.q_ref, bf16[1728,768]{1,0:T(8,128)(2,1)} %get-tuple-element.45.k_ref, ...), custom_call_target="tpu_custom_call" | custom-call | tf_op jit(solution)/shard_map/pallas_call | solution.py:629
  101.9 0.7 shard_map.248
  102.6 103.8 %shard_map.249 = (bf16[1728,768]{1,0:T(8,128)(2,1)}, f32[1728,768]{1,0:T(8,128)}, bf16[1728,768]{1,0:T(8,128)(2,1)}, f32[1,768]{1,0:T(1,128)}, f32[1,768]{1,0:T(1,128)}, /*index=5*/bf16[2,3584,768]{2,1,0:T(8,128)(2,1)}) custom-call(bf16[1728,768]{1,0:T(8,128)(2,1)} %get-tuple-element.47.frame_ref, bf16[1728,768]{1,0:T(8,128)(2,1)} %get-tuple-element.51.o_ref.o_full, ...), custom_call_target="tpu_custom_call" | custom-call | tf_op jit(solution)/shard_map/pallas_call | solution.py:839
  206.5 132.0 %shard_map.250 = (bf16[1728,768]{1,0:T(8,128)(2,1)}, bf16[1728,768]{1,0:T(8,128)(2,1)}, bf16[1728,768]{1,0:T(8,128)(2,1)}, bf16[3584,768]{1,0:T(8,128)(2,1)}, bf16[2,864,768]{2,1,0:T(8,128)(2,1)}) custom-call(bf16[1728,768]{1,0:T(8,128)(2,1)} %get-tuple-element.44.q_ref, bf16[1728,768]{1,0:T(8,128)(2,1)} %get-tuple-element.45.k_ref, ...), custom_call_target="tpu_custom_call" | custom-call | tf_op jit(solution)/shard_map/pallas_call | solution.py:993
  338.4 76.4 %shard_map.251 = (bf16[2304,384]{1,0:T(8,128)(2,1)}, bf16[2,864,768]{2,1,0:T(8,128)(2,1)}, f32[8,384]{1,0:T(8,128)}, f32[40,384]{1,0:T(8,128)}, bf16[3584,768]{1,0:T(8,128)(2,1)}) custom-call(bf16[1728,768]{1,0:T(8,128)(2,1)} %get-tuple-element.47.frame_ref, f32[1728,768]{1,0:T(8,128)} %get-tuple-element.62.gh_ref, ...), custom_call_target="tpu_custom_call", output_to_operand_aliasing={{4}: (9, {})} | custom-call | tf_op jit(solution)/shard_map/pallas_call | solution.py:1193
  414.9 0.0 copy-start.2
  414.9 1.5 slice_reduce_fusion
  416.4 0.0 slice-start
  416.4 2.3 slice.68
  418.7 0.0 copy-done.2
  418.7 0.0 slice-start.1
  418.7 0.2 fusion.1
  418.9 1.1 maximum_convert_fusion.2
  419.9 1.6 maximum_convert_fusion
  421.5 0.0 slice-done
  421.5 0.0 slice-done.1
  421.5 2.8 fusion
  424.3 0.0 copy-start
  424.3 2.7 copy.32
  427.1 0.0 copy-done
  427.1 0.0 copy-start.1
  427.1 1.5 copy.39
  428.6 1.2 copy-done.1
  429.8 0.0 copy-start.3
  429.8 1.5 copy.40
  431.3 0.0 copy-done.3
  431.3 0.6 copy.41
  (1 shorter events, 0.0 us)
Async XLA Ops:
  414.9 3.8 copy-start.2
  416.4 5.2 %slice-start = ((s8[5505024]{0:T(1024)(128)(4,1)}), s8[4194304]{0:T(1024)(128)(4,1)S(1)}, s32[]{:S(2)}) async-start(s8[5505024]{0:T(1024)(128)(4,1)} %bitcast.5), calls=%async_computation | async-start | bytes 8388608
  418.7 2.9 slice-start.1
  424.3 2.7 copy-start
  427.1 2.7 copy-start.1
  429.8 1.5 copy-start.3

commit v6 on v5

--- a/solution.py
+++ b/solution.py
@@ -692,7 +692,7 @@
 
 def feed_kernel(
     block, steps, seq_axis,
-    frame_ref, o_ref, o_full, target_ref, emb_ref, gain_ref, shift_ref, weight_ref,
+    frame_ref, o_ref, o_full, target_ref, table_ref,
     wo_own, wo_other, wu_own, wu_other, wd_own, wd_other,
     y_ref, gh_ref, go_ref, sg_ref, ss_ref, grads,
     wo, wu, wd, act, slope, second_in, result_grad, hidden_grad, normed_s, hidden_s, acc, stage,
@@ -751,10 +751,10 @@
     @pl.when(i < steps)
     def _():
         rows = pl.ds(pl.multiple_of(i * block, block), block)
-        hidden = frame_ref[...].astype(F32) + emb_ref[...] + dot(o_ref[...], wo[...])
+        hidden = frame_ref[...].astype(F32) + table_ref[4:5, :] + dot(o_ref[...], wo[...])
         normed, inv_std = norm_rows(hidden)
         normed_s[...] = normed
-        second_in[rows, :] = (normed * gain_ref[...] + shift_ref[...]).astype(BF)
+        second_in[rows, :] = (normed * table_ref[2:3, :] + table_ref[3:4, :]).astype(BF)
         acc[...] = hidden
 
         u = dot(second_in[rows, :], wu[0])
@@ -768,7 +768,7 @@
             u = later
         result = acc[...]
         y_ref[...] = result.astype(BF)
-        grad = weight_ref[...] * (result - target_ref[...].astype(F32))
+        grad = table_ref[5:6, :] * (result - target_ref[...].astype(F32))
         result_grad[rows, :] = grad.astype(BF)
         hidden_s[...] = grad
         acc[...] = jnp.zeros_like(acc)
@@ -784,7 +784,7 @@
         normed = normed_s[...]
         ss_ref[...] += jnp.sum(grad, axis=0, keepdims=True)
         sg_ref[...] += jnp.sum(grad * normed, axis=0, keepdims=True)
-        grad = hidden_s[...] + norm_rows_back(grad, normed, inv_std, gain_ref[...])
+        grad = hidden_s[...] + norm_rows_back(grad, normed, inv_std, table_ref[2:3, :])
         gh_ref[...] = grad
         grad = grad.astype(BF)
         hidden_grad[rows, :] = grad
@@ -828,7 +828,7 @@
                         copy.wait()
 
 
-def feed_call(frame, attended, target, emb, gain, shift, weight, halves, grad_rows, block):
+def feed_call(frame, attended, target, table, halves, grad_rows, block):
     rows, width = frame.shape
     chunks = halves[2].shape[1] // width
     steps = rows // block
@@ -839,7 +839,7 @@
     return pl.pallas_call(
         functools.partial(feed_kernel, block, steps, "seq"),
         grid=(steps + 2 * chunks + 1,),
-        in_specs=[tile, tile, whole, tile, vec, vec, vec, vec]
+        in_specs=[tile, tile, whole, tile, pl.BlockSpec((8, width), lambda i: (0, 0))]
         + [anys] * 6,
         out_specs=[tile, tile, tile, vec, vec, anys],
         out_shape=[
@@ -867,7 +867,7 @@
             pltpu.SemaphoreType.DMA((2, 2)),
         ],
         compiler_params=params(),
-    )(frame, attended, attended, target, emb, gain, shift, weight, *halves)
+    )(frame, attended, attended, target, table, *halves)
 
 
 def split_three(x):
@@ -1240,14 +1240,13 @@
     queries, keys, values, frame, weights, table, bound = start_call(
         frames, lead_index, lead_counts, vectors, lead_table, early, dp, rows // 6
     )
-    gain2, shift2, emb, frame_weight = (table[n : n + 1] for n in (2, 3, 4, 5))
     attended, logs, target, wu_other, wd_other, wo_other = attend_call(
         queries, keys, values, targets, late, dp, rows // 2
     )
     attended, logs = shifted_call(bound, queries, keys, values, attended, logs, rows // 4)
     halves = (output_weight, wo_other, up_weight, wu_other, down_weight, wd_other)
     result, hidden_grad, attended_grad, sg2, ss2, grads = feed_call(
-        frame, attended, target, emb, gain2, shift2, frame_weight, halves,
+        frame, attended, target, table, halves,
         padded_rows(9 * half, dp), rows // 6,
     )
     gq, gk, gv, late_sum, output = attend_back_call(

time: 432 us -> 431 us (level)
  no operation moved by 1% of the time
where the time goes in v6:
time: 431 us
  Pallas kernels  412 us (96%)
  local copies, waits for them, and re-layouts  15 us (3%)
    pallas_call x1, Pallas kernels, attend_back_call(): pl.pallas_call(functools.partial(attend_back_kernel, dp, parts), grid=(wi...  132 us
    pallas_call x1, Pallas kernels, feed_call(): pl.pallas_call(functools.partial(feed_kernel, block, steps, 'seq'), grid=...  104 us
    pallas_call x1, Pallas kernels, last_call(): pl.pallas_call(functools.partial(last_kernel, dp, parts, late_parts, bloc...  76.9 us
    pallas_call x1, Pallas kernels, attend_call(): pl.pallas_call(functools.partial(attend_kernel, dp), grid=(width // PAIR,...  54 us
    pallas_call x1, Pallas kernels, start_call(): pl.pallas_call(functools.partial(start_kernel, dp), grid=(rows // block,)...  44.5 us

profile of v6, /device:TPU:0, one launch (start us, length us, event | category | flops | bytes accessed | tf_op | source)
XLA Modules:
  0.0 431.1 jit_solution(3776686958880853655)
XLA Ops:
  0.6 0.7 pad_maximum_fusion
  1.4 0.6 reshape.35.vectors_ref
  2.0 44.5 %shard_map.246 = (bf16[1728,768]{1,0:T(8,128)(2,1)}, bf16[1728,768]{1,0:T(8,128)(2,1)}, bf16[1728,768]{1,0:T(8,128)(2,1)}, bf16[1728,768]{1,0:T(8,128)(2,1)}, bf...) custom-call(bf16[2,864,768]{2,1,0:T(8,128)(2,1)} %frames.1, s32[2]{0:T(128)} %leads_ref.1, ...), custom_call_target="tpu_custom_call" | custom-call | tf_op jit(solution)/shard_map/pallas_call | solution.py:481
  46.4 54.0 %shard_map.247 = (bf16[1728,768]{1,0:T(8,128)(2,1)}, f32[1728,768]{1,0:T(8,128)}, bf16[1728,768]{1,0:T(8,128)(2,1)}, bf16[384,3072]{1,0:T(8,128)(2,1)}, bf16[153...) custom-call(bf16[1728,768]{1,0:T(8,128)(2,1)} %get-tuple-element.44.q_ref, bf16[1728,768]{1,0:T(8,128)(2,1)} %get-tuple-element.45.k_ref, ...), custom_call_target="tpu_custom_call" | custom-call | tf_op jit(solution)/shard_map/pallas_call | solution.py:629
  100.5 0.6 shard_map.248
  101.1 103.8 %shard_map.249 = (bf16[1728,768]{1,0:T(8,128)(2,1)}, f32[1728,768]{1,0:T(8,128)}, bf16[1728,768]{1,0:T(8,128)(2,1)}, f32[1,768]{1,0:T(1,128)}, f32[1,768]{1,0:T(1,128)}, /*index=5*/bf16[2,3584,768]{2,1,0:T(8,128)(2,1)}) custom-call(bf16[1728,768]{1,0:T(8,128)(2,1)} %get-tuple-element.47.frame_ref, bf16[1728,768]{1,0:T(8,128)(2,1)} %get-tuple-element.51.o_ref.o_full, ...), custom_call_target="tpu_custom_call" | custom-call | tf_op jit(solution)/shard_map/pallas_call | solution.py:839
  204.9 132.0 %shard_map.250 = (bf16[1728,768]{1,0:T(8,128)(2,1)}, bf16[1728,768]{1,0:T(8,128)(2,1)}, bf16[1728,768]{1,0:T(8,128)(2,1)}, bf16[3584,768]{1,0:T(8,128)(2,1)}, bf16[2,864,768]{2,1,0:T(8,128)(2,1)}) custom-call(bf16[1728,768]{1,0:T(8,128)(2,1)} %get-tuple-element.44.q_ref, bf16[1728,768]{1,0:T(8,128)(2,1)} %get-tuple-element.45.k_ref, ...), custom_call_target="tpu_custom_call" | custom-call | tf_op jit(solution)/shard_map/pallas_call | solution.py:993
  336.9 76.9 %shard_map.251 = (bf16[2304,384]{1,0:T(8,128)(2,1)}, bf16[2,864,768]{2,1,0:T(8,128)(2,1)}, f32[8,384]{1,0:T(8,128)}, f32[40,384]{1,0:T(8,128)}, bf16[3584,768]{1,0:T(8,128)(2,1)}) custom-call(bf16[1728,768]{1,0:T(8,128)(2,1)} %get-tuple-element.47.frame_ref, f32[1728,768]{1,0:T(8,128)} %get-tuple-element.62.gh_ref, ...), custom_call_target="tpu_custom_call", output_to_operand_aliasing={{4}: (9, {})} | custom-call | tf_op jit(solution)/shard_map/pallas_call | solution.py:1193
  413.8 0.0 copy-start.2
  413.9 1.5 slice_reduce_fusion
  415.4 0.0 slice-start
  415.4 2.3 slice.52
  417.7 0.0 copy-done.2
  417.7 0.0 slice-start.1
  417.7 0.2 fusion.1
  417.8 1.1 maximum_convert_fusion.2
  418.9 1.6 maximum_convert_fusion
  420.5 0.0 slice-done
  420.5 0.0 slice-done.1
  420.5 2.8 fusion
  423.3 0.0 copy-start
  423.3 2.7 copy.32
  426.1 0.0 copy-done
  426.1 0.0 copy-start.1
  426.1 1.5 copy.39
  427.6 1.2 copy-done.1
  428.8 0.0 copy-start.3
  428.8 1.5 copy.40
  430.3 0.0 copy-done.3
  430.3 0.6 copy.41
  (1 shorter events, 0.0 us)
Async XLA Ops:
  413.8 3.8 copy-start.2
  415.4 5.2 %slice-start = ((s8[5505024]{0:T(1024)(128)(4,1)}), s8[4194304]{0:T(1024)(128)(4,1)S(1)}, s32[]{:S(2)}) async-start(s8[5505024]{0:T(1024)(128)(4,1)} %bitcast.5), calls=%async_computation | async-start | bytes 8388608
  417.7 2.9 slice-start.1
  423.3 2.7 copy-start
  426.1 2.7 copy-start.1
  428.8 1.5 copy-start.3
